TPU v7x, 128 devices: a whole 4x4x4 slice. The times are simulated.
128 devices in a mesh: seq: 32 (over x, y, core), head: 4 (over z).
Axes of the slice: x: 4, y: 4, z: 4, core: 2. Of those that a mesh axis runs over, the one named last changes fastest.
Arguments:
- queries: bfloat16 [49152, 8192], P('seq', 'head'), may hold values from -0.59765625 to 0.59765625
- keys: bfloat16 [49152, 8192], P('seq', 'head'), may hold values from -6 to 6
- values: bfloat16 [49152, 8192], P('seq', 'head'), may hold values from -6 to 6
- doc_start: int32 [49152], P('seq'), may hold values from 0 to 49151, as said below
- norm_gain: float32 [8192], P('head'), may hold values from 0.1 to 1.9
Outputs:
- normed: bfloat16 [49152, 8192], P('seq', 'head')
Inputs may be any that keep to these rules, and one draw needn't show every extreme that they name: doc_start[t] <= t and never falls; doc_start[0] = 0; position t begins a document exactly where doc_start[t] = t; 17 documents in all, the first of them at least three quarters of the tokens long, the last a single token.
All inputs are finite; a program needn't handle non-finite values.
Results may differ from a plain program's by a relative error of at most 0.0049.
Values sent between devices are 32-bit elements; how exact they have to be, the bound alone decides.
No kernel may reach another device: no remote copies, remote signals or barrier semaphores. Data moves between devices by JAX's collectives and lax.ppermute only.
A program may use at most 192 MiB of HBM per device.

v0:
```python
import jax
import jax.numpy as jnp
from jax import lax
from jax.sharding import PartitionSpec as P

HEADS = 64
DH = 128
GROUP = 256


def shifted(value, axis, steps):
    count = lax.axis_size(axis)
    leading, last = (max(0, -steps), min(count, count - steps))
    return lax.ppermute(value, axis, [(source, source + steps) for source in range(leading, last)])


def combine(earlier, later):
    return (jnp.maximum(earlier[0], later[0]), later[1] + (1.0 - later[0]) * earlier[1])


def on_device(queries, keys, values, doc_start, norm_gain):
    tokens, width = queries.shape
    heads = width // DH
    blocks = tokens // GROUP
    qs = queries.reshape(blocks, GROUP, heads, DH)
    ks = keys.reshape(blocks, GROUP, heads, DH)
    vs = values.reshape(blocks, GROUP, heads, DH)
    starts = doc_start.reshape(blocks, GROUP)
    places = (lax.axis_index("seq") * tokens + jnp.arange(tokens, dtype=jnp.int32)).reshape(
        blocks, GROUP
    )
    firsts = places[:, 0]
    valid = (places[:, None, :] <= places[:, :, None]) & (places[:, None, :] >= starts[:, :, None])
    scores = jnp.einsum("cthd,cjhd->chtj", qs, ks, preferred_element_type=jnp.float32)
    scores = jnp.where(valid[:, None], scores, 0.0).astype(jnp.bfloat16)
    intra = jnp.einsum("chtj,cjhe->cthe", scores, vs, preferred_element_type=jnp.float32)
    lasts = starts[:, -1]
    keep = places >= lasts[:, None]
    kept = jnp.where(keep[:, :, None, None], ks, jnp.zeros_like(ks))
    states = jnp.einsum("cjhd,cjhe->chde", kept, vs, preferred_element_type=jnp.float32)
    resets = (lasts >= firsts).astype(jnp.float32)
    own_flag = jnp.float32(0.0)
    own_state = jnp.zeros((heads, DH, DH), jnp.float32)
    for block in range(blocks):
        own_state = states[block] + (1.0 - resets[block]) * own_state
        own_flag = jnp.maximum(own_flag, resets[block])
    empty = (jnp.float32(0.0), jnp.zeros((heads, DH, DH), jnp.float32))

    def advance(turn, received):
        sent = combine(received, (own_flag, own_state))
        return shifted((sent[0], sent[1]), "seq", 1)

    incoming = lax.fori_loop(0, lax.axis_size("seq") - 1, advance, empty)
    running = incoming[1]
    carried = []
    for block in range(blocks):
        carried.append(running)
        running = states[block] + (1.0 - resets[block]) * running
    carry_b = jnp.stack(carried).astype(jnp.bfloat16)
    inter = jnp.einsum("cthd,chde->cthe", qs, carry_b, preferred_element_type=jnp.float32)
    usable = starts < firsts[:, None]
    attn = intra + jnp.where(usable[:, :, None, None], inter, 0.0)
    attn = attn.reshape(tokens, width)
    squares = jnp.sum(attn * attn, axis=1)
    total = lax.psum(squares, "head")
    factor = lax.rsqrt(total / (HEADS * DH) + 1e-06)
    return (attn * factor[:, None] * norm_gain[None, :]).astype(jnp.bfloat16)


def solution(mesh):
    return jax.shard_map(
        on_device,
        mesh=mesh,
        in_specs=(P("seq", "head"), P("seq", "head"), P("seq", "head"), P("seq"), P("head")),
        out_specs=P("seq", "head"),
        check_vma=False,
    )
```

profile of v0, /device:TPU:2, one launch (start us, length us, event | category | flops | bytes accessed | tf_op | source)
XLA Modules:
  0.0 689.9 jit_solution(7283398050808409107)
XLA Ops:
  39.3 569.2 %while.12 = (s32[]{:T(128)}, f32[16,128,128]{2,1,0:T(8,128)S(1)}, f32[]{:T(128)}, f32[16,128,128]{2,1,0:T(8,128)S(1)}, s32[]{:T(128)}) while((s32[]{:T(128)}, f32[16,128,128]{2,1,0:T(8,128)S(1)}, f32[]{:T(128)}, f32[16,128,128]{2,1,0:T(8,128)S(1)}, s32[]{:T(128)}) %tuple.34), condition=%wide.region_1.2_spmd, body=%wide.region_0.1_spmd.sunk | while | flops 524290 | bytes 7340137 | solution.py:53
  41.3 16.3 %collective-permute-done = f32[16,128,128]{2,1,0:T(8,128)S(1)} collective-permute-done((f32[16,128,128]{2,1,0:T(8,128)S(1)}, f32[16,128,128]{2,1,0:T(8,128)S(1)}, u32[]{:S(2)}, u32[]{:S(2)}) %collective-permute-start) | collective-permute-done | bytes 1048608 | tf_op jit(solution)/shard_map/while/body/eval_jaxpr/ppermute | solution.py:14
  59.7 16.3 %collective-permute-done = f32[16,128,128]{2,1,0:T(8,128)S(1)} collective-permute-done((f32[16,128,128]{2,1,0:T(8,128)S(1)}, f32[16,128,128]{2,1,0:T(8,128)S(1)}, u32[]{:S(2)}, u32[]{:S(2)}) %collective-permute-start) | collective-permute-done | bytes 1048608 | tf_op jit(solution)/shard_map/while/body/eval_jaxpr/ppermute | solution.py:14
  78.1 16.3 %collective-permute-done = f32[16,128,128]{2,1,0:T(8,128)S(1)} collective-permute-done((f32[16,128,128]{2,1,0:T(8,128)S(1)}, f32[16,128,128]{2,1,0:T(8,128)S(1)}, u32[]{:S(2)}, u32[]{:S(2)}) %collective-permute-start) | collective-permute-done | bytes 1048608 | tf_op jit(solution)/shard_map/while/body/eval_jaxpr/ppermute | solution.py:14
  96.4 16.3 %collective-permute-done = f32[16,128,128]{2,1,0:T(8,128)S(1)} collective-permute-done((f32[16,128,128]{2,1,0:T(8,128)S(1)}, f32[16,128,128]{2,1,0:T(8,128)S(1)}, u32[]{:S(2)}, u32[]{:S(2)}) %collective-permute-start) | collective-permute-done | bytes 1048608 | tf_op jit(solution)/shard_map/while/body/eval_jaxpr/ppermute | solution.py:14
  114.8 16.3 %collective-permute-done = f32[16,128,128]{2,1,0:T(8,128)S(1)} collective-permute-done((f32[16,128,128]{2,1,0:T(8,128)S(1)}, f32[16,128,128]{2,1,0:T(8,128)S(1)}, u32[]{:S(2)}, u32[]{:S(2)}) %collective-permute-start) | collective-permute-done | bytes 1048608 | tf_op jit(solution)/shard_map/while/body/eval_jaxpr/ppermute | solution.py:14
  133.1 16.3 %collective-permute-done = f32[16,128,128]{2,1,0:T(8,128)S(1)} collective-permute-done((f32[16,128,128]{2,1,0:T(8,128)S(1)}, f32[16,128,128]{2,1,0:T(8,128)S(1)}, u32[]{:S(2)}, u32[]{:S(2)}) %collective-permute-start) | collective-permute-done | bytes 1048608 | tf_op jit(solution)/shard_map/while/body/eval_jaxpr/ppermute | solution.py:14
  151.5 16.3 %collective-permute-done = f32[16,128,128]{2,1,0:T(8,128)S(1)} collective-permute-done((f32[16,128,128]{2,1,0:T(8,128)S(1)}, f32[16,128,128]{2,1,0:T(8,128)S(1)}, u32[]{:S(2)}, u32[]{:S(2)}) %collective-permute-start) | collective-permute-done | bytes 1048608 | tf_op jit(solution)/shard_map/while/body/eval_jaxpr/ppermute | solution.py:14
  169.9 16.3 %collective-permute-done = f32[16,128,128]{2,1,0:T(8,128)S(1)} collective-permute-done((f32[16,128,128]{2,1,0:T(8,128)S(1)}, f32[16,128,128]{2,1,0:T(8,128)S(1)}, u32[]{:S(2)}, u32[]{:S(2)}) %collective-permute-start) | collective-permute-done | bytes 1048608 | tf_op jit(solution)/shard_map/while/body/eval_jaxpr/ppermute | solution.py:14
  188.2 16.3 %collective-permute-done = f32[16,128,128]{2,1,0:T(8,128)S(1)} collective-permute-done((f32[16,128,128]{2,1,0:T(8,128)S(1)}, f32[16,128,128]{2,1,0:T(8,128)S(1)}, u32[]{:S(2)}, u32[]{:S(2)}) %collective-permute-start) | collective-permute-done | bytes 1048608 | tf_op jit(solution)/shard_map/while/body/eval_jaxpr/ppermute | solution.py:14
  206.6 16.3 %collective-permute-done = f32[16,128,128]{2,1,0:T(8,128)S(1)} collective-permute-done((f32[16,128,128]{2,1,0:T(8,128)S(1)}, f32[16,128,128]{2,1,0:T(8,128)S(1)}, u32[]{:S(2)}, u32[]{:S(2)}) %collective-permute-start) | collective-permute-done | bytes 1048608 | tf_op jit(solution)/shard_map/while/body/eval_jaxpr/ppermute | solution.py:14
  225.0 16.3 %collective-permute-done = f32[16,128,128]{2,1,0:T(8,128)S(1)} collective-permute-done((f32[16,128,128]{2,1,0:T(8,128)S(1)}, f32[16,128,128]{2,1,0:T(8,128)S(1)}, u32[]{:S(2)}, u32[]{:S(2)}) %collective-permute-start) | collective-permute-done | bytes 1048608 | tf_op jit(solution)/shard_map/while/body/eval_jaxpr/ppermute | solution.py:14
  243.3 16.3 %collective-permute-done = f32[16,128,128]{2,1,0:T(8,128)S(1)} collective-permute-done((f32[16,128,128]{2,1,0:T(8,128)S(1)}, f32[16,128,128]{2,1,0:T(8,128)S(1)}, u32[]{:S(2)}, u32[]{:S(2)}) %collective-permute-start) | collective-permute-done | bytes 1048608 | tf_op jit(solution)/shard_map/while/body/eval_jaxpr/ppermute | solution.py:14
  261.7 16.3 %collective-permute-done = f32[16,128,128]{2,1,0:T(8,128)S(1)} collective-permute-done((f32[16,128,128]{2,1,0:T(8,128)S(1)}, f32[16,128,128]{2,1,0:T(8,128)S(1)}, u32[]{:S(2)}, u32[]{:S(2)}) %collective-permute-start) | collective-permute-done | bytes 1048608 | tf_op jit(solution)/shard_map/while/body/eval_jaxpr/ppermute | solution.py:14
  280.0 16.3 %collective-permute-done = f32[16,128,128]{2,1,0:T(8,128)S(1)} collective-permute-done((f32[16,128,128]{2,1,0:T(8,128)S(1)}, f32[16,128,128]{2,1,0:T(8,128)S(1)}, u32[]{:S(2)}, u32[]{:S(2)}) %collective-permute-start) | collective-permute-done | bytes 1048608 | tf_op jit(solution)/shard_map/while/body/eval_jaxpr/ppermute | solution.py:14
  298.4 16.3 %collective-permute-done = f32[16,128,128]{2,1,0:T(8,128)S(1)} collective-permute-done((f32[16,128,128]{2,1,0:T(8,128)S(1)}, f32[16,128,128]{2,1,0:T(8,128)S(1)}, u32[]{:S(2)}, u32[]{:S(2)}) %collective-permute-start) | collective-permute-done | bytes 1048608 | tf_op jit(solution)/shard_map/while/body/eval_jaxpr/ppermute | solution.py:14
  316.8 16.3 %collective-permute-done = f32[16,128,128]{2,1,0:T(8,128)S(1)} collective-permute-done((f32[16,128,128]{2,1,0:T(8,128)S(1)}, f32[16,128,128]{2,1,0:T(8,128)S(1)}, u32[]{:S(2)}, u32[]{:S(2)}) %collective-permute-start) | collective-permute-done | bytes 1048608 | tf_op jit(solution)/shard_map/while/body/eval_jaxpr/ppermute | solution.py:14
  335.1 16.3 %collective-permute-done = f32[16,128,128]{2,1,0:T(8,128)S(1)} collective-permute-done((f32[16,128,128]{2,1,0:T(8,128)S(1)}, f32[16,128,128]{2,1,0:T(8,128)S(1)}, u32[]{:S(2)}, u32[]{:S(2)}) %collective-permute-start) | collective-permute-done | bytes 1048608 | tf_op jit(solution)/shard_map/while/body/eval_jaxpr/ppermute | solution.py:14
  353.5 16.3 %collective-permute-done = f32[16,128,128]{2,1,0:T(8,128)S(1)} collective-permute-done((f32[16,128,128]{2,1,0:T(8,128)S(1)}, f32[16,128,128]{2,1,0:T(8,128)S(1)}, u32[]{:S(2)}, u32[]{:S(2)}) %collective-permute-start) | collective-permute-done | bytes 1048608 | tf_op jit(solution)/shard_map/while/body/eval_jaxpr/ppermute | solution.py:14
  371.9 16.3 %collective-permute-done = f32[16,128,128]{2,1,0:T(8,128)S(1)} collective-permute-done((f32[16,128,128]{2,1,0:T(8,128)S(1)}, f32[16,128,128]{2,1,0:T(8,128)S(1)}, u32[]{:S(2)}, u32[]{:S(2)}) %collective-permute-start) | collective-permute-done | bytes 1048608 | tf_op jit(solution)/shard_map/while/body/eval_jaxpr/ppermute | solution.py:14
  390.2 16.3 %collective-permute-done = f32[16,128,128]{2,1,0:T(8,128)S(1)} collective-permute-done((f32[16,128,128]{2,1,0:T(8,128)S(1)}, f32[16,128,128]{2,1,0:T(8,128)S(1)}, u32[]{:S(2)}, u32[]{:S(2)}) %collective-permute-start) | collective-permute-done | bytes 1048608 | tf_op jit(solution)/shard_map/while/body/eval_jaxpr/ppermute | solution.py:14
  408.6 16.3 %collective-permute-done = f32[16,128,128]{2,1,0:T(8,128)S(1)} collective-permute-done((f32[16,128,128]{2,1,0:T(8,128)S(1)}, f32[16,128,128]{2,1,0:T(8,128)S(1)}, u32[]{:S(2)}, u32[]{:S(2)}) %collective-permute-start) | collective-permute-done | bytes 1048608 | tf_op jit(solution)/shard_map/while/body/eval_jaxpr/ppermute | solution.py:14
  463.7 16.3 %collective-permute-done = f32[16,128,128]{2,1,0:T(8,128)S(1)} collective-permute-done((f32[16,128,128]{2,1,0:T(8,128)S(1)}, f32[16,128,128]{2,1,0:T(8,128)S(1)}, u32[]{:S(2)}, u32[]{:S(2)}) %collective-permute-start) | collective-permute-done | bytes 1048608 | tf_op jit(solution)/shard_map/while/body/eval_jaxpr/ppermute | solution.py:14
  537.1 16.3 %collective-permute-done = f32[16,128,128]{2,1,0:T(8,128)S(1)} collective-permute-done((f32[16,128,128]{2,1,0:T(8,128)S(1)}, f32[16,128,128]{2,1,0:T(8,128)S(1)}, u32[]{:S(2)}, u32[]{:S(2)}) %collective-permute-start) | collective-permute-done | bytes 1048608 | tf_op jit(solution)/shard_map/while/body/eval_jaxpr/ppermute | solution.py:14
  (117 shorter events, 306.9 us)
Async XLA Ops:
  39.4 18.2 %collective-permute-start = (f32[16,128,128]{2,1,0:T(8,128)S(1)}, f32[16,128,128]{2,1,0:T(8,128)S(1)}, u32[]{:S(2)}, u32[]{:S(2)}) collective-permute-start(f32[16,128,128]{2,1,0:T(8,128)S(1)} %multiply_add_fusion.8), channel_id=1, source_target_pairs={{0,4},{4,8},{8,12},{12,16},{16,20},{20,24},{24,28},{28,32},{32,36}... | collective-permute-start | bytes 3145736 | tf_op jit(solution)/shard_map/while/body/eval_jaxpr/ppermute | solution.py:14
  57.8 18.2 %collective-permute-start = (f32[16,128,128]{2,1,0:T(8,128)S(1)}, f32[16,128,128]{2,1,0:T(8,128)S(1)}, u32[]{:S(2)}, u32[]{:S(2)}) collective-permute-start(f32[16,128,128]{2,1,0:T(8,128)S(1)} %multiply_add_fusion.8), channel_id=1, source_target_pairs={{0,4},{4,8},{8,12},{12,16},{16,20},{20,24},{24,28},{28,32},{32,36}... | collective-permute-start | bytes 3145736 | tf_op jit(solution)/shard_map/while/body/eval_jaxpr/ppermute | solution.py:14
  76.1 18.2 %collective-permute-start = (f32[16,128,128]{2,1,0:T(8,128)S(1)}, f32[16,128,128]{2,1,0:T(8,128)S(1)}, u32[]{:S(2)}, u32[]{:S(2)}) collective-permute-start(f32[16,128,128]{2,1,0:T(8,128)S(1)} %multiply_add_fusion.8), channel_id=1, source_target_pairs={{0,4},{4,8},{8,12},{12,16},{16,20},{20,24},{24,28},{28,32},{32,36}... | collective-permute-start | bytes 3145736 | tf_op jit(solution)/shard_map/while/body/eval_jaxpr/ppermute | solution.py:14
  94.5 18.2 %collective-permute-start = (f32[16,128,128]{2,1,0:T(8,128)S(1)}, f32[16,128,128]{2,1,0:T(8,128)S(1)}, u32[]{:S(2)}, u32[]{:S(2)}) collective-permute-start(f32[16,128,128]{2,1,0:T(8,128)S(1)} %multiply_add_fusion.8), channel_id=1, source_target_pairs={{0,4},{4,8},{8,12},{12,16},{16,20},{20,24},{24,28},{28,32},{32,36}... | collective-permute-start | bytes 3145736 | tf_op jit(solution)/shard_map/while/body/eval_jaxpr/ppermute | solution.py:14
  112.9 18.2 %collective-permute-start = (f32[16,128,128]{2,1,0:T(8,128)S(1)}, f32[16,128,128]{2,1,0:T(8,128)S(1)}, u32[]{:S(2)}, u32[]{:S(2)}) collective-permute-start(f32[16,128,128]{2,1,0:T(8,128)S(1)} %multiply_add_fusion.8), channel_id=1, source_target_pairs={{0,4},{4,8},{8,12},{12,16},{16,20},{20,24},{24,28},{28,32},{32,36}... | collective-permute-start | bytes 3145736 | tf_op jit(solution)/shard_map/while/body/eval_jaxpr/ppermute | solution.py:14
  131.2 18.2 %collective-permute-start = (f32[16,128,128]{2,1,0:T(8,128)S(1)}, f32[16,128,128]{2,1,0:T(8,128)S(1)}, u32[]{:S(2)}, u32[]{:S(2)}) collective-permute-start(f32[16,128,128]{2,1,0:T(8,128)S(1)} %multiply_add_fusion.8), channel_id=1, source_target_pairs={{0,4},{4,8},{8,12},{12,16},{16,20},{20,24},{24,28},{28,32},{32,36}... | collective-permute-start | bytes 3145736 | tf_op jit(solution)/shard_map/while/body/eval_jaxpr/ppermute | solution.py:14
  149.6 18.2 %collective-permute-start = (f32[16,128,128]{2,1,0:T(8,128)S(1)}, f32[16,128,128]{2,1,0:T(8,128)S(1)}, u32[]{:S(2)}, u32[]{:S(2)}) collective-permute-start(f32[16,128,128]{2,1,0:T(8,128)S(1)} %multiply_add_fusion.8), channel_id=1, source_target_pairs={{0,4},{4,8},{8,12},{12,16},{16,20},{20,24},{24,28},{28,32},{32,36}... | collective-permute-start | bytes 3145736 | tf_op jit(solution)/shard_map/while/body/eval_jaxpr/ppermute | solution.py:14
  167.9 18.2 %collective-permute-start = (f32[16,128,128]{2,1,0:T(8,128)S(1)}, f32[16,128,128]{2,1,0:T(8,128)S(1)}, u32[]{:S(2)}, u32[]{:S(2)}) collective-permute-start(f32[16,128,128]{2,1,0:T(8,128)S(1)} %multiply_add_fusion.8), channel_id=1, source_target_pairs={{0,4},{4,8},{8,12},{12,16},{16,20},{20,24},{24,28},{28,32},{32,36}... | collective-permute-start | bytes 3145736 | tf_op jit(solution)/shard_map/while/body/eval_jaxpr/ppermute | solution.py:14
  186.3 18.2 %collective-permute-start = (f32[16,128,128]{2,1,0:T(8,128)S(1)}, f32[16,128,128]{2,1,0:T(8,128)S(1)}, u32[]{:S(2)}, u32[]{:S(2)}) collective-permute-start(f32[16,128,128]{2,1,0:T(8,128)S(1)} %multiply_add_fusion.8), channel_id=1, source_target_pairs={{0,4},{4,8},{8,12},{12,16},{16,20},{20,24},{24,28},{28,32},{32,36}... | collective-permute-start | bytes 3145736 | tf_op jit(solution)/shard_map/while/body/eval_jaxpr/ppermute | solution.py:14
  204.7 18.2 %collective-permute-start = (f32[16,128,128]{2,1,0:T(8,128)S(1)}, f32[16,128,128]{2,1,0:T(8,128)S(1)}, u32[]{:S(2)}, u32[]{:S(2)}) collective-permute-start(f32[16,128,128]{2,1,0:T(8,128)S(1)} %multiply_add_fusion.8), channel_id=1, source_target_pairs={{0,4},{4,8},{8,12},{12,16},{16,20},{20,24},{24,28},{28,32},{32,36}... | collective-permute-start | bytes 3145736 | tf_op jit(solution)/shard_map/while/body/eval_jaxpr/ppermute | solution.py:14
  223.0 18.2 %collective-permute-start = (f32[16,128,128]{2,1,0:T(8,128)S(1)}, f32[16,128,128]{2,1,0:T(8,128)S(1)}, u32[]{:S(2)}, u32[]{:S(2)}) collective-permute-start(f32[16,128,128]{2,1,0:T(8,128)S(1)} %multiply_add_fusion.8), channel_id=1, source_target_pairs={{0,4},{4,8},{8,12},{12,16},{16,20},{20,24},{24,28},{28,32},{32,36}... | collective-permute-start | bytes 3145736 | tf_op jit(solution)/shard_map/while/body/eval_jaxpr/ppermute | solution.py:14
  241.4 18.2 %collective-permute-start = (f32[16,128,128]{2,1,0:T(8,128)S(1)}, f32[16,128,128]{2,1,0:T(8,128)S(1)}, u32[]{:S(2)}, u32[]{:S(2)}) collective-permute-start(f32[16,128,128]{2,1,0:T(8,128)S(1)} %multiply_add_fusion.8), channel_id=1, source_target_pairs={{0,4},{4,8},{8,12},{12,16},{16,20},{20,24},{24,28},{28,32},{32,36}... | collective-permute-start | bytes 3145736 | tf_op jit(solution)/shard_map/while/body/eval_jaxpr/ppermute | solution.py:14
  259.8 18.2 %collective-permute-start = (f32[16,128,128]{2,1,0:T(8,128)S(1)}, f32[16,128,128]{2,1,0:T(8,128)S(1)}, u32[]{:S(2)}, u32[]{:S(2)}) collective-permute-start(f32[16,128,128]{2,1,0:T(8,128)S(1)} %multiply_add_fusion.8), channel_id=1, source_target_pairs={{0,4},{4,8},{8,12},{12,16},{16,20},{20,24},{24,28},{28,32},{32,36}... | collective-permute-start | bytes 3145736 | tf_op jit(solution)/shard_map/while/body/eval_jaxpr/ppermute | solution.py:14
  278.1 18.2 %collective-permute-start = (f32[16,128,128]{2,1,0:T(8,128)S(1)}, f32[16,128,128]{2,1,0:T(8,128)S(1)}, u32[]{:S(2)}, u32[]{:S(2)}) collective-permute-start(f32[16,128,128]{2,1,0:T(8,128)S(1)} %multiply_add_fusion.8), channel_id=1, source_target_pairs={{0,4},{4,8},{8,12},{12,16},{16,20},{20,24},{24,28},{28,32},{32,36}... | collective-permute-start | bytes 3145736 | tf_op jit(solution)/shard_map/while/body/eval_jaxpr/ppermute | solution.py:14
  296.5 18.2 %collective-permute-start = (f32[16,128,128]{2,1,0:T(8,128)S(1)}, f32[16,128,128]{2,1,0:T(8,128)S(1)}, u32[]{:S(2)}, u32[]{:S(2)}) collective-permute-start(f32[16,128,128]{2,1,0:T(8,128)S(1)} %multiply_add_fusion.8), channel_id=1, source_target_pairs={{0,4},{4,8},{8,12},{12,16},{16,20},{20,24},{24,28},{28,32},{32,36}... | collective-permute-start | bytes 3145736 | tf_op jit(solution)/shard_map/while/body/eval_jaxpr/ppermute | solution.py:14
  314.8 18.2 %collective-permute-start = (f32[16,128,128]{2,1,0:T(8,128)S(1)}, f32[16,128,128]{2,1,0:T(8,128)S(1)}, u32[]{:S(2)}, u32[]{:S(2)}) collective-permute-start(f32[16,128,128]{2,1,0:T(8,128)S(1)} %multiply_add_fusion.8), channel_id=1, source_target_pairs={{0,4},{4,8},{8,12},{12,16},{16,20},{20,24},{24,28},{28,32},{32,36}... | collective-permute-start | bytes 3145736 | tf_op jit(solution)/shard_map/while/body/eval_jaxpr/ppermute | solution.py:14
  333.2 18.2 %collective-permute-start = (f32[16,128,128]{2,1,0:T(8,128)S(1)}, f32[16,128,128]{2,1,0:T(8,128)S(1)}, u32[]{:S(2)}, u32[]{:S(2)}) collective-permute-start(f32[16,128,128]{2,1,0:T(8,128)S(1)} %multiply_add_fusion.8), channel_id=1, source_target_pairs={{0,4},{4,8},{8,12},{12,16},{16,20},{20,24},{24,28},{28,32},{32,36}... | collective-permute-start | bytes 3145736 | tf_op jit(solution)/shard_map/while/body/eval_jaxpr/ppermute | solution.py:14
  351.6 18.2 %collective-permute-start = (f32[16,128,128]{2,1,0:T(8,128)S(1)}, f32[16,128,128]{2,1,0:T(8,128)S(1)}, u32[]{:S(2)}, u32[]{:S(2)}) collective-permute-start(f32[16,128,128]{2,1,0:T(8,128)S(1)} %multiply_add_fusion.8), channel_id=1, source_target_pairs={{0,4},{4,8},{8,12},{12,16},{16,20},{20,24},{24,28},{28,32},{32,36}... | collective-permute-start | bytes 3145736 | tf_op jit(solution)/shard_map/while/body/eval_jaxpr/ppermute | solution.py:14
  388.3 18.2 %collective-permute-start = (f32[16,128,128]{2,1,0:T(8,128)S(1)}, f32[16,128,128]{2,1,0:T(8,128)S(1)}, u32[]{:S(2)}, u32[]{:S(2)}) collective-permute-start(f32[16,128,128]{2,1,0:T(8,128)S(1)} %multiply_add_fusion.8), channel_id=1, source_target_pairs={{0,4},{4,8},{8,12},{12,16},{16,20},{20,24},{24,28},{28,32},{32,36}... | collective-permute-start | bytes 3145736 | tf_op jit(solution)/shard_map/while/body/eval_jaxpr/ppermute | solution.py:14
  406.6 18.2 %collective-permute-start = (f32[16,128,128]{2,1,0:T(8,128)S(1)}, f32[16,128,128]{2,1,0:T(8,128)S(1)}, u32[]{:S(2)}, u32[]{:S(2)}) collective-permute-start(f32[16,128,128]{2,1,0:T(8,128)S(1)} %multiply_add_fusion.8), channel_id=1, source_target_pairs={{0,4},{4,8},{8,12},{12,16},{16,20},{20,24},{24,28},{28,32},{32,36}... | collective-permute-start | bytes 3145736 | tf_op jit(solution)/shard_map/while/body/eval_jaxpr/ppermute | solution.py:14
  461.7 18.2 %collective-permute-start = (f32[16,128,128]{2,1,0:T(8,128)S(1)}, f32[16,128,128]{2,1,0:T(8,128)S(1)}, u32[]{:S(2)}, u32[]{:S(2)}) collective-permute-start(f32[16,128,128]{2,1,0:T(8,128)S(1)} %multiply_add_fusion.8), channel_id=1, source_target_pairs={{0,4},{4,8},{8,12},{12,16},{16,20},{20,24},{24,28},{28,32},{32,36}... | collective-permute-start | bytes 3145736 | tf_op jit(solution)/shard_map/while/body/eval_jaxpr/ppermute | solution.py:14
  480.1 18.2 %collective-permute-start = (f32[16,128,128]{2,1,0:T(8,128)S(1)}, f32[16,128,128]{2,1,0:T(8,128)S(1)}, u32[]{:S(2)}, u32[]{:S(2)}) collective-permute-start(f32[16,128,128]{2,1,0:T(8,128)S(1)} %multiply_add_fusion.8), channel_id=1, source_target_pairs={{0,4},{4,8},{8,12},{12,16},{16,20},{20,24},{24,28},{28,32},{32,36}... | collective-permute-start | bytes 3145736 | tf_op jit(solution)/shard_map/while/body/eval_jaxpr/ppermute | solution.py:14
  535.2 18.2 %collective-permute-start = (f32[16,128,128]{2,1,0:T(8,128)S(1)}, f32[16,128,128]{2,1,0:T(8,128)S(1)}, u32[]{:S(2)}, u32[]{:S(2)}) collective-permute-start(f32[16,128,128]{2,1,0:T(8,128)S(1)} %multiply_add_fusion.8), channel_id=1, source_target_pairs={{0,4},{4,8},{8,12},{12,16},{16,20},{20,24},{24,28},{28,32},{32,36}... | collective-permute-start | bytes 3145736 | tf_op jit(solution)/shard_map/while/body/eval_jaxpr/ppermute | solution.py:14
  553.5 18.2 %collective-permute-start = (f32[16,128,128]{2,1,0:T(8,128)S(1)}, f32[16,128,128]{2,1,0:T(8,128)S(1)}, u32[]{:S(2)}, u32[]{:S(2)}) collective-permute-start(f32[16,128,128]{2,1,0:T(8,128)S(1)} %multiply_add_fusion.8), channel_id=1, source_target_pairs={{0,4},{4,8},{8,12},{12,16},{16,20},{20,24},{24,28},{28,32},{32,36}... | collective-permute-start | bytes 3145736 | tf_op jit(solution)/shard_map/while/body/eval_jaxpr/ppermute | solution.py:14
  (16 other events, 217.4 us)
where the time goes:
time: 691 us; the launch traced here: 690 us
  waiting for transfers between devices  505 us (73%)
  starting transfers between devices  59.5 us (9%)
  local copies, waits for them, and re-layouts  47 us (7%)
  matrix products  32.3 us (5%)
  other arithmetic  25.8 us (4%)
  blocking collectives  11.9 us (2%)
  between operations  7.6 us (1%)
    ppermute x31, waiting for transfers between devices, shifted(): lax.ppermute(value, axis, [(source, source + steps) for source in range(l...  505 us
    ppermute x31, starting transfers between devices, shifted(): lax.ppermute(value, axis, [(source, source + steps) for source in range(l...  59.5 us
    unnamed x21, local copies, waits for them, and re-layouts  23.5 us
    dot_general x1, matrix products, on_device(): jnp.einsum('chtj,cjhe->cthe', scores, vs, preferred_element_type=jnp.floa...  16.2 us
    dot_general x1, matrix products, on_device(): jnp.einsum('cthd,chde->cthe', qs, carry_b, preferred_element_type=jnp.flo...  14.1 us
  transfers between devices with their start and end apart: 31, of which 31 were waited for; matrix products, arithmetic and copies ran while one was open for 0% of the time, Pallas kernels for 0%

commit v1 on v0

v1 whole, which is shorter than its diff:
```python
import functools

import jax
import jax.numpy as jnp
from jax import lax
from jax.experimental import pallas as pl
from jax.experimental.pallas import tpu as pltpu
from jax.sharding import PartitionSpec as P

HEADS = 64
DH = 128
GROUP = 256
EPS = 1e-06
SEQ_Y = 4
SEQ_X = 4
MIB = 1 << 20
CORE, ROW_Y, ROW_X, BASE, FIRST, LAST, CHIP, OPEN = range(8)

ANY = pl.BlockSpec(memory_space=pl.ANY)
VMEM = pl.BlockSpec(memory_space=pltpu.VMEM)
SMEM = pl.BlockSpec(memory_space=pltpu.SMEM)
F32 = jnp.float32


def device_of(x, y, core):
    return (x * SEQ_Y + y) * 2 + core


def places():
    return [(x, y, c) for x in range(SEQ_X) for y in range(SEQ_Y) for c in range(2)]


def swap_cores(value):
    return lax.ppermute(
        value, "seq", [(device_of(x, y, c), device_of(x, y, 1 - c)) for x, y, c in places()]
    )


def turn_row(value, steps):
    return lax.ppermute(
        value,
        "seq",
        [(device_of(x, y, c), device_of(x, (y + steps) % SEQ_Y, c)) for x, y, c in places()],
    )


def next_rows(value, steps):
    return lax.ppermute(
        value,
        "seq",
        [(device_of(x, y, c), device_of(x + steps, y, c)) for x, y, c in places() if x + steps < SEQ_X],
    )


def params(limit, **more):
    return pltpu.CompilerParams(vmem_limit_bytes=limit * MIB, **more)


def state_kernel(meta, k_ref, v_ref, out_ref):
    step = pl.program_id(0)
    tokens, width = k_ref.shape
    rows = meta[BASE] + lax.broadcasted_iota(jnp.int32, (tokens, width), 0)
    kept = jnp.where(rows >= meta[LAST], k_ref[...].astype(F32), 0.0).astype(jnp.bfloat16)
    both = lax.dot_general(kept, v_ref[...], (((0,), (0,)), ((), ())), preferred_element_type=F32)
    at = pl.multiple_of(step * width, width)
    out_ref[pl.ds(at, DH), :] = both[:DH, :DH]
    out_ref[pl.ds(at + DH, DH), :] = both[DH:, DH:]

    @pl.when(step == 0)
    def _():
        row = lax.broadcasted_iota(jnp.int32, (8, DH), 0)
        flags = jnp.where(row == 0, meta[FIRST], meta[LAST])
        out_ref[pl.ds(out_ref.shape[0] - 8, 8), :] = flags.astype(F32)


def half_state(meta, keys, values, other):
    tokens, width = keys.shape
    pairs = width // (4 * DH)

    def at(step, meta):
        half = 1 - meta[CORE] if other else meta[CORE]
        return 0, half * pairs + step

    block = pl.BlockSpec((tokens, 2 * DH), at)
    rows = width // 2 + 8
    return pl.pallas_call(
        state_kernel,
        out_shape=jax.ShapeDtypeStruct((rows, DH), F32),
        grid_spec=pltpu.PrefetchScalarGridSpec(
            num_scalar_prefetch=1,
            grid=(pairs,),
            in_specs=[block, block],
            out_specs=pl.BlockSpec((rows, DH), lambda step, meta: (0, 0)),
        ),
        compiler_params=params(16),
        cost_estimate=pl.CostEstimate(
            flops=2 * tokens * (width // 2) * DH, bytes_accessed=2 * tokens * width, transcendentals=0
        ),
    )(meta, keys, values)


def marks(ref):
    at = ref.shape[0] - 8
    return ref[at : at + 1, :], ref[at + 1 : at + 2, :]


def cores_kernel(meta, keep, recv, own, to1, to2, to3):
    total = keep.shape[0] - 8
    part = total // SEQ_Y
    on_first = meta[CORE] == 0
    k_first, k_last = marks(keep)
    r_first, r_last = marks(recv)
    first = jnp.where(on_first, k_first, r_first)
    last = jnp.where(on_first, r_last, k_last)
    edge = (meta[CHIP] + meta[OPEN]).astype(F32)
    joined = jnp.where(last < edge, 1.0, 0.0)
    w_keep = jnp.where(on_first, joined, 1.0)
    w_recv = jnp.where(on_first, 1.0, joined)
    row = lax.broadcasted_iota(jnp.int32, (8, DH), 0)
    flags = jnp.where(row == 0, first, last)
    for steps, out in enumerate((own, to1, to2, to3)):
        at = pl.multiple_of(lax.rem(meta[ROW_Y] + steps, SEQ_Y) * part, part)
        out[:part, :] = keep[pl.ds(at, part), :] * w_keep + recv[pl.ds(at, part), :] * w_recv
        out[part:, :] = flags


def sources(meta):
    return [lax.rem(meta[ROW_Y] + SEQ_Y - d, SEQ_Y) for d in range(SEQ_Y)]


def ends(meta, place):
    return ((meta[ROW_X] * SEQ_Y + place + 1) * (2 * meta[OPEN])).astype(F32)


def row_kernel(meta, own, from1, from2, from3, out):
    part = out.shape[0]
    refs = (own, from1, from2, from3)
    where = sources(meta)
    row_last = jnp.zeros((1, DH), F32)
    for place, ref in zip(where, refs):
        row_last = row_last + jnp.where(place == SEQ_Y - 1, marks(ref)[1], 0.0)
    total = jnp.zeros((part, DH), F32)
    for place, ref in zip(where, refs):
        total = total + ref[:part, :] * jnp.where(row_last < ends(meta, place), 1.0, 0.0)
    out[...] = total


def carry_kernel(meta, own, from1, from2, from3, up1, up2, up3, out0, out1, out2, out3):
    part = out0.shape[0]
    refs = (own, from1, from2, from3)
    ups = (up1, up2, up3)
    where = sources(meta)
    for steps, out in enumerate((out0, out1, out2, out3)):
        target = (SEQ_Y - steps) % SEQ_Y
        place = where[target]
        first = marks(refs[target])[0]
        total = jnp.zeros((part, DH), F32)
        for source in range(SEQ_Y):
            if source != target:
                before = jnp.where(where[source] < place, 1.0, 0.0)
                weight = jnp.where(first < ends(meta, where[source]), before, 0.0)
                total = total + refs[source][:part, :] * weight
        for back, ref in enumerate(ups):
            edge = ((meta[ROW_X] - back) * (SEQ_Y * 2 * meta[OPEN])).astype(F32)
            total = total + ref[...] * jnp.where(first < edge, 1.0, 0.0)
        out[...] = total


def spread_kernel(meta, own, got1, got2, got3, keep, recv, mine, send):
    part = own.shape[0]
    on_first = meta[CORE] == 0
    second_first = jnp.where(on_first, marks(recv)[0], marks(keep)[0])
    edge = (meta[CHIP] + meta[OPEN]).astype(F32)
    w_state = jnp.where(second_first < edge, 1.0, 0.0)
    w_carry = jnp.where(second_first < meta[CHIP].astype(F32), 1.0, 0.0)
    w_keep = jnp.where(on_first, w_state, 0.0)
    w_recv = jnp.where(on_first, 0.0, w_state)
    for place, ref in zip(sources(meta), (own, got1, got2, got3)):
        at = pl.multiple_of(place * part, part)
        carry = ref[...]
        later = keep[pl.ds(at, part), :] * w_keep + recv[pl.ds(at, part), :] * w_recv + carry * w_carry
        mine[pl.ds(at, part), :] = jnp.where(on_first, carry, later)
        send[pl.ds(at, part), :] = jnp.where(on_first, later, carry)


def small(kernel, meta, args, outs):
    return pl.pallas_call(
        kernel,
        out_shape=[jax.ShapeDtypeStruct((rows, DH), F32) for rows in outs],
        in_specs=[SMEM] + [VMEM] * len(args),
        out_specs=[VMEM] * len(outs),
        compiler_params=params(8),
        cost_estimate=pl.CostEstimate(flops=0, bytes_accessed=2 * MIB, transcendentals=0),
    )(meta, *args)


def local_kernel(meta, starts_ref, q_ref, k_ref, v_ref, out_ref):
    tokens, width = q_ref.shape
    blocks = tokens // GROUP
    carries = [jnp.zeros((DH, DH), F32) for _ in range(width // DH)]
    key_place = lax.broadcasted_iota(jnp.int32, (GROUP, GROUP), 1)
    query_place = lax.broadcasted_iota(jnp.int32, (GROUP, GROUP), 0)
    for block in range(blocks):
        rows = slice(block * GROUP, (block + 1) * GROUP)
        first = meta[BASE] + block * GROUP
        starts = starts_ref[block : block + 1, :]
        column = jnp.broadcast_to(starts, (DH, GROUP)).T
        wide = jnp.concatenate([column, column], axis=1)
        valid = (key_place <= query_place) & (key_place + first >= wide)
        last = starts[:, GROUP - 1 :]
        keep = query_place[:, :DH] + first >= jnp.broadcast_to(last, (GROUP, DH))
        usable = column < first
        go_on = jnp.where(last < first, 1.0, 0.0)
        for head in range(width // DH):
            cols = slice(head * DH, (head + 1) * DH)
            q, k, v = q_ref[rows, cols], k_ref[rows, cols], v_ref[rows, cols]
            scores = lax.dot_general(q, k, (((1,), (1,)), ((), ())), preferred_element_type=F32)
            scores = jnp.where(valid, scores, 0.0).astype(jnp.bfloat16)
            attn = jnp.dot(scores, v, preferred_element_type=F32)
            if block:
                inter = jnp.dot(q, carries[head].astype(jnp.bfloat16), preferred_element_type=F32)
                attn = attn + jnp.where(usable, inter, 0.0)
            out_ref[rows, cols] = attn
            if block < blocks - 1:
                kept = jnp.where(keep, k.astype(F32), 0.0).astype(jnp.bfloat16)
                state = lax.dot_general(kept, v, (((0,), (0,)), ((), ())), preferred_element_type=F32)
                carries[head] = state + go_on * carries[head]


def local_attention(meta, starts, queries, keys, values, chunk, chunks):
    tokens, width = queries.shape
    wide = width // chunks
    steps = wide // (2 * DH)
    block = pl.BlockSpec((tokens, 2 * DH), lambda step, meta: (0, chunk * steps + step))
    heads = wide // DH
    return pl.pallas_call(
        local_kernel,
        out_shape=jax.ShapeDtypeStruct((tokens, wide), F32),
        grid_spec=pltpu.PrefetchScalarGridSpec(
            num_scalar_prefetch=1,
            grid=(steps,),
            in_specs=[pl.BlockSpec(starts.shape, lambda step, meta: (0, 0)), block, block, block],
            out_specs=pl.BlockSpec((tokens, 2 * DH), lambda step, meta: (0, step)),
        ),
        compiler_params=params(24),
        cost_estimate=pl.CostEstimate(
            flops=heads * tokens * (4 * GROUP + 4 * DH) * DH,
            bytes_accessed=tokens * wide * 10,
            transcendentals=0,
        ),
    )(meta, starts, queries, keys, values)


def finish_kernel(meta, *refs, chunks):
    locals_ = refs[:chunks]
    q_ref, mine, got = refs[chunks : chunks + 3]
    outs = refs[chunks + 3 : 2 * chunks + 3]
    squares = refs[2 * chunks + 3]
    states = refs[2 * chunks + 4]
    tokens, width = q_ref.shape
    pairs = width // (2 * DH)
    wide = width // chunks
    on_first = meta[CORE] == 0
    states[...] = jnp.zeros_like(states)
    for pair in range(pairs):
        low = pair < pairs // 2
        at = (pair % (pairs // 2)) * 2 * DH
        for side in range(2):
            rows = slice(at + side * DH, at + (side + 1) * DH)
            one = jnp.where(on_first, mine[rows, :], got[rows, :])
            two = jnp.where(on_first, got[rows, :], mine[rows, :])
            state = one if low else two
            states[pair, side * DH : (side + 1) * DH, side * DH : (side + 1) * DH] = state.astype(jnp.bfloat16)

    def block(index, _):
        at = pl.multiple_of(index * GROUP, GROUP)
        rows = pl.ds(at, GROUP)
        place = at + lax.broadcasted_iota(jnp.int32, (GROUP, 2 * DH), 0)
        usable = place < meta[8]
        total = jnp.zeros((GROUP, DH), F32)
        for pair in range(pairs):
            col = pair * 2 * DH
            cols = slice(col % wide, col % wide + 2 * DH)
            inter = jnp.dot(q_ref[rows, col : col + 2 * DH], states[pair], preferred_element_type=F32)
            attn = locals_[col // wide][rows, cols] + jnp.where(usable, inter, 0.0)
            outs[col // wide][rows, cols] = attn
            total = total + attn[:, :DH] * attn[:, :DH] + attn[:, DH:] * attn[:, DH:]
        squares[:, pl.ds(at, GROUP)] = jnp.sum(total.T, axis=0, keepdims=True)
        return 0

    lax.fori_loop(0, tokens // GROUP, block, 0)


def finish(meta, locals_, queries, mine, got):
    tokens, width = queries.shape
    chunks = len(locals_)
    wide = width // chunks
    *outs, squares = pl.pallas_call(
        functools.partial(finish_kernel, chunks=chunks),
        out_shape=[pltpu.VMEM((tokens, wide), F32)] * chunks + [jax.ShapeDtypeStruct((1, tokens), F32)],
        in_specs=[SMEM] + [VMEM] * (chunks + 3),
        out_specs=[VMEM] * (chunks + 1),
        scratch_shapes=[pltpu.VMEM((width // (2 * DH), 2 * DH, 2 * DH), jnp.bfloat16)],
        input_output_aliases={1 + c: c for c in range(chunks)},
        compiler_params=params(24),
        cost_estimate=pl.CostEstimate(
            flops=2 * tokens * width * DH, bytes_accessed=tokens * width * 6, transcendentals=0
        ),
    )(meta, *[pltpu.with_memory_space_constraint(v, pltpu.VMEM) for v in locals_], pltpu.with_memory_space_constraint(queries, pltpu.VMEM), mine, got)
    return outs, squares


def norm_kernel(total_ref, gain_ref, *refs, chunks, rows):
    ins = refs[:chunks]
    out, buffer, sems = refs[chunks:]
    tokens = ins[0].shape[0]
    wide = ins[0].shape[1]
    width = wide * chunks

    def copy(index, slot):
        return pltpu.make_async_copy(
            buffer.at[slot], out.at[pl.ds(index * rows, rows), :], sems.at[slot]
        )

    steps = tokens // rows
    for index in range(steps):
        slot = index % 2
        if index >= 2:
            copy(index - 2, slot).wait()
        span = slice(index * rows, (index + 1) * rows)
        mean = total_ref[:, span] / float(HEADS * DH)
        factor = jnp.broadcast_to(lax.rsqrt(mean + EPS), (DH, rows)).T
        for col in range(0, width, DH):
            cols = slice(col % wide, col % wide + DH)
            value = ins[col // wide][span, cols] * factor * gain_ref[:, col : col + DH]
            buffer[slot, :, col : col + DH] = value.astype(jnp.bfloat16)
        copy(index, slot).start()
    for index in range(steps - 2, steps):
        copy(index, index % 2).wait()


def normalise(total, gain, parts):
    tokens, wide = parts[0].shape
    chunks = len(parts)
    width = wide * chunks
    rows = 128
    return pl.pallas_call(
        functools.partial(norm_kernel, chunks=chunks, rows=rows),
        out_shape=jax.ShapeDtypeStruct((tokens, width), jnp.bfloat16),
        in_specs=[VMEM] * (chunks + 2),
        out_specs=ANY,
        scratch_shapes=[pltpu.VMEM((2, rows, width), jnp.bfloat16), pltpu.SemaphoreType.DMA((2,))],
        compiler_params=params(16),
        cost_estimate=pl.CostEstimate(flops=2 * tokens * width, bytes_accessed=6 * tokens * width, transcendentals=0),
    )(total, gain, *[pltpu.with_memory_space_constraint(v, pltpu.VMEM) for v in parts])


def on_device(queries, keys, values, doc_start, norm_gain):
    tokens, width = queries.shape
    seq = lax.axis_index("seq")
    base = seq * tokens
    core = lax.rem(seq, 2)
    chip = seq // 2
    meta = jnp.stack(
        [core, lax.rem(chip, SEQ_Y), chip // SEQ_Y, base, doc_start[0], doc_start[-1], chip * 2 * tokens, jnp.int32(tokens)]
    )
    opened = jnp.sum((doc_start < base).astype(jnp.int32))
    full_meta = jnp.concatenate([meta, opened[None]])
    starts = doc_start.reshape(tokens // GROUP, GROUP)

    away = half_state(meta, keys, values, True)
    recv = swap_cores(away)
    keep = half_state(meta, keys, values, False)
    part = (keep.shape[0] - 8) // SEQ_Y

    chunks = 4
    local = functools.partial(local_attention, meta, starts, queries, keys, values, chunks=chunks)

    mine = small(cores_kernel, meta, (keep, recv), [part + 8] * SEQ_Y)
    rows = [mine[0]] + [turn_row(mine[d], d) for d in (1, 2, 3)]
    locals_ = [local(0), local(1)]
    (whole,) = small(row_kernel, meta, rows, [part])
    ups = [next_rows(whole, d) for d in (1, 2, 3)]
    locals_.append(local(2))
    carries = small(carry_kernel, meta, (*rows, *ups), [part] * SEQ_Y)
    got = [carries[0]] + [turn_row(carries[d], d) for d in (1, 2, 3)]
    locals_.append(local(3))
    own, send = small(spread_kernel, meta, (*got, keep, recv), [part * SEQ_Y] * 2)
    other = swap_cores(send)
    parts, squares = finish(full_meta, locals_, queries, own, other)
    total = lax.psum(squares, "head")
    return normalise(total, norm_gain.reshape(1, width), parts)


def solution(mesh):
    return jax.shard_map(
        on_device,
        mesh=mesh,
        in_specs=(P("seq", "head"), P("seq", "head"), P("seq", "head"), P("seq"), P("head")),
        out_specs=P("seq", "head"),
        check_vma=False,
    )
```

time: 691 us -> 118 us (0.17)
  waiting for transfers between devices: 505 us -> 14.6 us
  starting transfers between devices: 59.5 us -> 18.4 us
  Pallas kernels: 0 us -> 40.9 us
  matrix products: 32.3 us -> 0 us
  other arithmetic: 25.8 us -> 0.71 us
  local copies, waits for them, and re-layouts: 47 us -> 30.1 us
  between operations: 7.6 us -> 0.41 us
    ppermute x31 -> x11, waiting for transfers between devices: 505 us -> 14.6 us  [the longest x6 9.44 us: turn_row(): lax.ppermute(value, 'seq', [(device_of(x, y, c), device_of(x, (y + steps)...]
    ppermute x31 -> x11, starting transfers between devices: 59.5 us -> 18.4 us  [the longest x6 11 us: turn_row(): lax.ppermute(value, 'seq', [(device_of(x, y, c), device_of(x, (y + steps)...]
    pallas_call x0 -> x12, Pallas kernels: none -> 40.9 us  [the longest x4 18.1 us: local_attention(): pl.pallas_call(local_kernel, out_shape=jax.ShapeDtypeStruct((tokens, wide...]
    dot_general x3 -> x0, matrix products: 32.3 us -> none  [the longest x1 16.2 us: on_device(): jnp.einsum('chtj,cjhe->cthe', scores, vs, preferred_element_type=jnp.floa...]
    add x1 -> x0, local copies, waits for them, and re-layouts: 12.8 us -> none  [on_device(): attn = intra + jnp.where(usable[:, :, None, None], inter, 0.0)]
    convert_element_type x2 -> x0, other arithmetic: 11.5 us -> none  [the longest x1 11.5 us: on_device(): return (attn * factor[:, None] * norm_gain[None, :]).astype(jnp.bfloat16)]
    reshape x1, local copies, waits for them, and re-layouts: 9.06 us -> 0.01 us  [on_device(): starts = doc_start.reshape(tokens // GROUP, GROUP)]
    unnamed x21 -> x34, local copies, waits for them, and re-layouts: 23.5 us -> 25.4 us
  transfers between devices with their start and end apart: 31 -> 11, of which waited for: 31 -> 7; matrix products, arithmetic and copies ran while one was open for 0% -> 2% of each run, Pallas kernels for 0% -> 18%
where the time goes in v1:
time: 118 us; the launch traced here: 117 us
  Pallas kernels  40.9 us (35%)
  local copies, waits for them, and re-layouts  30.1 us (26%)
  starting transfers between devices  18.4 us (16%)
  waiting for transfers between devices  14.6 us (12%)
  blocking collectives  11.8 us (10%)
    unnamed x34, local copies, waits for them, and re-layouts  25.4 us
    pallas_call x4, Pallas kernels, local_attention(): pl.pallas_call(local_kernel, out_shape=jax.ShapeDtypeStruct((tokens, wide...  18.1 us
    psum x1, blocking collectives, on_device(): total = lax.psum(squares, 'head')  11.8 us
    ppermute x6, starting transfers between devices, turn_row(): lax.ppermute(value, 'seq', [(device_of(x, y, c), device_of(x, (y + steps)...  11 us
    ppermute x6, waiting for transfers between devices, turn_row(): lax.ppermute(value, 'seq', [(device_of(x, y, c), device_of(x, (y + steps)...  9.44 us
    ppermute x3, starting transfers between devices, next_rows(): lax.ppermute(value, 'seq', [(device_of(x, y, c), device_of(x + steps, y,...  7.25 us
    pallas_call x2, Pallas kernels, half_state(): pl.pallas_call(state_kernel, out_shape=jax.ShapeDtypeStruct((rows, DH), F...  6.72 us
    pallas_call x1, Pallas kernels, finish(): pl.pallas_call(functools.partial(finish_kernel, chunks=chunks), out_shape...  6.28 us
  transfers between devices with their start and end apart: 11, of which 7 were waited for; matrix products, arithmetic and copies ran while one was open for 2% of the time, Pallas kernels for 18%

profile of v1, /device:TPU:2, one launch (start us, length us, event | category | flops | bytes accessed | tf_op | source)
XLA Modules:
  0.0 116.8 jit_solution(1754693537321436709)
XLA Ops:
  2.7 2.8 %copy-done = bf16[1536,2048]{1,0:T(8,128)(2,1)S(1)} copy-done((bf16[1536,2048]{1,0:T(8,128)(2,1)S(1)}, bf16[1536,2048]{1,0:T(8,128)(2,1)}, u32[]{:S(2)}) %copy-start) | copy-done | bytes 6291480
  5.4 2.8 %copy-done.2 = bf16[1536,2048]{1,0:T(8,128)(2,1)S(1)} copy-done((bf16[1536,2048]{1,0:T(8,128)(2,1)S(1)}, bf16[1536,2048]{1,0:T(8,128)(2,1)}, u32[]{:S(2)}) %copy-start.2) | copy-done | bytes 6291480
  8.2 3.4 %shard_map.60 = f32[1032,128]{1,0:T(8,128)S(1)} custom-call(s32[8]{0:T(128)S(1)} %stack.23.meta, bf16[1536,2048]{1,0:T(8,128)(2,1)S(1)} %copy-done, bf16[1536,2048]{1,0:T(8,128)(2,1)S(1)} %copy-done.2), custom_call_target="tpu_custom_call" | custom-call | flops 402653184 | bytes 6291456 | tf_op jit(solution)/shard_map/pallas_call | solution.py:86
  11.7 3.4 %shard_map.59.keep = f32[1032,128]{1,0:T(8,128)S(1)} custom-call(s32[8]{0:T(128)S(1)} %stack.23.meta, bf16[1536,2048]{1,0:T(8,128)(2,1)S(1)} %copy-done, bf16[1536,2048]{1,0:T(8,128)(2,1)S(1)} %copy-done.2), custom_call_target="tpu_custom_call" | custom-call | flops 402653184 | bytes 6291456 | tf_op jit(solution)/shard_map/pallas_call | solution.py:86
  17.4 2.9 %collective-permute-start.2 = (f32[264,128]{1,0:T(8,128)S(1)}, f32[264,128]{1,0:T(8,128)S(1)}, u32[]{:S(2)}, u32[]{:S(2)}) collective-permute-start(f32[264,128]{1,0:T(8,128)S(1)} %get-tuple-element.22), channel_id=1, source_target_pairs={{0,16},{4,20},{8,24},{12,28},{16,0},{20,4},{24,8},{28,12},{32,48},... | collective-permute-start | bytes 405512 | tf_op jit(solution)/shard_map/ppermute | solution.py:40
  23.0 4.1 %collective-permute-done.2.from2 = f32[264,128]{1,0:T(8,128)S(1)} collective-permute-done((f32[264,128]{1,0:T(8,128)S(1)}, f32[264,128]{1,0:T(8,128)S(1)}, u32[]{:S(2)}, u32[]{:S(2)}) %collective-permute-start.2) | collective-permute-done | bytes 135200 | tf_op jit(solution)/shard_map/ppermute | solution.py:40
  28.4 4.7 %collective-permute-start.5 = (f32[256,128]{1,0:T(8,128)S(1)}, f32[256,128]{1,0:T(8,128)S(1)}, u32[]{:S(2)}, u32[]{:S(2)}) collective-permute-start(f32[256,128]{1,0:T(8,128)S(1)} %shard_map.62), channel_id=1, source_target_pairs={{0,64},{4,68},{8,72},{12,76},{16,80},{20,84},{24,88},{28,92},{32,9... | collective-permute-start | bytes 393224 | tf_op jit(solution)/shard_map/ppermute | solution.py:48
  33.1 1.9 %collective-permute-start.4 = (f32[256,128]{1,0:T(8,128)S(1)}, f32[256,128]{1,0:T(8,128)S(1)}, u32[]{:S(2)}, u32[]{:S(2)}) collective-permute-start(f32[256,128]{1,0:T(8,128)S(1)} %shard_map.62), channel_id=1, source_target_pairs={{0,32},{4,36},{8,40},{12,44},{16,48},{20,52},{24,56},{28,60},{32,6... | collective-permute-start | bytes 393224 | tf_op jit(solution)/shard_map/ppermute | solution.py:48
  35.7 4.4 %collective-permute-done.4.up1 = f32[256,128]{1,0:T(8,128)S(1)} collective-permute-done((f32[256,128]{1,0:T(8,128)S(1)}, f32[256,128]{1,0:T(8,128)S(1)}, u32[]{:S(2)}, u32[]{:S(2)}) %collective-permute-start.4) | collective-permute-done | bytes 131104 | tf_op jit(solution)/shard_map/ppermute | solution.py:48
  42.1 2.7 %collective-permute-start.8 = (f32[256,128]{1,0:T(8,128)S(1)}, f32[256,128]{1,0:T(8,128)S(1)}, u32[]{:S(2)}, u32[]{:S(2)}) collective-permute-start(f32[256,128]{1,0:T(8,128)S(1)} %get-tuple-element.26), channel_id=1, source_target_pairs={{0,16},{4,20},{8,24},{12,28},{16,0},{20,4},{24,8},{28,12},{32,48},... | collective-permute-start | bytes 393224 | tf_op jit(solution)/shard_map/ppermute | solution.py:40
  46.0 2.4 %collective-permute-done.7.got1 = f32[256,128]{1,0:T(8,128)S(1)} collective-permute-done((f32[256,128]{1,0:T(8,128)S(1)}, f32[256,128]{1,0:T(8,128)S(1)}, u32[]{:S(2)}, u32[]{:S(2)}) %collective-permute-start.7) | collective-permute-done | bytes 131104 | tf_op jit(solution)/shard_map/ppermute | solution.py:40
  53.0 2.0 %concatenate.4.meta = s32[9]{0:T(128)S(1)} concatenate(s32[1]{0:T(128)} %bitcast, s32[1]{0:T(128)} %bitcast.1, s32[1]{0:T(128)} %bitcast.2, s32[1]{0:T(128)} %bitcast.3, s32[1]{0:T(128)} %get-tuple-element.36, s32[1]{0:T(128)} %get-tuple-element.35, s32[1]{0:T(128)} %bitcast.4, s32[1]{0:T(128)} %constant.37.clone.1, s32[1]{0:T(128)} %bitcast.5), dimensions={0} | concatenate | bytes 72 | tf_op jit(solution)/shard_map/concatenate | solution.py:368
  55.1 2.8 %copy-done.1 = bf16[1536,2048]{1,0:T(8,128)(2,1)S(1)} copy-done((bf16[1536,2048]{1,0:T(8,128)(2,1)S(1)}, bf16[1536,2048]{1,0:T(8,128)(2,1)}, u32[]{:S(2)}) %copy-start.1) | copy-done | bytes 6291480
  57.8 2.8 %copy-done.3 = bf16[1536,2048]{1,0:T(8,128)(2,1)S(1)} copy-done((bf16[1536,2048]{1,0:T(8,128)(2,1)S(1)}, bf16[1536,2048]{1,0:T(8,128)(2,1)}, u32[]{:S(2)}) %copy-start.3) | copy-done | bytes 6291480
  60.6 2.8 %copy-done.4 = bf16[1536,2048]{1,0:T(8,128)(2,1)S(1)} copy-done((bf16[1536,2048]{1,0:T(8,128)(2,1)S(1)}, bf16[1536,2048]{1,0:T(8,128)(2,1)}, u32[]{:S(2)}) %copy-start.4) | copy-done | bytes 6291480
  63.4 4.5 %shard_map.58.refs_3_ = f32[1536,512]{1,0:T(8,128)S(1)} custom-call(s32[8]{0:T(128)S(1)} %stack.23.meta, s32[6,256]{1,0:T(8,128)S(1)} %reshape.6.starts_ref, bf16[1536,2048]{1,0:T(8,128)(2,1)S(1)} %copy-done.4, bf16[1536,2048]{1,0:T(8,128)(2,1)S(1)} %copy-done.1, bf16[1536,2048]{1,0:T(8,128)(2,1)S(1)} %copy-done.3), custom_call_target="tpu_custom_call" | custom-call | flops 1207959552 | bytes 7864320 | tf_op jit(solution)/shard_map/pallas_call | solution.py:236
  67.9 4.5 %shard_map.57.refs_2_ = f32[1536,512]{1,0:T(8,128)S(1)} custom-call(s32[8]{0:T(128)S(1)} %stack.23.meta, s32[6,256]{1,0:T(8,128)S(1)} %reshape.6.starts_ref, bf16[1536,2048]{1,0:T(8,128)(2,1)S(1)} %copy-done.4, bf16[1536,2048]{1,0:T(8,128)(2,1)S(1)} %copy-done.1, bf16[1536,2048]{1,0:T(8,128)(2,1)S(1)} %copy-done.3), custom_call_target="tpu_custom_call" | custom-call | flops 1207959552 | bytes 7864320 | tf_op jit(solution)/shard_map/pallas_call | solution.py:236
  72.5 4.5 %shard_map.56.refs_1_ = f32[1536,512]{1,0:T(8,128)S(1)} custom-call(s32[8]{0:T(128)S(1)} %stack.23.meta, s32[6,256]{1,0:T(8,128)S(1)} %reshape.6.starts_ref, bf16[1536,2048]{1,0:T(8,128)(2,1)S(1)} %copy-done.4, bf16[1536,2048]{1,0:T(8,128)(2,1)S(1)} %copy-done.1, bf16[1536,2048]{1,0:T(8,128)(2,1)S(1)} %copy-done.3), custom_call_target="tpu_custom_call" | custom-call | flops 1207959552 | bytes 7864320 | tf_op jit(solution)/shard_map/pallas_call | solution.py:236
  77.1 4.5 %shard_map.55.refs_0_ = f32[1536,512]{1,0:T(8,128)S(1)} custom-call(s32[8]{0:T(128)S(1)} %stack.23.meta, s32[6,256]{1,0:T(8,128)S(1)} %reshape.6.starts_ref, bf16[1536,2048]{1,0:T(8,128)(2,1)S(1)} %copy-done.4, bf16[1536,2048]{1,0:T(8,128)(2,1)S(1)} %copy-done.1, bf16[1536,2048]{1,0:T(8,128)(2,1)S(1)} %copy-done.3), custom_call_target="tpu_custom_call" | custom-call | flops 1207959552 | bytes 7864320 | tf_op jit(solution)/shard_map/pallas_call | solution.py:236
  81.7 6.3 %shard_map.65 = (f32[1536,512]{1,0:T(8,128)S(1)}, f32[1536,512]{1,0:T(8,128)S(1)}, f32[1536,512]{1,0:T(8,128)S(1)}, f32[1536,512]{1,0:T(8,128)S(1)}, f32[1,1536]{1,0:T(1,128)S(1)}) custom-call(s32[9]{0:T(128)S(1)} %concatenate.4.meta, f32[1536,512]{1,0:T(8,128)S(1)} %shard_map.55.refs_0_, ...), custom_call_target="tpu_custom_call", output_to_operand_aliasing={{0}: (1, {}), {1}: (2, {}), {2}: (3, {}), {3}: (4, {})} | custom-call | flops 805306368 | bytes 18874368 | tf_op jit(solution)/shard_map/pallas_call | solution.py:298
  92.9 11.8 %psum.7.total_ref = f32[1,1536]{1,0:T(1,128)S(1)} all-reduce(f32[1,1536]{1,0:T(1,128)S(1)} %get-tuple-element.30), channel_id=1, replica_groups=mesh['seq'=32,'head'=4] {'head'}, use_global_device_ids=true, to_apply=%region_1.2 | all-reduce | flops 1536 | bytes 12288 | tf_op jit(solution)/shard_map/psum | solution.py:391
  106.7 1.9 %copy-done.8 = f32[1536,512]{1,0:T(8,128)S(1)} copy-done((f32[1536,512]{1,0:T(8,128)S(1)}, f32[1536,512]{1,0:T(8,128)}, u32[]{:S(2)}) %copy-start.8) | copy-done | bytes 3145752
  108.6 1.9 %copy-done.10 = f32[1536,512]{1,0:T(8,128)S(1)} copy-done((f32[1536,512]{1,0:T(8,128)S(1)}, f32[1536,512]{1,0:T(8,128)}, u32[]{:S(2)}) %copy-start.10) | copy-done | bytes 3145752
  110.4 6.2 %shard_map.66 = bf16[1536,2048]{1,0:T(8,128)(2,1)} custom-call(f32[1,1536]{1,0:T(1,128)S(1)} %psum.7.total_ref, f32[1,2048]{1,0:T(1,128)S(1)} %bitcast.9, f32[1536,512]{1,0:T(8,128)S(1)} %copy-done.10, f32[1536,512]{1,0:T(8,128)S(1)} %copy-done.8, f32[1536,512]{1,0:T(8,128)S(1)} %copy-done.6, f32[1536,512]{1,0:T(8,128)S(1)} %get-tuple-element.34.refs_3_), custom_call_target="tpu_custom_call" | custom-call | flops 6291456 | bytes 18874368 | tf_op jit(solution)/shard_map/pallas_call | solution.py:347
  (51 shorter events, 24.5 us)
Async XLA Ops:
  2.7 2.8 %copy-start = (bf16[1536,2048]{1,0:T(8,128)(2,1)S(1)}, bf16[1536,2048]{1,0:T(8,128)(2,1)}, u32[]{:S(2)}) copy-start(bf16[1536,2048]{1,0:T(8,128)(2,1)} %k_ref.11) | copy-start | bytes 18874372
  5.4 2.8 %copy-start.2 = (bf16[1536,2048]{1,0:T(8,128)(2,1)S(1)}, bf16[1536,2048]{1,0:T(8,128)(2,1)}, u32[]{:S(2)}) copy-start(bf16[1536,2048]{1,0:T(8,128)(2,1)} %v_ref.11) | copy-start | bytes 18874372
  11.6 34.4 %copy-start.14 = (s32[1536]{0:T(1024)S(1)}, s32[1536]{0:T(1024)}, u32[]{:S(2)}) copy-start(s32[1536]{0:T(1024)} %param.8) | copy-start | bytes 18436
  11.6 3.5 %collective-permute-start = (f32[1032,128]{1,0:T(8,128)S(1)}, f32[1032,128]{1,0:T(8,128)S(1)}, u32[]{:S(2)}, u32[]{:S(2)}) collective-permute-start(f32[1032,128]{1,0:T(8,128)S(1)} %shard_map.60), channel_id=1, source_target_pairs={{0,4},{4,0},{8,12},{12,8},{16,20},{20,16},{24,28},{28,24},{32,36},... | collective-permute-start | bytes 1585160 | tf_op jit(solution)/shard_map/ppermute | solution.py:34
  15.7 7.3 %collective-permute-start.1 = (f32[264,128]{1,0:T(8,128)S(1)}, f32[264,128]{1,0:T(8,128)S(1)}, u32[]{:S(2)}, u32[]{:S(2)}) collective-permute-start(f32[264,128]{1,0:T(8,128)S(1)} %get-tuple-element.21), channel_id=1, source_target_pairs={{0,8},{4,12},{8,16},{12,20},{16,24},{20,28},{24,0},{28,4},{32,40},... | collective-permute-start | bytes 405512 | tf_op jit(solution)/shard_map/ppermute | solution.py:40
  17.4 9.8 %collective-permute-start.2 = (f32[264,128]{1,0:T(8,128)S(1)}, f32[264,128]{1,0:T(8,128)S(1)}, u32[]{:S(2)}, u32[]{:S(2)}) collective-permute-start(f32[264,128]{1,0:T(8,128)S(1)} %get-tuple-element.22), channel_id=1, source_target_pairs={{0,16},{4,20},{8,24},{12,28},{16,0},{20,4},{24,8},{28,12},{32,48},... | collective-permute-start | bytes 405512 | tf_op jit(solution)/shard_map/ppermute | solution.py:40
  20.3 6.9 %collective-permute-start.3 = (f32[264,128]{1,0:T(8,128)S(1)}, f32[264,128]{1,0:T(8,128)S(1)}, u32[]{:S(2)}, u32[]{:S(2)}) collective-permute-start(f32[264,128]{1,0:T(8,128)S(1)} %get-tuple-element.23), channel_id=1, source_target_pairs={{0,24},{4,28},{8,0},{12,4},{16,8},{20,12},{24,16},{28,20},{32,56},... | collective-permute-start | bytes 405512 | tf_op jit(solution)/shard_map/ppermute | solution.py:40
  27.7 7.3 %collective-permute-start.6 = (f32[256,128]{1,0:T(8,128)S(1)}, f32[256,128]{1,0:T(8,128)S(1)}, u32[]{:S(2)}, u32[]{:S(2)}) collective-permute-start(f32[256,128]{1,0:T(8,128)S(1)} %shard_map.62), channel_id=1, source_target_pairs={{0,96},{4,100},{8,104},{12,108},{16,112},{20,116},{24,120},{28,124... | collective-permute-start | bytes 393224 | tf_op jit(solution)/shard_map/ppermute | solution.py:48
  28.4 7.3 %collective-permute-start.5 = (f32[256,128]{1,0:T(8,128)S(1)}, f32[256,128]{1,0:T(8,128)S(1)}, u32[]{:S(2)}, u32[]{:S(2)}) collective-permute-start(f32[256,128]{1,0:T(8,128)S(1)} %shard_map.62), channel_id=1, source_target_pairs={{0,64},{4,68},{8,72},{12,76},{16,80},{20,84},{24,88},{28,92},{32,9... | collective-permute-start | bytes 393224 | tf_op jit(solution)/shard_map/ppermute | solution.py:48
  33.1 7.0 %collective-permute-start.4 = (f32[256,128]{1,0:T(8,128)S(1)}, f32[256,128]{1,0:T(8,128)S(1)}, u32[]{:S(2)}, u32[]{:S(2)}) collective-permute-start(f32[256,128]{1,0:T(8,128)S(1)} %shard_map.62), channel_id=1, source_target_pairs={{0,32},{4,36},{8,40},{12,44},{16,48},{20,52},{24,56},{28,60},{32,6... | collective-permute-start | bytes 393224 | tf_op jit(solution)/shard_map/ppermute | solution.py:48
  40.9 7.6 %collective-permute-start.7 = (f32[256,128]{1,0:T(8,128)S(1)}, f32[256,128]{1,0:T(8,128)S(1)}, u32[]{:S(2)}, u32[]{:S(2)}) collective-permute-start(f32[256,128]{1,0:T(8,128)S(1)} %get-tuple-element.25), channel_id=1, source_target_pairs={{0,8},{4,12},{8,16},{12,20},{16,24},{20,28},{24,0},{28,4},{32,40},... | collective-permute-start | bytes 393224 | tf_op jit(solution)/shard_map/ppermute | solution.py:40
  42.1 7.8 %collective-permute-start.8 = (f32[256,128]{1,0:T(8,128)S(1)}, f32[256,128]{1,0:T(8,128)S(1)}, u32[]{:S(2)}, u32[]{:S(2)}) collective-permute-start(f32[256,128]{1,0:T(8,128)S(1)} %get-tuple-element.26), channel_id=1, source_target_pairs={{0,16},{4,20},{8,24},{12,28},{16,0},{20,4},{24,8},{28,12},{32,48},... | collective-permute-start | bytes 393224 | tf_op jit(solution)/shard_map/ppermute | solution.py:40
  44.7 5.3 %collective-permute-start.9 = (f32[256,128]{1,0:T(8,128)S(1)}, f32[256,128]{1,0:T(8,128)S(1)}, u32[]{:S(2)}, u32[]{:S(2)}) collective-permute-start(f32[256,128]{1,0:T(8,128)S(1)} %get-tuple-element.27), channel_id=1, source_target_pairs={{0,24},{4,28},{8,0},{12,4},{16,8},{20,12},{24,16},{28,20},{32,56},... | collective-permute-start | bytes 393224 | tf_op jit(solution)/shard_map/ppermute | solution.py:40
  52.3 29.3 %collective-permute-start.10 = (f32[1024,128]{1,0:T(8,128)}, f32[1024,128]{1,0:T(8,128)}, u32[]{:S(2)}, u32[]{:S(2)}) collective-permute-start(f32[1024,128]{1,0:T(8,128)} %get-tuple-element.29), channel_id=1, source_target_pairs={{0,4},{4,0},{8,12},{12,8},{16,20},{20,16},{24,28},{28,24},{32,36},... | collective-permute-start | bytes 1572872 | tf_op jit(solution)/shard_map/ppermute | solution.py:34
  55.1 2.8 %copy-start.1 = (bf16[1536,2048]{1,0:T(8,128)(2,1)S(1)}, bf16[1536,2048]{1,0:T(8,128)(2,1)}, u32[]{:S(2)}) copy-start(bf16[1536,2048]{1,0:T(8,128)(2,1)} %k_ref.11) | copy-start | bytes 18874372
  57.8 2.8 %copy-start.3 = (bf16[1536,2048]{1,0:T(8,128)(2,1)S(1)}, bf16[1536,2048]{1,0:T(8,128)(2,1)}, u32[]{:S(2)}) copy-start(bf16[1536,2048]{1,0:T(8,128)(2,1)} %v_ref.11) | copy-start | bytes 18874372
  60.6 2.8 %copy-start.4 = (bf16[1536,2048]{1,0:T(8,128)(2,1)S(1)}, bf16[1536,2048]{1,0:T(8,128)(2,1)}, u32[]{:S(2)}) copy-start(bf16[1536,2048]{1,0:T(8,128)(2,1)} %refs_4_.1) | copy-start | bytes 18874372
  72.5 9.1 %slice-start = ((s8[6291456]{0:T(1024)(128)(4,1)}), s8[4194304]{0:T(1024)(128)(4,1)S(1)}, s32[]{:S(2)}) async-start(s8[6291456]{0:T(1024)(128)(4,1)} %bitcast.7), calls=%async_computation | async-start | bytes 8388608
  77.0 4.6 %slice-start.1 = ((s8[6291456]{0:T(1024)(128)(4,1)}), s8[2097152]{0:T(1024)(128)(4,1)S(1)}, s32[]{:S(2)}) async-start(s8[6291456]{0:T(1024)(128)(4,1)} %bitcast.7), calls=%async_computation.1 | async-start | bytes 4194304
  77.1 4.6 %copy-start.12 = (f32[1024,128]{1,0:T(8,128)S(1)}, f32[1024,128]{1,0:T(8,128)}, u32[]{:S(2)}) copy-start(f32[1024,128]{1,0:T(8,128)} %copy-done.11) | copy-start | bytes 1572868
  81.6 23.1 %copy-start.13 = (f32[2048]{0:T(1024)S(1)}, f32[2048]{0:T(1024)}, u32[]{:S(2)}) copy-start(f32[2048]{0:T(1024)} %param.9) | copy-start | bytes 24580
  104.8 1.9 %copy-start.6 = (f32[1536,512]{1,0:T(8,128)S(1)}, f32[1536,512]{1,0:T(8,128)}, u32[]{:S(2)}) copy-start(f32[1536,512]{1,0:T(8,128)} %copy-done.5) | copy-start | bytes 9437188
  106.7 1.9 %copy-start.8 = (f32[1536,512]{1,0:T(8,128)S(1)}, f32[1536,512]{1,0:T(8,128)}, u32[]{:S(2)}) copy-start(f32[1536,512]{1,0:T(8,128)} %copy-done.7) | copy-start | bytes 9437188
  108.6 1.9 %copy-start.10 = (f32[1536,512]{1,0:T(8,128)S(1)}, f32[1536,512]{1,0:T(8,128)}, u32[]{:S(2)}) copy-start(f32[1536,512]{1,0:T(8,128)} %copy-done.9) | copy-start | bytes 9437188
  (4 other events, 5.8 us)

commit v2 on v0

v2 whole, which is shorter than its diff:
```python
import functools

import jax
import jax.numpy as jnp
from jax import lax
from jax.experimental import pallas as pl
from jax.experimental.pallas import tpu as pltpu
from jax.sharding import PartitionSpec as P

HEADS = 64
DH = 128
GROUP = 256
EPS = 1e-06
SEQ_Y = 4
SEQ_X = 4
MIB = 1 << 20
ANY = pl.BlockSpec(memory_space=pl.ANY)
VMEM = pl.BlockSpec(memory_space=pltpu.VMEM)
SMEM = pl.BlockSpec(memory_space=pltpu.SMEM)
F32 = jnp.float32


def device_of(x, y, core):
    return (x * SEQ_Y + y) * 2 + core


def places():
    return [(x, y, c) for x in range(SEQ_X) for y in range(SEQ_Y) for c in range(2)]


def swap_cores(value):
    return lax.ppermute(
        value, "seq", [(device_of(x, y, c), device_of(x, y, 1 - c)) for x, y, c in places()]
    )


def turn_row(value, steps):
    return lax.ppermute(
        value,
        "seq",
        [(device_of(x, y, c), device_of(x, (y + steps) % SEQ_Y, c)) for x, y, c in places()],
    )


def swap_rows(value, steps):
    return lax.ppermute(
        value, "seq", [(device_of(x, y, c), device_of(x ^ steps, y, c)) for x, y, c in places()]
    )


def params(limit):
    return pltpu.CompilerParams(vmem_limit_bytes=limit * MIB)


def in_hbm(value):
    return pltpu.with_memory_space_constraint(value, pltpu.HBM)


def in_vmem(value):
    return pltpu.with_memory_space_constraint(value, pltpu.VMEM)


def after(value, *others):
    return lax.optimization_barrier((value, *others))[0]


def spot():
    seq = lax.axis_index("seq")
    chip = lax.div(seq, 2)
    return lax.rem(seq, 2), lax.rem(chip, SEQ_Y), lax.div(chip, SEQ_Y), seq


def halves(core, half):
    return [pl.multiple_of(side * half, half) for side in (1 - core, core)]


def state_kernel(starts_hbm, k_hbm, v_hbm, away, keep, k_ref, v_ref, starts, sems, starts_sem):
    tokens, width = k_ref.shape
    half = width // 2
    core, _, _, seq = spot()
    base = seq * tokens
    steps = tokens // GROUP
    starts_copy = pltpu.make_async_copy(starts_hbm, starts.at[0], starts_sem)

    def copies(step):
        rows = pl.ds(pl.multiple_of(step * GROUP, GROUP), GROUP)
        return [
            pltpu.make_async_copy(source.at[rows, :], ref.at[rows, :], sems.at[index, step])
            for index, (source, ref) in enumerate(((k_hbm, k_ref), (v_hbm, v_ref)))
        ]

    starts_copy.start()
    for step in range(steps):
        for copy in copies(step):
            copy.start()
    for out in (away, keep):
        out[...] = jnp.zeros_like(out)
    row = lax.broadcasted_iota(jnp.int32, (8, DH), 0)
    place = lax.broadcasted_iota(jnp.int32, (GROUP, 2 * DH), 0)
    starts_copy.wait()
    first = jnp.broadcast_to(starts[:, :1], (1, DH))
    last = jnp.broadcast_to(starts[:, tokens - 1 :], (1, DH))
    for out in (away, keep):
        out[half:, :] = jnp.where(row == 0, first, last).astype(F32)
    last = jnp.broadcast_to(jnp.concatenate([last, last], axis=1), (GROUP, 2 * DH))

    def body(step, _):
        for copy in copies(step):
            copy.wait()
        at = pl.multiple_of(step * GROUP, GROUP)
        rows = pl.ds(at, GROUP)
        kept = jnp.where(base + at + place >= last, 1.0, 0.0).astype(jnp.bfloat16)
        for out, side in zip((away, keep), halves(core, half)):
            for col in range(0, half, 2 * DH):
                cols = pl.ds(side + col, 2 * DH)
                both = lax.dot_general(
                    k_ref[rows, cols] * kept, v_ref[rows, cols], (((0,), (0,)), ((), ())), preferred_element_type=F32
                )
                out[col : col + DH, :] += both[:DH, :DH]
                out[col + DH : col + 2 * DH, :] += both[DH:, DH:]
        return 0

    lax.fori_loop(0, steps, body, 0)


def own_states(starts, keys, values):
    tokens, width = keys.shape
    state = pltpu.VMEM((width // 2 + 8, DH), F32)
    held = pltpu.VMEM((tokens, width), jnp.bfloat16)
    return pl.pallas_call(
        state_kernel,
        out_shape=[state, state, held, held, pltpu.VMEM((1, tokens), jnp.int32)],
        in_specs=[ANY, ANY, ANY],
        out_specs=[VMEM] * 5,
        scratch_shapes=[
            pltpu.SemaphoreType.DMA((2, tokens // GROUP)),
            pltpu.SemaphoreType.DMA,
        ],
        compiler_params=params(4),
        cost_estimate=pl.CostEstimate(
            flops=2 * tokens * width * DH, bytes_accessed=4 * tokens * width, transcendentals=0
        ),
    )(in_hbm(starts), in_hbm(keys), in_hbm(values))


def marks(ref):
    at = ref.shape[0] - 8
    return ref[at : at + 1, :], ref[at + 1 : at + 2, :]


def chip_edges(tokens, seq):
    first = lax.div(seq, 2) * (2 * tokens)
    return first.astype(F32), (first + tokens).astype(F32)


def cores_kernel(keep, recv, own, to1, to2, to3, *, tokens):
    total = keep.shape[0] - 8
    part = total // SEQ_Y
    core, y, _, seq = spot()
    on_first = core == 0
    k_first, k_last = marks(keep)
    r_first, r_last = marks(recv)
    first = jnp.where(on_first, k_first, r_first)
    last = jnp.where(on_first, r_last, k_last)
    edge = chip_edges(tokens, seq)[1]
    joined = jnp.where(last < edge, 1.0, 0.0)
    w_keep = jnp.where(on_first, joined, 1.0)
    w_recv = jnp.where(on_first, 1.0, joined)
    row = lax.broadcasted_iota(jnp.int32, (8, DH), 0)
    flags = jnp.where(row == 0, first, last)
    for steps, out in enumerate((own, to1, to2, to3)):
        at = pl.multiple_of(lax.rem(y + steps, SEQ_Y) * part, part)
        out[:part, :] = keep[pl.ds(at, part), :] * w_keep + recv[pl.ds(at, part), :] * w_recv
        out[part:, :] = flags


def sources(y):
    return [lax.rem(y + SEQ_Y - d, SEQ_Y) for d in range(SEQ_Y)]


def ends(tokens, x, place):
    return ((x * SEQ_Y + place + 1) * (2 * tokens)).astype(F32)


def row_kernel(own, from1, from2, from3, out, *, tokens):
    part = out.shape[0]
    refs = (own, from1, from2, from3)
    _, y, x, _ = spot()
    where = sources(y)
    row_last = jnp.zeros((1, DH), F32)
    for place, ref in zip(where, refs):
        row_last = row_last + jnp.where(place == SEQ_Y - 1, marks(ref)[1], 0.0)
    total = jnp.zeros((part, DH), F32)
    for place, ref in zip(where, refs):
        total = total + ref[:part, :] * jnp.where(row_last < ends(tokens, x, place), 1.0, 0.0)
    out[...] = total


def carry_kernel(own, from1, from2, from3, up3, up2, up1, out0, out1, out2, out3, *, tokens):
    part = out0.shape[0]
    refs = (own, from1, from2, from3)
    ups = (up3, up2, up1)
    _, y, x, _ = spot()
    where = sources(y)
    for steps, out in enumerate((out0, out1, out2, out3)):
        target = (SEQ_Y - steps) % SEQ_Y
        place = where[target]
        first = marks(refs[target])[0]
        total = jnp.zeros((part, DH), F32)
        for source in range(SEQ_Y):
            if source != target:
                before = jnp.where(where[source] < place, 1.0, 0.0)
                weight = jnp.where(first < ends(tokens, x, where[source]), before, 0.0)
                total = total + refs[source][:part, :] * weight
        for steps, ref in zip((3, 2, 1), ups):
            row = x ^ steps
            before = jnp.where(row < x, 1.0, 0.0)
            total = total + ref[...] * jnp.where(first < ends(tokens, row, SEQ_Y - 1), before, 0.0)
        out[...] = total


def spread_kernel(own, got1, got2, got3, keep, recv, mine, send, *, tokens):
    part = own.shape[0]
    core, y, _, seq = spot()
    on_first = core == 0
    chip, edge = chip_edges(tokens, seq)
    second_first = jnp.where(on_first, marks(recv)[0], marks(keep)[0])
    w_state = jnp.where(second_first < edge, 1.0, 0.0)
    w_carry = jnp.where(second_first < chip, 1.0, 0.0)
    w_keep = jnp.where(on_first, w_state, 0.0)
    w_recv = jnp.where(on_first, 0.0, w_state)
    for place, ref in zip(sources(y), (own, got1, got2, got3)):
        at = pl.multiple_of(place * part, part)
        carry = ref[...]
        later = keep[pl.ds(at, part), :] * w_keep + recv[pl.ds(at, part), :] * w_recv + carry * w_carry
        mine[pl.ds(at, part), :] = jnp.where(on_first, carry, later)
        send[pl.ds(at, part), :] = jnp.where(on_first, later, carry)


def small(kernel, tokens, args, outs):
    return pl.pallas_call(
        functools.partial(kernel, tokens=tokens),
        out_shape=[jax.ShapeDtypeStruct((rows, DH), F32) for rows in outs],
        in_specs=[VMEM] * len(args),
        out_specs=[VMEM] * len(outs),
        compiler_params=params(4),
        cost_estimate=pl.CostEstimate(flops=0, bytes_accessed=2 * MIB, transcendentals=0),
    )(*args)


def local_kernel(starts_ref, q_ref, k_ref, v_ref, out_ref, *, kept, column):
    tokens, width = out_ref.shape
    core, _, _, seq = spot()
    side = halves(core, q_ref.shape[1] // 2)[kept] + column
    key_place = lax.broadcasted_iota(jnp.int32, (GROUP, GROUP), 1)
    query_place = lax.broadcasted_iota(jnp.int32, (GROUP, GROUP), 0)
    blocks = tokens // GROUP
    carries = [None] * (width // DH)
    for block in range(blocks):
        rows = slice(block * GROUP, (block + 1) * GROUP)
        first = seq * tokens + block * GROUP
        starts = starts_ref[:, rows]
        begin = jnp.broadcast_to(starts, (DH, GROUP)).T
        valid = (key_place <= query_place) & (key_place + first >= jnp.concatenate([begin, begin], axis=1))
        last = starts[:, GROUP - 1 :]
        keep = query_place[:, :DH] + first >= jnp.broadcast_to(last, (GROUP, DH))
        keep = jnp.where(keep, 1.0, 0.0).astype(jnp.bfloat16)
        usable = jnp.where(begin < first, 1.0, 0.0).astype(jnp.bfloat16)
        go_on = jnp.where(last < first, 1.0, 0.0)
        for head in range(width // DH):
            cols = pl.ds(side + head * DH, DH)
            q, k, v = q_ref[rows, cols], k_ref[rows, cols], v_ref[rows, cols]
            scores = lax.dot_general(q, k, (((1,), (1,)), ((), ())), preferred_element_type=F32)
            scores = jnp.where(valid, scores, 0.0).astype(jnp.bfloat16)
            if block < blocks - 1:
                both = jnp.dot(
                    jnp.concatenate([scores, (k * keep).T], axis=0), v, preferred_element_type=F32
                )
                attn, state = both[:GROUP], both[GROUP:]
            else:
                attn, state = jnp.dot(scores, v, preferred_element_type=F32), None
            if block:
                attn = attn + jnp.dot(q * usable, carries[head].astype(jnp.bfloat16), preferred_element_type=F32)
            out_ref[rows, head * DH : (head + 1) * DH] = attn
            if state is not None:
                carries[head] = state if block == 0 else state + go_on * carries[head]


def local_attention(starts, queries, keys, values, kept, column, wide):
    tokens = queries.shape[0]
    return pl.pallas_call(
        functools.partial(local_kernel, kept=kept, column=column),
        out_shape=pltpu.VMEM((tokens, wide), F32),
        in_specs=[VMEM] * 4,
        out_specs=VMEM,
        compiler_params=params(4),
        cost_estimate=pl.CostEstimate(
            flops=wide * tokens * (4 * GROUP + 4 * DH), bytes_accessed=tokens * wide * 10, transcendentals=0
        ),
    )(starts, in_vmem(queries), in_vmem(keys), in_vmem(values))


def finish_kernel(starts_ref, q_ref, *refs, sizes, rows):
    count = len(sizes)
    locals_, (away, own) = refs[:count], refs[count : count + 2]
    outs, squares, states = refs[count + 2 : 2 * count + 2], refs[2 * count + 2], refs[2 * count + 3]
    tokens, width = q_ref.shape
    half = width // 2
    core, _, _, seq = spot()
    opened = jnp.sum((starts_ref[...] < seq * tokens).astype(jnp.int32))
    pairs = []
    for index, size in enumerate(sizes):
        for col in range(0, size, 2 * DH):
            pairs.append((index, col))
    states[...] = jnp.zeros_like(states)
    for pair in range(len(pairs)):
        source = away if pair < len(pairs) // 2 else own
        at = pair * 2 * DH % half
        for side in range(2):
            span = slice(side * DH, (side + 1) * DH)
            states[pair, span, span] = source[at + side * DH : at + (side + 1) * DH, :].astype(jnp.bfloat16)
    sides = halves(core, half)

    def step(index, _):
        start = pl.multiple_of(index * rows, rows)
        span = pl.ds(start, rows)
        usable = start + lax.broadcasted_iota(jnp.int32, (rows, 2 * DH), 0) < opened
        total = jnp.zeros((rows, DH), F32)
        for pair, (part, col) in enumerate(pairs):
            side = sides[pair // (len(pairs) // 2)]
            q = q_ref[span, pl.ds(side + pair * 2 * DH % half, 2 * DH)]
            inter = jnp.dot(q, states[pair], preferred_element_type=F32)
            cols = slice(col, col + 2 * DH)
            attn = locals_[part][span, cols] + jnp.where(usable, inter, 0.0)
            outs[part][span, cols] = attn
            total = total + attn[:, :DH] * attn[:, :DH] + attn[:, DH:] * attn[:, DH:]
        squares[:, span] = jnp.sum(total.T, axis=0, keepdims=True)
        return 0

    lax.fori_loop(0, tokens // rows, step, 0)


def finish(starts, queries, locals_, away, own):
    tokens, width = queries.shape
    sizes = [part.shape[1] for part in locals_]
    count = len(sizes)
    *outs, squares = pl.pallas_call(
        functools.partial(finish_kernel, sizes=sizes, rows=2 * GROUP),
        out_shape=[pltpu.VMEM((tokens, size), F32) for size in sizes] + [jax.ShapeDtypeStruct((1, tokens), F32)],
        in_specs=[VMEM] * (count + 4),
        out_specs=[VMEM] * (count + 1),
        scratch_shapes=[pltpu.VMEM((width // (2 * DH), 2 * DH, 2 * DH), jnp.bfloat16)],
        compiler_params=params(8),
        cost_estimate=pl.CostEstimate(
            flops=2 * tokens * width * DH, bytes_accessed=tokens * width * 6, transcendentals=0
        ),
    )(starts, in_vmem(queries), *[in_vmem(part) for part in locals_], away, own)
    return outs, squares


def norm_kernel(sq0, sq1, sq2, sq3, gain_ref, *refs, sizes, rows):
    count = len(sizes)
    ins = refs[:count]
    out, buffer, sems = refs[count:]
    tokens, width = out.shape
    half = width // 2
    core = spot()[0]
    sides = halves(core, half)
    places = []
    for index, size in enumerate(sizes):
        for col in range(0, size, DH):
            places.append((index, col))

    def copy(index):
        at = pl.ds(pl.multiple_of(index * rows, rows), rows)
        return pltpu.make_async_copy(buffer.at[at, :], out.at[at, :], sems.at[index])

    def step(index, _):
        span = pl.ds(pl.multiple_of(index * rows, rows), rows)
        total = (sq0[:, span] + sq1[:, span]) + (sq2[:, span] + sq3[:, span])
        factor = jnp.broadcast_to(lax.rsqrt(total / (HEADS * DH) + EPS), (DH, rows)).T
        for number, (index_in, col) in enumerate(places):
            side = sides[number // (len(places) // 2)]
            cols = pl.ds(side + number * DH % half, DH)
            value = ins[index_in][span, col : col + DH] * factor * gain_ref[:, cols]
            buffer[span, cols] = value.astype(jnp.bfloat16)
        copy(index).start()
        return 0

    steps = tokens // rows
    lax.fori_loop(0, steps, step, 0)
    for index in range(steps):
        copy(index).wait()


def normalise(squares, gain, parts):
    tokens = parts[0].shape[0]
    sizes = [part.shape[1] for part in parts]
    width = sum(sizes)
    rows = 2 * DH
    return pl.pallas_call(
        functools.partial(norm_kernel, sizes=sizes, rows=rows),
        out_shape=jax.ShapeDtypeStruct((tokens, width), jnp.bfloat16),
        in_specs=[VMEM] * (len(sizes) + 5),
        out_specs=ANY,
        scratch_shapes=[
            pltpu.VMEM((tokens, width), jnp.bfloat16),
            pltpu.SemaphoreType.DMA((tokens // rows,)),
        ],
        compiler_params=params(8),
        cost_estimate=pl.CostEstimate(flops=2 * tokens * width, bytes_accessed=6 * tokens * width, transcendentals=0),
    )(*squares, gain, *[in_vmem(part) for part in parts])


def on_device(queries, keys, values, doc_start, norm_gain):
    tokens, width = queries.shape
    half = width // 2

    away, keep, keys, values, starts = own_states(doc_start, keys, values)
    recv = swap_cores(away)
    queries = after(queries, away)
    part = half // SEQ_Y

    def local(kept, column, wide, gate):
        return local_attention(after(starts, gate), queries, keys, values, kept, column, wide)

    mine = small(cores_kernel, tokens, (keep, recv), [part + 8] * SEQ_Y)
    rows = [mine[0]] + [turn_row(mine[d], d) for d in (1, 2, 3)]
    first = local(0, 0, 3 * half // 4, mine[0])
    rows[3], first = lax.optimization_barrier((rows[3], first))
    (whole,) = small(row_kernel, tokens, rows, [part])
    ups = [swap_rows(whole, d) for d in (3, 2, 1)]
    third = local(1, 0, half // 2, whole)
    ups[2], third = lax.optimization_barrier((ups[2], third))
    carries = small(carry_kernel, tokens, (*rows, *ups), [part] * SEQ_Y)
    got = [carries[0]] + [turn_row(carries[d], d) for d in (1, 2, 3)]
    fourth = local(1, half // 2, half // 2, carries[0])
    got[3], fourth = lax.optimization_barrier((got[3], fourth))
    own, send = small(spread_kernel, tokens, (*got, keep, recv), [part * SEQ_Y] * 2)
    other = swap_cores(send)
    second = local(0, 3 * half // 4, half // 4, own)
    parts, squares = finish(starts, queries, [first, second, third, fourth], other, own)
    sums = [squares] + [
        lax.ppermute(squares, "head", [(z, z ^ d) for z in range(4)]) for d in (3, 2, 1)
    ]
    return normalise(sums, norm_gain.reshape(1, width), parts)


def solution(mesh):
    return jax.shard_map(
        on_device,
        mesh=mesh,
        in_specs=(P("seq", "head"), P("seq", "head"), P("seq", "head"), P("seq"), P("head")),
        out_specs=P("seq", "head"),
        check_vma=False,
    )
```

time: 691 us -> 62.5 us (0.09)
  the two profiles are of different devices: /device:TPU:2 before, /device:TPU:0 now
where the time goes in v2:
time: 62.5 us; the launch traced here: 62.4 us
  Pallas kernels  28.6 us (46%)
  starting transfers between devices  19.8 us (32%)
  waiting for transfers between devices  13.7 us (22%)
    pallas_call x4, Pallas kernels, local_attention(): pl.pallas_call(functools.partial(local_kernel, kept=kept, column=column),...  12.7 us
    ppermute x6, starting transfers between devices, turn_row(): lax.ppermute(value, 'seq', [(device_of(x, y, c), device_of(x, (y + steps)...  9.23 us
    pallas_call x1, Pallas kernels, own_states(): pl.pallas_call(state_kernel, out_shape=[state, state, held, held, pltpu.V...  8.18 us
    ppermute x3, starting transfers between devices, on_device(): lax.ppermute(squares, 'head', [(z, z ^ d) for z in range(4)])  5.58 us
    ppermute x3, waiting for transfers between devices, on_device(): lax.ppermute(squares, 'head', [(z, z ^ d) for z in range(4)])  4.84 us
    ppermute x3, starting transfers between devices, swap_rows(): lax.ppermute(value, 'seq', [(device_of(x, y, c), device_of(x ^ steps, y,...  4.78 us
    ppermute x6, waiting for transfers between devices, turn_row(): lax.ppermute(value, 'seq', [(device_of(x, y, c), device_of(x, (y + steps)...  4.45 us
    pallas_call x1, Pallas kernels, normalise(): pl.pallas_call(functools.partial(norm_kernel, sizes=sizes, rows=rows), ou...  4 us
  transfers between devices with their start and end apart: 14, of which 8 were waited for; matrix products, arithmetic and copies ran while one was open for 0% of the time, Pallas kernels for 20%

profile of v2, /device:TPU:0, one launch (start us, length us, event | category | flops | bytes accessed | tf_op | source)
XLA Modules:
  0.0 62.4 jit_solution(2039144090398681079)
XLA Ops:
  0.0 8.2 %shard_map.55 = (f32[1032,128]{1,0:T(8,128)S(1)}, f32[1032,128]{1,0:T(8,128)S(1)}, bf16[1536,2048]{1,0:T(8,128)(2,1)S(1)}, bf16[1536,2048]{1,0:T(8,128)(2,1)S(1)}, s32[1,1536]{1,0:T(1,128)S(1)}) custom-call(s32[1536]{0:T(1024)} %starts_hbm.1, bf16[1536,2048]{1,0:T(8,128)(2,1)} %k_hbm.1, bf16[1536,2048]{1,0:T(8,128)(2,1)} %v_hbm.1), custom_call_target="tpu_custom_call" | custom-call | flops 805306368 | bytes 12582912 | tf_op jit(solution)/shard_map/pallas_call | solution.py:130
  8.3 1.9 %collective-permute-done.recv = f32[1032,128]{1,0:T(8,128)S(1)} collective-permute-done((f32[1032,128]{1,0:T(8,128)S(1)}, f32[1032,128]{1,0:T(8,128)S(1)}, u32[]{:S(2)}, u32[]{:S(2)}) %collective-permute-start) | collective-permute-done | bytes 528416 | tf_op jit(solution)/shard_map/ppermute | solution.py:32
  10.3 3.2 %collective-permute-start.1 = (f32[264,128]{1,0:T(8,128)S(1)}, f32[264,128]{1,0:T(8,128)S(1)}, u32[]{:S(2)}, u32[]{:S(2)}) collective-permute-start(f32[264,128]{1,0:T(8,128)S(1)} %get-tuple-element.40), channel_id=1, source_target_pairs={{0,24},{4,28},{8,0},{12,4},{16,8},{20,12},{24,16},{28,20},{32,56},... | collective-permute-start | bytes 405512 | tf_op jit(solution)/shard_map/ppermute | solution.py:38
  13.4 2.2 %collective-permute-start.3 = (f32[264,128]{1,0:T(8,128)S(1)}, f32[264,128]{1,0:T(8,128)S(1)}, u32[]{:S(2)}, u32[]{:S(2)}) collective-permute-start(f32[264,128]{1,0:T(8,128)S(1)} %get-tuple-element.47), channel_id=1, source_target_pairs={{0,16},{4,20},{8,24},{12,28},{16,0},{20,4},{24,8},{28,12},{32,48},... | collective-permute-start | bytes 405512 | tf_op jit(solution)/shard_map/ppermute | solution.py:38
  15.6 4.6 %shard_map.57.refs_0_ = f32[1536,768]{1,0:T(8,128)S(1)} custom-call(s32[1,1536]{1,0:T(1,128)S(1)} %get-tuple-element.58.starts_ref, bf16[1536,2048]{1,0:T(8,128)(2,1)S(1)} %copy-done, bf16[1536,2048]{1,0:T(8,128)(2,1)S(1)} %get-tuple-element.43.k_ref, bf16[1536,2048]{1,0:T(8,128)(2,1)S(1)} %get-tuple-element.44.v_ref), custom_call_target="tpu_custom_call" | custom-call | flops 1811939328 | bytes 11796480 | tf_op jit(solution)/shard_map/pallas_call | solution.py:291
  20.2 2.7 %collective-permute-done.2.from1 = f32[264,128]{1,0:T(8,128)S(1)} collective-permute-done((f32[264,128]{1,0:T(8,128)S(1)}, f32[264,128]{1,0:T(8,128)S(1)}, u32[]{:S(2)}, u32[]{:S(2)}) %collective-permute-start.2) | collective-permute-done | bytes 135200 | tf_op jit(solution)/shard_map/ppermute | solution.py:38
  23.0 1.6 %collective-permute-start.6 = (f32[256,128]{1,0:T(8,128)S(1)}, f32[256,128]{1,0:T(8,128)S(1)}, u32[]{:S(2)}, u32[]{:S(2)}) collective-permute-start(f32[256,128]{1,0:T(8,128)S(1)} %shard_map.58), channel_id=1, source_target_pairs={{0,32},{4,36},{8,40},{12,44},{16,48},{20,52},{24,56},{28,60},{32,0... | collective-permute-start | bytes 393224 | tf_op jit(solution)/shard_map/ppermute | solution.py:46
  24.5 2.7 %collective-permute-start.5 = (f32[256,128]{1,0:T(8,128)S(1)}, f32[256,128]{1,0:T(8,128)S(1)}, u32[]{:S(2)}, u32[]{:S(2)}) collective-permute-start(f32[256,128]{1,0:T(8,128)S(1)} %shard_map.58), channel_id=1, source_target_pairs={{0,64},{4,68},{8,72},{12,76},{16,80},{20,84},{24,88},{28,92},{32,9... | collective-permute-start | bytes 393224 | tf_op jit(solution)/shard_map/ppermute | solution.py:46
  27.3 0.5 collective-permute-start.4
  27.7 3.1 %shard_map.59.refs_2_ = f32[1536,512]{1,0:T(8,128)S(1)} custom-call(s32[1,1536]{1,0:T(1,128)S(1)} %get-tuple-element.58.starts_ref, bf16[1536,2048]{1,0:T(8,128)(2,1)S(1)} %copy-done, bf16[1536,2048]{1,0:T(8,128)(2,1)S(1)} %get-tuple-element.43.k_ref, bf16[1536,2048]{1,0:T(8,128)(2,1)S(1)} %get-tuple-element.44.v_ref), custom_call_target="tpu_custom_call" | custom-call | flops 1207959552 | bytes 7864320 | tf_op jit(solution)/shard_map/pallas_call | solution.py:291
  30.9 0.7 %collective-permute-done.5.up2 = f32[256,128]{1,0:T(8,128)S(1)} collective-permute-done((f32[256,128]{1,0:T(8,128)S(1)}, f32[256,128]{1,0:T(8,128)S(1)}, u32[]{:S(2)}, u32[]{:S(2)}) %collective-permute-start.5) | collective-permute-done | bytes 131104 | tf_op jit(solution)/shard_map/ppermute | solution.py:46
  31.6 1.8 %collective-permute-done.4.up3 = f32[256,128]{1,0:T(8,128)S(1)} collective-permute-done((f32[256,128]{1,0:T(8,128)S(1)}, f32[256,128]{1,0:T(8,128)S(1)}, u32[]{:S(2)}, u32[]{:S(2)}) %collective-permute-start.4) | collective-permute-done | bytes 131104 | tf_op jit(solution)/shard_map/ppermute | solution.py:46
  33.7 0.4 collective-permute-start.9
  34.1 1.7 %collective-permute-start.7 = (f32[256,128]{1,0:T(8,128)S(1)}, f32[256,128]{1,0:T(8,128)S(1)}, u32[]{:S(2)}, u32[]{:S(2)}) collective-permute-start(f32[256,128]{1,0:T(8,128)S(1)} %get-tuple-element.52), channel_id=1, source_target_pairs={{0,8},{4,12},{8,16},{12,20},{16,24},{20,28},{24,0},{28,4},{32,40},... | collective-permute-start | bytes 393224 | tf_op jit(solution)/shard_map/ppermute | solution.py:38
  35.8 1.8 %collective-permute-start.8 = (f32[256,128]{1,0:T(8,128)S(1)}, f32[256,128]{1,0:T(8,128)S(1)}, u32[]{:S(2)}, u32[]{:S(2)}) collective-permute-start(f32[256,128]{1,0:T(8,128)S(1)} %get-tuple-element.53), channel_id=1, source_target_pairs={{0,16},{4,20},{8,24},{12,28},{16,0},{20,4},{24,8},{28,12},{32,48},... | collective-permute-start | bytes 393224 | tf_op jit(solution)/shard_map/ppermute | solution.py:38
  37.6 3.1 %shard_map.61.refs_3_ = f32[1536,512]{1,0:T(8,128)S(1)} custom-call(s32[1,1536]{1,0:T(1,128)S(1)} %get-tuple-element.58.starts_ref, bf16[1536,2048]{1,0:T(8,128)(2,1)S(1)} %copy-done, bf16[1536,2048]{1,0:T(8,128)(2,1)S(1)} %get-tuple-element.43.k_ref, bf16[1536,2048]{1,0:T(8,128)(2,1)S(1)} %get-tuple-element.44.v_ref), custom_call_target="tpu_custom_call" | custom-call | flops 1207959552 | bytes 7864320 | tf_op jit(solution)/shard_map/pallas_call | solution.py:291
  41.1 1.4 %collective-permute-done.8.got2 = f32[256,128]{1,0:T(8,128)S(1)} collective-permute-done((f32[256,128]{1,0:T(8,128)S(1)}, f32[256,128]{1,0:T(8,128)S(1)}, u32[]{:S(2)}, u32[]{:S(2)}) %collective-permute-start.8) | collective-permute-done | bytes 131104 | tf_op jit(solution)/shard_map/ppermute | solution.py:38
  42.7 1.9 %shard_map.63.refs_1_ = f32[1536,256]{1,0:T(8,128)S(1)} custom-call(s32[1,1536]{1,0:T(1,128)S(1)} %get-tuple-element.58.starts_ref, bf16[1536,2048]{1,0:T(8,128)(2,1)S(1)} %copy-done, bf16[1536,2048]{1,0:T(8,128)(2,1)S(1)} %get-tuple-element.43.k_ref, bf16[1536,2048]{1,0:T(8,128)(2,1)S(1)} %get-tuple-element.44.v_ref), custom_call_target="tpu_custom_call" | custom-call | flops 603979776 | bytes 3932160 | tf_op jit(solution)/shard_map/pallas_call | solution.py:291
  44.6 3.1 %shard_map.64 = (f32[1536,768]{1,0:T(8,128)S(1)}, f32[1536,256]{1,0:T(8,128)S(1)}, f32[1536,512]{1,0:T(8,128)S(1)}, f32[1536,512]{1,0:T(8,128)S(1)}, f32[1,1536]{1,0:T(1,128)S(1)}) custom-call(s32[1,1536]{1,0:T(1,128)S(1)} %get-tuple-element.58.starts_ref, bf16[1536,2048]{1,0:T(8,128)(2,1)S(1)} %copy-done, f32[1536,768]{1,0:T(8,128)S(1)} %shard_map.57.refs_0_, ...), custom_call_target="tpu_custom_call" | custom-call | flops 805306368 | bytes 18874368 | tf_op jit(solution)/shard_map/pallas_call | solution.py:347
  47.8 2.0 %collective-permute-start.13 = (f32[1,1536]{1,0:T(1,128)S(1)}, f32[1,1536]{1,0:T(1,128)S(1)}, u32[]{:S(2)}, u32[]{:S(2)}) collective-permute-start(f32[1,1536]{1,0:T(1,128)S(1)} %get-tuple-element.62.sq0), channel_id=1, source_target_pairs={{0,1},{1,0},{2,3},{3,2},{4,5},{5,4},{6,7},{7,6},{8,9},{9,8},{10,11... | collective-permute-start | bytes 18440 | tf_op jit(solution)/shard_map/ppermute | solution.py:444
  49.8 3.6 %collective-permute-start.12 = (f32[1,1536]{1,0:T(1,128)S(1)}, f32[1,1536]{1,0:T(1,128)S(1)}, u32[]{:S(2)}, u32[]{:S(2)}) collective-permute-start(f32[1,1536]{1,0:T(1,128)S(1)} %get-tuple-element.62.sq0), channel_id=1, source_target_pairs={{0,2},{1,3},{2,0},{3,1},{4,6},{5,7},{6,4},{7,5},{8,10},{9,11},{10,... | collective-permute-start | bytes 18440 | tf_op jit(solution)/shard_map/ppermute | solution.py:444
  53.4 1.7 %collective-permute-done.12.sq2 = f32[1,1536]{1,0:T(1,128)S(1)} collective-permute-done((f32[1,1536]{1,0:T(1,128)S(1)}, f32[1,1536]{1,0:T(1,128)S(1)}, u32[]{:S(2)}, u32[]{:S(2)}) %collective-permute-start.12) | collective-permute-done | bytes 6176 | tf_op jit(solution)/shard_map/ppermute | solution.py:444
  55.0 3.2 %collective-permute-done.11.sq1 = f32[1,1536]{1,0:T(1,128)S(1)} collective-permute-done((f32[1,1536]{1,0:T(1,128)S(1)}, f32[1,1536]{1,0:T(1,128)S(1)}, u32[]{:S(2)}, u32[]{:S(2)}) %collective-permute-start.11) | collective-permute-done | bytes 6176 | tf_op jit(solution)/shard_map/ppermute | solution.py:444
  58.2 4.0 %shard_map.65 = bf16[1536,2048]{1,0:T(8,128)(2,1)} custom-call(f32[1,1536]{1,0:T(1,128)S(1)} %get-tuple-element.62.sq0, f32[1,1536]{1,0:T(1,128)S(1)} %collective-permute-done.11.sq1, f32[1,1536]{1,0:T(1,128)S(1)} %collective-permute-done.12.sq2, f32[1,1536]{1,0:T(1,128)S(1)} %collective-permute-done.13.sq3, f32[1,2048]{1,0:T(1,128)S(1)} %bitcast.1, ...), custom_call_target="tpu_custom_call" | custom-call | flops 6291456 | bytes 18874368 | tf_op jit(solution)/shard_map/pallas_call | solution.py:401
  (19 shorter events, 1.1 us)
Async XLA Ops:
  0.0 15.6 %copy-start = (bf16[1536,2048]{1,0:T(8,128)(2,1)S(1)}, bf16[1536,2048]{1,0:T(8,128)(2,1)}, u32[]{:S(2)}) copy-start(bf16[1536,2048]{1,0:T(8,128)(2,1)} %q_ref.4) | copy-start | bytes 18874372
  8.2 2.0 %collective-permute-start = (f32[1032,128]{1,0:T(8,128)S(1)}, f32[1032,128]{1,0:T(8,128)S(1)}, u32[]{:S(2)}, u32[]{:S(2)}) collective-permute-start(f32[1032,128]{1,0:T(8,128)S(1)} %get-tuple-element.37), channel_id=1, source_target_pairs={{0,4},{4,0},{8,12},{12,8},{16,20},{20,16},{24,28},{28,24},{32,36},... | collective-permute-start | bytes 1585160 | tf_op jit(solution)/shard_map/ppermute | solution.py:32
  10.3 10.0 %collective-permute-start.1 = (f32[264,128]{1,0:T(8,128)S(1)}, f32[264,128]{1,0:T(8,128)S(1)}, u32[]{:S(2)}, u32[]{:S(2)}) collective-permute-start(f32[264,128]{1,0:T(8,128)S(1)} %get-tuple-element.40), channel_id=1, source_target_pairs={{0,24},{4,28},{8,0},{12,4},{16,8},{20,12},{24,16},{28,20},{32,56},... | collective-permute-start | bytes 405512 | tf_op jit(solution)/shard_map/ppermute | solution.py:38
  13.4 9.5 %collective-permute-start.2 = (f32[264,128]{1,0:T(8,128)S(1)}, f32[264,128]{1,0:T(8,128)S(1)}, u32[]{:S(2)}, u32[]{:S(2)}) collective-permute-start(f32[264,128]{1,0:T(8,128)S(1)} %get-tuple-element.46), channel_id=1, source_target_pairs={{0,8},{4,12},{8,16},{12,20},{16,24},{20,28},{24,0},{28,4},{32,40},... | collective-permute-start | bytes 405512 | tf_op jit(solution)/shard_map/ppermute | solution.py:38
  13.4 9.5 %collective-permute-start.3 = (f32[264,128]{1,0:T(8,128)S(1)}, f32[264,128]{1,0:T(8,128)S(1)}, u32[]{:S(2)}, u32[]{:S(2)}) collective-permute-start(f32[264,128]{1,0:T(8,128)S(1)} %get-tuple-element.47), channel_id=1, source_target_pairs={{0,16},{4,20},{8,24},{12,28},{16,0},{20,4},{24,8},{28,12},{32,48},... | collective-permute-start | bytes 405512 | tf_op jit(solution)/shard_map/ppermute | solution.py:38
  23.0 7.9 %collective-permute-start.6 = (f32[256,128]{1,0:T(8,128)S(1)}, f32[256,128]{1,0:T(8,128)S(1)}, u32[]{:S(2)}, u32[]{:S(2)}) collective-permute-start(f32[256,128]{1,0:T(8,128)S(1)} %shard_map.58), channel_id=1, source_target_pairs={{0,32},{4,36},{8,40},{12,44},{16,48},{20,52},{24,56},{28,60},{32,0... | collective-permute-start | bytes 393224 | tf_op jit(solution)/shard_map/ppermute | solution.py:46
  24.5 7.1 %collective-permute-start.5 = (f32[256,128]{1,0:T(8,128)S(1)}, f32[256,128]{1,0:T(8,128)S(1)}, u32[]{:S(2)}, u32[]{:S(2)}) collective-permute-start(f32[256,128]{1,0:T(8,128)S(1)} %shard_map.58), channel_id=1, source_target_pairs={{0,64},{4,68},{8,72},{12,76},{16,80},{20,84},{24,88},{28,92},{32,9... | collective-permute-start | bytes 393224 | tf_op jit(solution)/shard_map/ppermute | solution.py:46
  27.3 6.2 %collective-permute-start.4 = (f32[256,128]{1,0:T(8,128)S(1)}, f32[256,128]{1,0:T(8,128)S(1)}, u32[]{:S(2)}, u32[]{:S(2)}) collective-permute-start(f32[256,128]{1,0:T(8,128)S(1)} %shard_map.58), channel_id=1, source_target_pairs={{0,96},{4,100},{8,104},{12,108},{16,112},{20,116},{24,120},{28,124... | collective-permute-start | bytes 393224 | tf_op jit(solution)/shard_map/ppermute | solution.py:46
  33.7 7.0 %collective-permute-start.9 = (f32[256,128]{1,0:T(8,128)S(1)}, f32[256,128]{1,0:T(8,128)S(1)}, u32[]{:S(2)}, u32[]{:S(2)}) collective-permute-start(f32[256,128]{1,0:T(8,128)S(1)} %get-tuple-element.54), channel_id=1, source_target_pairs={{0,24},{4,28},{8,0},{12,4},{16,8},{20,12},{24,16},{28,20},{32,56},... | collective-permute-start | bytes 393224 | tf_op jit(solution)/shard_map/ppermute | solution.py:38
  34.1 7.0 %collective-permute-start.7 = (f32[256,128]{1,0:T(8,128)S(1)}, f32[256,128]{1,0:T(8,128)S(1)}, u32[]{:S(2)}, u32[]{:S(2)}) collective-permute-start(f32[256,128]{1,0:T(8,128)S(1)} %get-tuple-element.52), channel_id=1, source_target_pairs={{0,8},{4,12},{8,16},{12,20},{16,24},{20,28},{24,0},{28,4},{32,40},... | collective-permute-start | bytes 393224 | tf_op jit(solution)/shard_map/ppermute | solution.py:38
  35.8 6.7 %collective-permute-start.8 = (f32[256,128]{1,0:T(8,128)S(1)}, f32[256,128]{1,0:T(8,128)S(1)}, u32[]{:S(2)}, u32[]{:S(2)}) collective-permute-start(f32[256,128]{1,0:T(8,128)S(1)} %get-tuple-element.53), channel_id=1, source_target_pairs={{0,16},{4,20},{8,24},{12,28},{16,0},{20,4},{24,8},{28,12},{32,48},... | collective-permute-start | bytes 393224 | tf_op jit(solution)/shard_map/ppermute | solution.py:38
  42.6 2.0 %collective-permute-start.10 = (f32[1024,128]{1,0:T(8,128)S(1)}, f32[1024,128]{1,0:T(8,128)S(1)}, u32[]{:S(2)}, u32[]{:S(2)}) collective-permute-start(f32[1024,128]{1,0:T(8,128)S(1)} %get-tuple-element.61), channel_id=1, source_target_pairs={{0,4},{4,0},{8,12},{12,8},{16,20},{20,16},{24,28},{28,24},{32,36},... | collective-permute-start | bytes 1572872 | tf_op jit(solution)/shard_map/ppermute | solution.py:32
  44.6 13.6 %copy-start.1 = (f32[2048]{0:T(1024)S(1)}, f32[2048]{0:T(1024)}, u32[]{:S(2)}) copy-start(f32[2048]{0:T(1024)} %param.9) | copy-start | bytes 24580
  47.8 5.6 %collective-permute-start.13 = (f32[1,1536]{1,0:T(1,128)S(1)}, f32[1,1536]{1,0:T(1,128)S(1)}, u32[]{:S(2)}, u32[]{:S(2)}) collective-permute-start(f32[1,1536]{1,0:T(1,128)S(1)} %get-tuple-element.62.sq0), channel_id=1, source_target_pairs={{0,1},{1,0},{2,3},{3,2},{4,5},{5,4},{6,7},{7,6},{8,9},{9,8},{10,11... | collective-permute-start | bytes 18440 | tf_op jit(solution)/shard_map/ppermute | solution.py:444
  49.8 5.3 %collective-permute-start.12 = (f32[1,1536]{1,0:T(1,128)S(1)}, f32[1,1536]{1,0:T(1,128)S(1)}, u32[]{:S(2)}, u32[]{:S(2)}) collective-permute-start(f32[1,1536]{1,0:T(1,128)S(1)} %get-tuple-element.62.sq0), channel_id=1, source_target_pairs={{0,2},{1,3},{2,0},{3,1},{4,6},{5,7},{6,4},{7,5},{8,10},{9,11},{10,... | collective-permute-start | bytes 18440 | tf_op jit(solution)/shard_map/ppermute | solution.py:444
  53.4 4.8 %collective-permute-start.11 = (f32[1,1536]{1,0:T(1,128)S(1)}, f32[1,1536]{1,0:T(1,128)S(1)}, u32[]{:S(2)}, u32[]{:S(2)}) collective-permute-start(f32[1,1536]{1,0:T(1,128)S(1)} %get-tuple-element.62.sq0), channel_id=1, source_target_pairs={{0,3},{1,2},{2,1},{3,0},{4,7},{5,6},{6,5},{7,4},{8,11},{9,10},{10,... | collective-permute-start | bytes 18440 | tf_op jit(solution)/shard_map/ppermute | solution.py:444

commit v3 on v2

--- a/solution.py
+++ b/solution.py
@@ -74,73 +74,103 @@
     return [pl.multiple_of(side * half, half) for side in (1 - core, core)]
 
 
-def state_kernel(starts_hbm, k_hbm, v_hbm, away, keep, k_ref, v_ref, starts, sems, starts_sem):
+def state_kernel(starts_hbm, k_hbm, v_hbm, away, k_ref, v_ref, starts, sems, starts_sem, *, rows):
     tokens, width = k_ref.shape
     half = width // 2
     core, _, _, seq = spot()
     base = seq * tokens
-    steps = tokens // GROUP
     starts_copy = pltpu.make_async_copy(starts_hbm, starts.at[0], starts_sem)
-
-    def copies(step):
-        rows = pl.ds(pl.multiple_of(step * GROUP, GROUP), GROUP)
-        return [
-            pltpu.make_async_copy(source.at[rows, :], ref.at[rows, :], sems.at[index, step])
-            for index, (source, ref) in enumerate(((k_hbm, k_ref), (v_hbm, v_ref)))
+    spans = [slice(start, start + rows) for start in range(0, tokens, rows)]
+    copies = [
+        [
+            pltpu.make_async_copy(
+                source.at[span, pl.ds(side, half)],
+                ref.at[span, index * half : (index + 1) * half],
+                sems.at[2 * number + index, step],
+            )
+            for number, (source, ref) in enumerate(((k_hbm, k_ref), (v_hbm, v_ref)))
         ]
-
+        for index, side in enumerate(halves(core, half))
+        for step, span in enumerate(spans)
+    ]
     starts_copy.start()
-    for step in range(steps):
-        for copy in copies(step):
+    for group in copies:
+        for copy in group:
             copy.start()
-    for out in (away, keep):
-        out[...] = jnp.zeros_like(out)
     row = lax.broadcasted_iota(jnp.int32, (8, DH), 0)
-    place = lax.broadcasted_iota(jnp.int32, (GROUP, 2 * DH), 0)
+    place = base + lax.broadcasted_iota(jnp.int32, (rows, 2 * DH), 0)
     starts_copy.wait()
     first = jnp.broadcast_to(starts[:, :1], (1, DH))
     last = jnp.broadcast_to(starts[:, tokens - 1 :], (1, DH))
-    for out in (away, keep):
-        out[half:, :] = jnp.where(row == 0, first, last).astype(F32)
-    last = jnp.broadcast_to(jnp.concatenate([last, last], axis=1), (GROUP, 2 * DH))
-
-    def body(step, _):
-        for copy in copies(step):
+    away[half:, :] = jnp.where(row == 0, first, last).astype(F32)
+    last = jnp.broadcast_to(starts[:, tokens - 1 :], (rows, 2 * DH))
+    for step, span in enumerate(spans):
+        for copy in copies[step]:
             copy.wait()
-        at = pl.multiple_of(step * GROUP, GROUP)
-        rows = pl.ds(at, GROUP)
-        kept = jnp.where(base + at + place >= last, 1.0, 0.0).astype(jnp.bfloat16)
-        for out, side in zip((away, keep), halves(core, half)):
-            for col in range(0, half, 2 * DH):
-                cols = pl.ds(side + col, 2 * DH)
-                both = lax.dot_general(
-                    k_ref[rows, cols] * kept, v_ref[rows, cols], (((0,), (0,)), ((), ())), preferred_element_type=F32
-                )
-                out[col : col + DH, :] += both[:DH, :DH]
-                out[col + DH : col + 2 * DH, :] += both[DH:, DH:]
-        return 0
-
-    lax.fori_loop(0, steps, body, 0)
+        kept = jnp.where(place + step * rows >= last, 1.0, 0.0).astype(jnp.bfloat16)
+        add_states(away, k_ref, v_ref, span, kept, 0, step == 0)
+    for group in copies[len(spans) :]:
+        for copy in group:
+            copy.wait()
+
+
+def add_states(out, k_ref, v_ref, span, kept, column, first):
+    for col in range(0, out.shape[0] - 8, 2 * DH):
+        cols = slice(column + col, column + col + 2 * DH)
+        both = lax.dot_general(
+            k_ref[span, cols] * kept, v_ref[span, cols], (((0,), (0,)), ((), ())), preferred_element_type=F32
+        )
+        for head in range(2):
+            lanes = slice(head * DH, (head + 1) * DH)
+            at = slice(col + head * DH, col + (head + 1) * DH)
+            if first:
+                out[at, :] = both[lanes, lanes]
+            else:
+                out[at, :] += both[lanes, lanes]
+
+
+def keep_kernel(starts, k_ref, v_ref, keep, *, rows):
+    tokens, width = k_ref.shape
+    half = width // 2
+    base = spot()[3] * tokens
+    row = lax.broadcasted_iota(jnp.int32, (8, DH), 0)
+    first = jnp.broadcast_to(starts[:, :1], (1, DH))
+    last = jnp.broadcast_to(starts[:, tokens - 1 :], (1, DH))
+    keep[half:, :] = jnp.where(row == 0, first, last).astype(F32)
+    place = base + lax.broadcasted_iota(jnp.int32, (rows, 2 * DH), 0)
+    last = jnp.broadcast_to(starts[:, tokens - 1 :], (rows, 2 * DH))
+    for start in range(0, tokens, rows):
+        kept = jnp.where(place + start >= last, 1.0, 0.0).astype(jnp.bfloat16)
+        add_states(keep, k_ref, v_ref, slice(start, start + rows), kept, half, start == 0)
 
 
 def own_states(starts, keys, values):
     tokens, width = keys.shape
-    state = pltpu.VMEM((width // 2 + 8, DH), F32)
+    rows = 6 * GROUP
     held = pltpu.VMEM((tokens, width), jnp.bfloat16)
     return pl.pallas_call(
-        state_kernel,
-        out_shape=[state, state, held, held, pltpu.VMEM((1, tokens), jnp.int32)],
+        functools.partial(state_kernel, rows=rows),
+        out_shape=[pltpu.VMEM((width // 2 + 8, DH), F32), held, held, pltpu.VMEM((1, tokens), jnp.int32)],
         in_specs=[ANY, ANY, ANY],
-        out_specs=[VMEM] * 5,
-        scratch_shapes=[
-            pltpu.SemaphoreType.DMA((2, tokens // GROUP)),
-            pltpu.SemaphoreType.DMA,
-        ],
+        out_specs=[VMEM] * 4,
+        scratch_shapes=[pltpu.SemaphoreType.DMA((4, tokens // rows)), pltpu.SemaphoreType.DMA],
         compiler_params=params(4),
         cost_estimate=pl.CostEstimate(
-            flops=2 * tokens * width * DH, bytes_accessed=4 * tokens * width, transcendentals=0
+            flops=tokens * width * DH, bytes_accessed=4 * tokens * width, transcendentals=0
         ),
     )(in_hbm(starts), in_hbm(keys), in_hbm(values))
+
+
+def kept_states(starts, keys, values):
+    tokens, width = keys.shape
+    return pl.pallas_call(
+        functools.partial(keep_kernel, rows=2 * GROUP),
+        out_shape=pltpu.VMEM((width // 2 + 8, DH), F32),
+        in_specs=[VMEM] * 3,
+        out_specs=VMEM,
+        compiler_params=params(4),
+        cost_estimate=pl.CostEstimate(flops=tokens * width * DH, bytes_accessed=2 * tokens * width, transcendentals=0),
+    )(starts, in_vmem(keys), in_vmem(values))
 
 
 def marks(ref):
@@ -248,10 +278,11 @@
     )(*args)
 
 
-def local_kernel(starts_ref, q_ref, k_ref, v_ref, out_ref, *, kept, column):
+def local_kernel(starts_ref, q_ref, k_ref, v_ref, out_ref, *, column):
     tokens, width = out_ref.shape
     core, _, _, seq = spot()
-    side = halves(core, q_ref.shape[1] // 2)[kept] + column
+    half = q_ref.shape[1] // 2
+    sides = halves(core, half)
     key_place = lax.broadcasted_iota(jnp.int32, (GROUP, GROUP), 1)
     query_place = lax.broadcasted_iota(jnp.int32, (GROUP, GROUP), 0)
     blocks = tokens // GROUP
@@ -268,8 +299,9 @@
         usable = jnp.where(begin < first, 1.0, 0.0).astype(jnp.bfloat16)
         go_on = jnp.where(last < first, 1.0, 0.0)
         for head in range(width // DH):
-            cols = pl.ds(side + head * DH, DH)
-            q, k, v = q_ref[rows, cols], k_ref[rows, cols], v_ref[rows, cols]
+            col = column + head * DH
+            q = q_ref[rows, pl.ds(sides[col // half] + col % half, DH)]
+            k, v = k_ref[rows, col : col + DH], v_ref[rows, col : col + DH]
             scores = lax.dot_general(q, k, (((1,), (1,)), ((), ())), preferred_element_type=F32)
             scores = jnp.where(valid, scores, 0.0).astype(jnp.bfloat16)
             if block < blocks - 1:
@@ -286,10 +318,10 @@
                 carries[head] = state if block == 0 else state + go_on * carries[head]
 
 
-def local_attention(starts, queries, keys, values, kept, column, wide):
+def local_attention(starts, queries, keys, values, column, wide):
     tokens = queries.shape[0]
     return pl.pallas_call(
-        functools.partial(local_kernel, kept=kept, column=column),
+        functools.partial(local_kernel, column=column),
         out_shape=pltpu.VMEM((tokens, wide), F32),
         in_specs=[VMEM] * 4,
         out_specs=VMEM,
@@ -300,150 +332,155 @@
     )(starts, in_vmem(queries), in_vmem(keys), in_vmem(values))
 
 
-def finish_kernel(starts_ref, q_ref, *refs, sizes, rows):
-    count = len(sizes)
-    locals_, (away, own) = refs[:count], refs[count : count + 2]
-    outs, squares, states = refs[count + 2 : 2 * count + 2], refs[2 * count + 2], refs[2 * count + 3]
-    tokens, width = q_ref.shape
-    half = width // 2
+def finish_kernel(starts_ref, q_ref, carry, *refs, places, kept, rows, count):
+    locals_ = refs[:count]
+    before = refs[count] if len(refs) == count + 4 else None
+    out, squares, states = refs[-3:]
+    tokens, half = out.shape
     core, _, _, seq = spot()
+    side = halves(core, half)[kept]
     opened = jnp.sum((starts_ref[...] < seq * tokens).astype(jnp.int32))
-    pairs = []
-    for index, size in enumerate(sizes):
-        for col in range(0, size, 2 * DH):
-            pairs.append((index, col))
     states[...] = jnp.zeros_like(states)
-    for pair in range(len(pairs)):
-        source = away if pair < len(pairs) // 2 else own
-        at = pair * 2 * DH % half
-        for side in range(2):
-            span = slice(side * DH, (side + 1) * DH)
-            states[pair, span, span] = source[at + side * DH : at + (side + 1) * DH, :].astype(jnp.bfloat16)
-    sides = halves(core, half)
+    for head in range(half // DH):
+        span = slice(head % 2 * DH, (head % 2 + 1) * DH)
+        states[head // 2, span, span] = carry[head * DH : (head + 1) * DH, :].astype(jnp.bfloat16)
 
     def step(index, _):
         start = pl.multiple_of(index * rows, rows)
         span = pl.ds(start, rows)
         usable = start + lax.broadcasted_iota(jnp.int32, (rows, 2 * DH), 0) < opened
         total = jnp.zeros((rows, DH), F32)
-        for pair, (part, col) in enumerate(pairs):
-            side = sides[pair // (len(pairs) // 2)]
-            q = q_ref[span, pl.ds(side + pair * 2 * DH % half, 2 * DH)]
-            inter = jnp.dot(q, states[pair], preferred_element_type=F32)
-            cols = slice(col, col + 2 * DH)
-            attn = locals_[part][span, cols] + jnp.where(usable, inter, 0.0)
-            outs[part][span, cols] = attn
-            total = total + attn[:, :DH] * attn[:, :DH] + attn[:, DH:] * attn[:, DH:]
-        squares[:, span] = jnp.sum(total.T, axis=0, keepdims=True)
+        for pair in range(half // (2 * DH)):
+            q = q_ref[span, pl.ds(side + pair * 2 * DH, 2 * DH)]
+            inter = jnp.where(usable, jnp.dot(q, states[pair], preferred_element_type=F32), 0.0)
+            for head in range(2):
+                part, col = places[2 * pair + head]
+                attn = locals_[part][span, col : col + DH] + inter[:, head * DH : (head + 1) * DH]
+                at = (2 * pair + head) * DH
+                out[span, at : at + DH] = attn
+                total = total + attn * attn
+        summed = jnp.sum(total.T, axis=0, keepdims=True)
+        squares[:, span] = summed if before is None else summed + before[:, span]
         return 0
 
     lax.fori_loop(0, tokens // rows, step, 0)
 
 
-def finish(starts, queries, locals_, away, own):
+def finish(starts, queries, carry, locals_, places, kept, before):
     tokens, width = queries.shape
-    sizes = [part.shape[1] for part in locals_]
-    count = len(sizes)
-    *outs, squares = pl.pallas_call(
-        functools.partial(finish_kernel, sizes=sizes, rows=2 * GROUP),
-        out_shape=[pltpu.VMEM((tokens, size), F32) for size in sizes] + [jax.ShapeDtypeStruct((1, tokens), F32)],
-        in_specs=[VMEM] * (count + 4),
-        out_specs=[VMEM] * (count + 1),
-        scratch_shapes=[pltpu.VMEM((width // (2 * DH), 2 * DH, 2 * DH), jnp.bfloat16)],
+    half = width // 2
+    extra = [] if before is None else [before]
+    return pl.pallas_call(
+        functools.partial(finish_kernel, places=places, kept=kept, rows=tokens, count=len(locals_)),
+        out_shape=[pltpu.VMEM((tokens, half), F32), pltpu.VMEM((1, tokens), F32)],
+        in_specs=[VMEM] * (3 + len(locals_) + len(extra)),
+        out_specs=[VMEM] * 2,
+        scratch_shapes=[pltpu.VMEM((half // (2 * DH), 2 * DH, 2 * DH), jnp.bfloat16)],
         compiler_params=params(8),
         cost_estimate=pl.CostEstimate(
-            flops=2 * tokens * width * DH, bytes_accessed=tokens * width * 6, transcendentals=0
+            flops=tokens * width * DH, bytes_accessed=tokens * width * 3, transcendentals=0
         ),
-    )(starts, in_vmem(queries), *[in_vmem(part) for part in locals_], away, own)
-    return outs, squares
-
-
-def norm_kernel(sq0, sq1, sq2, sq3, gain_ref, *refs, sizes, rows):
-    count = len(sizes)
-    ins = refs[:count]
-    out, buffer, sems = refs[count:]
+    )(starts, in_vmem(queries), carry, *[in_vmem(part) for part in locals_], *extra)
+
+
+def norm_kernel(sq0, sq1, sq2, sq3, gain_ref, away, keep, out, buffer, gains, factors, sems, *, rows):
     tokens, width = out.shape
     half = width // 2
-    core = spot()[0]
-    sides = halves(core, half)
-    places = []
-    for index, size in enumerate(sizes):
-        for col in range(0, size, DH):
-            places.append((index, col))
-
-    def copy(index):
+    sides = halves(spot()[0], half)
+
+    def copies(index):
         at = pl.ds(pl.multiple_of(index * rows, rows), rows)
-        return pltpu.make_async_copy(buffer.at[at, :], out.at[at, :], sems.at[index])
+        return [
+            pltpu.make_async_copy(
+                buffer.at[at, number * half : (number + 1) * half], out.at[at, pl.ds(side, half)], sems.at[number, index]
+            )
+            for number, side in enumerate(sides)
+        ]
+
+    for number, side in enumerate(sides):
+        gains[:, number * half : (number + 1) * half] = gain_ref[:, pl.ds(side, half)]
+
+    total = (sq0[...] + sq1[...]) + (sq2[...] + sq3[...])
+    factors[...] = jnp.broadcast_to(lax.rsqrt(total / (HEADS * DH) + EPS), (DH, tokens)).T
 
     def step(index, _):
         span = pl.ds(pl.multiple_of(index * rows, rows), rows)
-        total = (sq0[:, span] + sq1[:, span]) + (sq2[:, span] + sq3[:, span])
-        factor = jnp.broadcast_to(lax.rsqrt(total / (HEADS * DH) + EPS), (DH, rows)).T
-        for number, (index_in, col) in enumerate(places):
-            side = sides[number // (len(places) // 2)]
-            cols = pl.ds(side + number * DH % half, DH)
-            value = ins[index_in][span, col : col + DH] * factor * gain_ref[:, cols]
-            buffer[span, cols] = value.astype(jnp.bfloat16)
-        copy(index).start()
+        factor = factors[span, :]
+        for number, (ref, copy) in enumerate(zip((away, keep), copies(index))):
+            for col in range(0, half, DH):
+                cols = slice(number * half + col, number * half + col + DH)
+                value = ref[span, col : col + DH] * factor * gains[:, cols]
+                buffer[span, cols] = value.astype(jnp.bfloat16)
+            copy.start()
         return 0
 
     steps = tokens // rows
     lax.fori_loop(0, steps, step, 0)
     for index in range(steps):
-        copy(index).wait()
-
-
-def normalise(squares, gain, parts):
-    tokens = parts[0].shape[0]
-    sizes = [part.shape[1] for part in parts]
-    width = sum(sizes)
-    rows = 2 * DH
-    return pl.pallas_call(
-        functools.partial(norm_kernel, sizes=sizes, rows=rows),
+        for copy in copies(index):
+            copy.wait()
+
+
+def normalise(squares, gain, away, keep):
+    tokens, half = away.shape
+    width = 2 * half
+    rows = DH
+    return pl.pallas_call(
+        functools.partial(norm_kernel, rows=rows),
         out_shape=jax.ShapeDtypeStruct((tokens, width), jnp.bfloat16),
-        in_specs=[VMEM] * (len(sizes) + 5),
+        in_specs=[VMEM] * 7,
         out_specs=ANY,
         scratch_shapes=[
             pltpu.VMEM((tokens, width), jnp.bfloat16),
-            pltpu.SemaphoreType.DMA((tokens // rows,)),
+            pltpu.VMEM((1, width), F32),
+            pltpu.VMEM((tokens, DH), F32),
+            pltpu.SemaphoreType.DMA((2, tokens // rows)),
         ],
         compiler_params=params(8),
         cost_estimate=pl.CostEstimate(flops=2 * tokens * width, bytes_accessed=6 * tokens * width, transcendentals=0),
-    )(*squares, gain, *[in_vmem(part) for part in parts])
+    )(*squares, gain, in_vmem(away), in_vmem(keep))
 
 
 def on_device(queries, keys, values, doc_start, norm_gain):
     tokens, width = queries.shape
     half = width // 2
-
-    away, keep, keys, values, starts = own_states(doc_start, keys, values)
+    heads = width // DH
+
+    away, keys, values, starts = own_states(doc_start, keys, values)
     recv = swap_cores(away)
+    keep = kept_states(starts, keys, values)
     queries = after(queries, away)
     part = half // SEQ_Y
 
-    def local(kept, column, wide, gate):
-        return local_attention(after(starts, gate), queries, keys, values, kept, column, wide)
+    shares = [3 * heads // 8, 5 * heads // 16, 5 * heads // 16]
+    places_ = [(part, col * DH) for part, share in enumerate(shares) for col in range(share)]
+
+    def local(number, gate):
+        column = sum(shares[:number]) * DH
+        return local_attention(after(starts, gate), queries, keys, values, column, shares[number] * DH)
 
     mine = small(cores_kernel, tokens, (keep, recv), [part + 8] * SEQ_Y)
     rows = [mine[0]] + [turn_row(mine[d], d) for d in (1, 2, 3)]
-    first = local(0, 0, 3 * half // 4, mine[0])
+    first = local(0, mine[0])
     rows[3], first = lax.optimization_barrier((rows[3], first))
     (whole,) = small(row_kernel, tokens, rows, [part])
     ups = [swap_rows(whole, d) for d in (3, 2, 1)]
-    third = local(1, 0, half // 2, whole)
-    ups[2], third = lax.optimization_barrier((ups[2], third))
+    second = local(1, whole)
+    ups[2], second = lax.optimization_barrier((ups[2], second))
     carries = small(carry_kernel, tokens, (*rows, *ups), [part] * SEQ_Y)
     got = [carries[0]] + [turn_row(carries[d], d) for d in (1, 2, 3)]
-    fourth = local(1, half // 2, half // 2, carries[0])
-    got[3], fourth = lax.optimization_barrier((got[3], fourth))
+    third = local(2, carries[0])
+    got[3], third = lax.optimization_barrier((got[3], third))
     own, send = small(spread_kernel, tokens, (*got, keep, recv), [part * SEQ_Y] * 2)
     other = swap_cores(send)
-    second = local(0, 3 * half // 4, half // 4, own)
-    parts, squares = finish(starts, queries, [first, second, third, fourth], other, own)
+    locals_ = [first, second, third]
+    kept_attn, kept_squares = finish(starts, queries, own, locals_, places_[heads // 2 :], 1, None)
+    other, kept_squares = lax.optimization_barrier((other, kept_squares))
+    away_attn, squares = finish(starts, queries, other, locals_, places_[: heads // 2], 0, kept_squares)
     sums = [squares] + [
         lax.ppermute(squares, "head", [(z, z ^ d) for z in range(4)]) for d in (3, 2, 1)
     ]
-    return normalise(sums, norm_gain.reshape(1, width), parts)
+    return normalise(sums, norm_gain.reshape(1, width), away_attn, kept_attn)
 
 
 def solution(mesh):

time: 62.5 us -> 56.9 us (0.910)
  waiting for transfers between devices: 13.7 us -> 9.92 us
  Pallas kernels: 28.6 us -> 25.2 us
  starting transfers between devices: 19.8 us -> 21.4 us
    pallas_call x7 -> x8, Pallas kernels: 28 us -> 24.6 us  [the longest x3 12.1 us: local_attention(): pl.pallas_call(functools.partial(local_kernel, column=column), out_shape=...]
    ppermute x6, waiting for transfers between devices: 4.45 us -> 1.17 us  [turn_row(): lax.ppermute(value, 'seq', [(device_of(x, y, c), device_of(x, (y + steps)...]
    ppermute x6, starting transfers between devices: 9.23 us -> 10.9 us  [turn_row(): lax.ppermute(value, 'seq', [(device_of(x, y, c), device_of(x, (y + steps)...]
    ppermute x2, waiting for transfers between devices: 1.91 us -> 0.83 us  [swap_cores(): lax.ppermute(value, 'seq', [(device_of(x, y, c), device_of(x, y, 1 - c))...]
  transfers between devices with their start and end apart: 14 -> 14, of which waited for: 8 -> 9; matrix products, arithmetic and copies ran while one was open for 0% -> 0% of each run, Pallas kernels for 20% -> 26%
where the time goes in v3:
time: 56.9 us; the launch traced here: 56.8 us
  Pallas kernels  25.2 us (44%)
  starting transfers between devices  21.4 us (38%)
  waiting for transfers between devices  9.92 us (17%)
    pallas_call x3, Pallas kernels, local_attention(): pl.pallas_call(functools.partial(local_kernel, column=column), out_shape=...  12.1 us
    ppermute x6, starting transfers between devices, turn_row(): lax.ppermute(value, 'seq', [(device_of(x, y, c), device_of(x, (y + steps)...  10.9 us
    ppermute x3, starting transfers between devices, on_device(): lax.ppermute(squares, 'head', [(z, z ^ d) for z in range(4)])  5.58 us
    pallas_call x1, Pallas kernels, own_states(): pl.pallas_call(functools.partial(state_kernel, rows=rows), out_shape=[plt...  4.85 us
    ppermute x3, waiting for transfers between devices, on_device(): lax.ppermute(squares, 'head', [(z, z ^ d) for z in range(4)])  4.84 us
    ppermute x3, starting transfers between devices, swap_rows(): lax.ppermute(value, 'seq', [(device_of(x, y, c), device_of(x ^ steps, y,...  4.78 us
    pallas_call x1, Pallas kernels, normalise(): pl.pallas_call(functools.partial(norm_kernel, rows=rows), out_shape=jax.S...  3.2 us
    ppermute x3, waiting for transfers between devices, swap_rows(): lax.ppermute(value, 'seq', [(device_of(x, y, c), device_of(x ^ steps, y,...  3.08 us
  transfers between devices with their start and end apart: 14, of which 9 were waited for; matrix products, arithmetic and copies ran while one was open for 0% of the time, Pallas kernels for 26%

profile of v3, /device:TPU:0, one launch (start us, length us, event | category | flops | bytes accessed | tf_op | source)
XLA Modules:
  0.0 56.8 jit_solution(15728463025102944765)
XLA Ops:
  0.0 4.8 %shard_map.55 = (f32[1032,128]{1,0:T(8,128)S(1)}, bf16[1536,2048]{1,0:T(8,128)(2,1)S(1)}, bf16[1536,2048]{1,0:T(8,128)(2,1)S(1)}, s32[1,1536]{1,0:T(1,128)S(1)}) custom-call(s32[1536]{0:T(1024)} %starts_hbm.1, bf16[1536,2048]{1,0:T(8,128)(2,1)} %k_hbm.1, bf16[1536,2048]{1,0:T(8,128)(2,1)} %v_hbm.1), custom_call_target="tpu_custom_call" | custom-call | flops 402653184 | bytes 12582912 | tf_op jit(solution)/shard_map/pallas_call | solution.py:151
  5.0 1.4 %shard_map.56.keep = f32[1032,128]{1,0:T(8,128)S(1)} custom-call(s32[1,1536]{1,0:T(1,128)S(1)} %get-tuple-element.52.starts.starts_ref, bf16[1536,2048]{1,0:T(8,128)(2,1)S(1)} %get-tuple-element.38.k_ref, bf16[1536,2048]{1,0:T(8,128)(2,1)S(1)} %get-tuple-element.39.v_ref), custom_call_target="tpu_custom_call" | custom-call | flops 402653184 | bytes 6291456 | tf_op jit(solution)/shard_map/pallas_call | solution.py:166
  6.9 1.7 %collective-permute-start.1 = (f32[264,128]{1,0:T(8,128)S(1)}, f32[264,128]{1,0:T(8,128)S(1)}, u32[]{:S(2)}, u32[]{:S(2)}) collective-permute-start(f32[264,128]{1,0:T(8,128)S(1)} %get-tuple-element.41), channel_id=1, source_target_pairs={{0,8},{4,12},{8,16},{12,20},{16,24},{20,28},{24,0},{28,4},{32,40},... | collective-permute-start | bytes 405512 | tf_op jit(solution)/shard_map/ppermute | solution.py:38
  8.7 2.9 %collective-permute-start.2 = (f32[264,128]{1,0:T(8,128)S(1)}, f32[264,128]{1,0:T(8,128)S(1)}, u32[]{:S(2)}, u32[]{:S(2)}) collective-permute-start(f32[264,128]{1,0:T(8,128)S(1)} %get-tuple-element.42), channel_id=1, source_target_pairs={{0,16},{4,20},{8,24},{12,28},{16,0},{20,4},{24,8},{28,12},{32,48},... | collective-permute-start | bytes 405512 | tf_op jit(solution)/shard_map/ppermute | solution.py:38
  11.6 1.3 %collective-permute-start.3 = (f32[264,128]{1,0:T(8,128)S(1)}, f32[264,128]{1,0:T(8,128)S(1)}, u32[]{:S(2)}, u32[]{:S(2)}) collective-permute-start(f32[264,128]{1,0:T(8,128)S(1)} %get-tuple-element.43), channel_id=1, source_target_pairs={{0,24},{4,28},{8,0},{12,4},{16,8},{20,12},{24,16},{28,20},{32,56},... | collective-permute-start | bytes 405512 | tf_op jit(solution)/shard_map/ppermute | solution.py:38
  12.9 4.5 %shard_map.58.refs_0_ = f32[1536,768]{1,0:T(8,128)S(1)} custom-call(s32[1,1536]{1,0:T(1,128)S(1)} %get-tuple-element.52.starts.starts_ref, bf16[1536,2048]{1,0:T(8,128)(2,1)S(1)} %bitcast.2, bf16[1536,2048]{1,0:T(8,128)(2,1)S(1)} %get-tuple-element.38.k_ref, bf16[1536,2048]{1,0:T(8,128)(2,1)S(1)} %get-tuple-element.39.v_ref), custom_call_target="tpu_custom_call" | custom-call | flops 1811939328 | bytes 11796480 | tf_op jit(solution)/shard_map/pallas_call | solution.py:323
  17.6 0.5 collective-permute-done.2.from2
  18.1 1.6 %collective-permute-start.6 = (f32[256,128]{1,0:T(8,128)S(1)}, f32[256,128]{1,0:T(8,128)S(1)}, u32[]{:S(2)}, u32[]{:S(2)}) collective-permute-start(f32[256,128]{1,0:T(8,128)S(1)} %shard_map.59), channel_id=1, source_target_pairs={{0,32},{4,36},{8,40},{12,44},{16,48},{20,52},{24,56},{28,60},{32,0... | collective-permute-start | bytes 393224 | tf_op jit(solution)/shard_map/ppermute | solution.py:46
  19.7 2.7 %collective-permute-start.5 = (f32[256,128]{1,0:T(8,128)S(1)}, f32[256,128]{1,0:T(8,128)S(1)}, u32[]{:S(2)}, u32[]{:S(2)}) collective-permute-start(f32[256,128]{1,0:T(8,128)S(1)} %shard_map.59), channel_id=1, source_target_pairs={{0,64},{4,68},{8,72},{12,76},{16,80},{20,84},{24,88},{28,92},{32,9... | collective-permute-start | bytes 393224 | tf_op jit(solution)/shard_map/ppermute | solution.py:46
  22.9 3.8 %shard_map.60.refs_1_ = f32[1536,640]{1,0:T(8,128)S(1)} custom-call(s32[1,1536]{1,0:T(1,128)S(1)} %get-tuple-element.52.starts.starts_ref, bf16[1536,2048]{1,0:T(8,128)(2,1)S(1)} %bitcast.2, bf16[1536,2048]{1,0:T(8,128)(2,1)S(1)} %get-tuple-element.38.k_ref, bf16[1536,2048]{1,0:T(8,128)(2,1)S(1)} %get-tuple-element.39.v_ref), custom_call_target="tpu_custom_call" | custom-call | flops 1509949440 | bytes 9830400 | tf_op jit(solution)/shard_map/pallas_call | solution.py:323
  26.7 1.3 %collective-permute-done.5.up2 = f32[256,128]{1,0:T(8,128)S(1)} collective-permute-done((f32[256,128]{1,0:T(8,128)S(1)}, f32[256,128]{1,0:T(8,128)S(1)}, u32[]{:S(2)}, u32[]{:S(2)}) %collective-permute-start.5) | collective-permute-done | bytes 131104 | tf_op jit(solution)/shard_map/ppermute | solution.py:46
  28.0 1.8 %collective-permute-done.4.up3 = f32[256,128]{1,0:T(8,128)S(1)} collective-permute-done((f32[256,128]{1,0:T(8,128)S(1)}, f32[256,128]{1,0:T(8,128)S(1)}, u32[]{:S(2)}, u32[]{:S(2)}) %collective-permute-start.4) | collective-permute-done | bytes 131104 | tf_op jit(solution)/shard_map/ppermute | solution.py:46
  30.1 1.3 %collective-permute-start.7 = (f32[256,128]{1,0:T(8,128)S(1)}, f32[256,128]{1,0:T(8,128)S(1)}, u32[]{:S(2)}, u32[]{:S(2)}) collective-permute-start(f32[256,128]{1,0:T(8,128)S(1)} %get-tuple-element.49), channel_id=1, source_target_pairs={{0,8},{4,12},{8,16},{12,20},{16,24},{20,28},{24,0},{28,4},{32,40},... | collective-permute-start | bytes 393224 | tf_op jit(solution)/shard_map/ppermute | solution.py:38
  31.4 2.6 %collective-permute-start.8 = (f32[256,128]{1,0:T(8,128)S(1)}, f32[256,128]{1,0:T(8,128)S(1)}, u32[]{:S(2)}, u32[]{:S(2)}) collective-permute-start(f32[256,128]{1,0:T(8,128)S(1)} %get-tuple-element.50), channel_id=1, source_target_pairs={{0,16},{4,20},{8,24},{12,28},{16,0},{20,4},{24,8},{28,12},{32,48},... | collective-permute-start | bytes 393224 | tf_op jit(solution)/shard_map/ppermute | solution.py:38
  33.9 1.0 %collective-permute-start.9 = (f32[256,128]{1,0:T(8,128)S(1)}, f32[256,128]{1,0:T(8,128)S(1)}, u32[]{:S(2)}, u32[]{:S(2)}) collective-permute-start(f32[256,128]{1,0:T(8,128)S(1)} %get-tuple-element.51), channel_id=1, source_target_pairs={{0,24},{4,28},{8,0},{12,4},{16,8},{20,12},{24,16},{28,20},{32,56},... | collective-permute-start | bytes 393224 | tf_op jit(solution)/shard_map/ppermute | solution.py:38
  35.0 3.8 %shard_map.62.refs_2_ = f32[1536,640]{1,0:T(8,128)S(1)} custom-call(s32[1,1536]{1,0:T(1,128)S(1)} %get-tuple-element.52.starts.starts_ref, bf16[1536,2048]{1,0:T(8,128)(2,1)S(1)} %bitcast.2, bf16[1536,2048]{1,0:T(8,128)(2,1)S(1)} %get-tuple-element.38.k_ref, bf16[1536,2048]{1,0:T(8,128)(2,1)S(1)} %get-tuple-element.39.v_ref), custom_call_target="tpu_custom_call" | custom-call | flops 1509949440 | bytes 9830400 | tf_op jit(solution)/shard_map/pallas_call | solution.py:323
  38.7 0.5 collective-permute-done.9.got3
  39.6 1.5 %shard_map.64 = (f32[1536,1024]{1,0:T(8,128)S(1)}, f32[1,1536]{1,0:T(1,128)S(1)}) custom-call(s32[1,1536]{1,0:T(1,128)S(1)} %get-tuple-element.52.starts.starts_ref, bf16[1536,2048]{1,0:T(8,128)(2,1)S(1)} %bitcast.2, f32[1024,128]{1,0:T(8,128)S(1)} %get-tuple-element.55.carry, f32[1536,768]{1,0:T(8,128)S(1)} %shard_map.58.refs_0_, ...), custom_call_target="tpu_custom_call" | custom-call | flops 402653184 | bytes 9437184 | tf_op jit(solution)/shard_map/pallas_call | solution.py:373
  41.5 1.5 %shard_map.65 = (f32[1536,1024]{1,0:T(8,128)S(1)}, f32[1,1536]{1,0:T(1,128)S(1)}) custom-call(s32[1,1536]{1,0:T(1,128)S(1)} %get-tuple-element.52.starts.starts_ref, bf16[1536,2048]{1,0:T(8,128)(2,1)S(1)} %bitcast.2, f32[1024,128]{1,0:T(8,128)S(1)} %collective-permute-done.10.carry, f32[1536,768]{1,0:T(8,128)S(1)} %shard_map.58.refs_0_, ...), custom_call_target="tpu_custom_call" | custom-call | flops 402653184 | bytes 9437184 | tf_op jit(solution)/shard_map/pallas_call | solution.py:373
  43.0 2.0 %collective-permute-start.13 = (f32[1,1536]{1,0:T(1,128)S(1)}, f32[1,1536]{1,0:T(1,128)S(1)}, u32[]{:S(2)}, u32[]{:S(2)}) collective-permute-start(f32[1,1536]{1,0:T(1,128)S(1)} %get-tuple-element.62.sq0), channel_id=1, source_target_pairs={{0,1},{1,0},{2,3},{3,2},{4,5},{5,4},{6,7},{7,6},{8,9},{9,8},{10,11... | collective-permute-start | bytes 18440 | tf_op jit(solution)/shard_map/ppermute | solution.py:481
  45.0 3.6 %collective-permute-start.12 = (f32[1,1536]{1,0:T(1,128)S(1)}, f32[1,1536]{1,0:T(1,128)S(1)}, u32[]{:S(2)}, u32[]{:S(2)}) collective-permute-start(f32[1,1536]{1,0:T(1,128)S(1)} %get-tuple-element.62.sq0), channel_id=1, source_target_pairs={{0,2},{1,3},{2,0},{3,1},{4,6},{5,7},{6,4},{7,5},{8,10},{9,11},{10,... | collective-permute-start | bytes 18440 | tf_op jit(solution)/shard_map/ppermute | solution.py:481
  48.6 1.7 %collective-permute-done.12.sq2 = f32[1,1536]{1,0:T(1,128)S(1)} collective-permute-done((f32[1,1536]{1,0:T(1,128)S(1)}, f32[1,1536]{1,0:T(1,128)S(1)}, u32[]{:S(2)}, u32[]{:S(2)}) %collective-permute-start.12) | collective-permute-done | bytes 6176 | tf_op jit(solution)/shard_map/ppermute | solution.py:481
  50.2 3.2 %collective-permute-done.11.sq1 = f32[1,1536]{1,0:T(1,128)S(1)} collective-permute-done((f32[1,1536]{1,0:T(1,128)S(1)}, f32[1,1536]{1,0:T(1,128)S(1)}, u32[]{:S(2)}, u32[]{:S(2)}) %collective-permute-start.11) | collective-permute-done | bytes 6176 | tf_op jit(solution)/shard_map/ppermute | solution.py:481
  53.4 3.2 %shard_map.66 = bf16[1536,2048]{1,0:T(8,128)(2,1)} custom-call(f32[1,1536]{1,0:T(1,128)S(1)} %get-tuple-element.62.sq0, f32[1,1536]{1,0:T(1,128)S(1)} %collective-permute-done.11.sq1, f32[1,1536]{1,0:T(1,128)S(1)} %collective-permute-done.12.sq2, f32[1,1536]{1,0:T(1,128)S(1)} %collective-permute-done.13.sq3, f32[1,2048]{1,0:T(1,128)S(1)} %bitcast.3, ...), custom_call_target="tpu_custom_call" | custom-call | flops 6291456 | bytes 18874368 | tf_op jit(solution)/shard_map/pallas_call | solution.py:428
  (23 shorter events, 2.2 us)
Async XLA Ops:
  0.0 12.9 %slice-start = ((s8[6291456]{0:T(1024)(128)(4,1)}), s8[4194304]{0:T(1024)(128)(4,1)S(1)}, s32[]{:S(2)}) async-start(s8[6291456]{0:T(1024)(128)(4,1)} %bitcast.1), calls=%async_computation | async-start | bytes 8388608
  4.9 2.0 %collective-permute-start = (f32[1032,128]{1,0:T(8,128)S(1)}, f32[1032,128]{1,0:T(8,128)S(1)}, u32[]{:S(2)}, u32[]{:S(2)}) collective-permute-start(f32[1032,128]{1,0:T(8,128)S(1)} %get-tuple-element.36), channel_id=1, source_target_pairs={{0,4},{4,0},{8,12},{12,8},{16,20},{20,16},{24,28},{28,24},{32,36},... | collective-permute-start | bytes 1585160 | tf_op jit(solution)/shard_map/ppermute | solution.py:32
  5.0 8.0 %slice-start.1 = ((s8[6291456]{0:T(1024)(128)(4,1)}), s8[2097152]{0:T(1024)(128)(4,1)S(1)}, s32[]{:S(2)}) async-start(s8[6291456]{0:T(1024)(128)(4,1)} %bitcast.1), calls=%async_computation.1 | async-start | bytes 4194304
  6.9 10.6 %collective-permute-start.1 = (f32[264,128]{1,0:T(8,128)S(1)}, f32[264,128]{1,0:T(8,128)S(1)}, u32[]{:S(2)}, u32[]{:S(2)}) collective-permute-start(f32[264,128]{1,0:T(8,128)S(1)} %get-tuple-element.41), channel_id=1, source_target_pairs={{0,8},{4,12},{8,16},{12,20},{16,24},{20,28},{24,0},{28,4},{32,40},... | collective-permute-start | bytes 405512 | tf_op jit(solution)/shard_map/ppermute | solution.py:38
  8.7 9.4 %collective-permute-start.2 = (f32[264,128]{1,0:T(8,128)S(1)}, f32[264,128]{1,0:T(8,128)S(1)}, u32[]{:S(2)}, u32[]{:S(2)}) collective-permute-start(f32[264,128]{1,0:T(8,128)S(1)} %get-tuple-element.42), channel_id=1, source_target_pairs={{0,16},{4,20},{8,24},{12,28},{16,0},{20,4},{24,8},{28,12},{32,48},... | collective-permute-start | bytes 405512 | tf_op jit(solution)/shard_map/ppermute | solution.py:38
  11.6 6.0 %collective-permute-start.3 = (f32[264,128]{1,0:T(8,128)S(1)}, f32[264,128]{1,0:T(8,128)S(1)}, u32[]{:S(2)}, u32[]{:S(2)}) collective-permute-start(f32[264,128]{1,0:T(8,128)S(1)} %get-tuple-element.43), channel_id=1, source_target_pairs={{0,24},{4,28},{8,0},{12,4},{16,8},{20,12},{24,16},{28,20},{32,56},... | collective-permute-start | bytes 405512 | tf_op jit(solution)/shard_map/ppermute | solution.py:38
  18.1 8.6 %collective-permute-start.6 = (f32[256,128]{1,0:T(8,128)S(1)}, f32[256,128]{1,0:T(8,128)S(1)}, u32[]{:S(2)}, u32[]{:S(2)}) collective-permute-start(f32[256,128]{1,0:T(8,128)S(1)} %shard_map.59), channel_id=1, source_target_pairs={{0,32},{4,36},{8,40},{12,44},{16,48},{20,52},{24,56},{28,60},{32,0... | collective-permute-start | bytes 393224 | tf_op jit(solution)/shard_map/ppermute | solution.py:46
  19.7 8.3 %collective-permute-start.5 = (f32[256,128]{1,0:T(8,128)S(1)}, f32[256,128]{1,0:T(8,128)S(1)}, u32[]{:S(2)}, u32[]{:S(2)}) collective-permute-start(f32[256,128]{1,0:T(8,128)S(1)} %shard_map.59), channel_id=1, source_target_pairs={{0,64},{4,68},{8,72},{12,76},{16,80},{20,84},{24,88},{28,92},{32,9... | collective-permute-start | bytes 393224 | tf_op jit(solution)/shard_map/ppermute | solution.py:46
  22.4 7.4 %collective-permute-start.4 = (f32[256,128]{1,0:T(8,128)S(1)}, f32[256,128]{1,0:T(8,128)S(1)}, u32[]{:S(2)}, u32[]{:S(2)}) collective-permute-start(f32[256,128]{1,0:T(8,128)S(1)} %shard_map.59), channel_id=1, source_target_pairs={{0,96},{4,100},{8,104},{12,108},{16,112},{20,116},{24,120},{28,124... | collective-permute-start | bytes 393224 | tf_op jit(solution)/shard_map/ppermute | solution.py:46
  30.1 9.2 %collective-permute-start.7 = (f32[256,128]{1,0:T(8,128)S(1)}, f32[256,128]{1,0:T(8,128)S(1)}, u32[]{:S(2)}, u32[]{:S(2)}) collective-permute-start(f32[256,128]{1,0:T(8,128)S(1)} %get-tuple-element.49), channel_id=1, source_target_pairs={{0,8},{4,12},{8,16},{12,20},{16,24},{20,28},{24,0},{28,4},{32,40},... | collective-permute-start | bytes 393224 | tf_op jit(solution)/shard_map/ppermute | solution.py:38
  31.4 7.9 %collective-permute-start.8 = (f32[256,128]{1,0:T(8,128)S(1)}, f32[256,128]{1,0:T(8,128)S(1)}, u32[]{:S(2)}, u32[]{:S(2)}) collective-permute-start(f32[256,128]{1,0:T(8,128)S(1)} %get-tuple-element.50), channel_id=1, source_target_pairs={{0,16},{4,20},{8,24},{12,28},{16,0},{20,4},{24,8},{28,12},{32,48},... | collective-permute-start | bytes 393224 | tf_op jit(solution)/shard_map/ppermute | solution.py:38
  33.9 5.3 %collective-permute-start.9 = (f32[256,128]{1,0:T(8,128)S(1)}, f32[256,128]{1,0:T(8,128)S(1)}, u32[]{:S(2)}, u32[]{:S(2)}) collective-permute-start(f32[256,128]{1,0:T(8,128)S(1)} %get-tuple-element.51), channel_id=1, source_target_pairs={{0,24},{4,28},{8,0},{12,4},{16,8},{20,12},{24,16},{28,20},{32,56},... | collective-permute-start | bytes 393224 | tf_op jit(solution)/shard_map/ppermute | solution.py:38
  39.5 2.0 %collective-permute-start.10 = (f32[1024,128]{1,0:T(8,128)S(1)}, f32[1024,128]{1,0:T(8,128)S(1)}, u32[]{:S(2)}, u32[]{:S(2)}) collective-permute-start(f32[1024,128]{1,0:T(8,128)S(1)} %get-tuple-element.54), channel_id=1, source_target_pairs={{0,4},{4,0},{8,12},{12,8},{16,20},{20,16},{24,28},{28,24},{32,36},... | collective-permute-start | bytes 1572872 | tf_op jit(solution)/shard_map/ppermute | solution.py:32
  41.5 11.9 %copy-start = (f32[2048]{0:T(1024)S(1)}, f32[2048]{0:T(1024)}, u32[]{:S(2)}) copy-start(f32[2048]{0:T(1024)} %param.9) | copy-start | bytes 24580
  43.0 5.6 %collective-permute-start.13 = (f32[1,1536]{1,0:T(1,128)S(1)}, f32[1,1536]{1,0:T(1,128)S(1)}, u32[]{:S(2)}, u32[]{:S(2)}) collective-permute-start(f32[1,1536]{1,0:T(1,128)S(1)} %get-tuple-element.62.sq0), channel_id=1, source_target_pairs={{0,1},{1,0},{2,3},{3,2},{4,5},{5,4},{6,7},{7,6},{8,9},{9,8},{10,11... | collective-permute-start | bytes 18440 | tf_op jit(solution)/shard_map/ppermute | solution.py:481
  45.0 5.3 %collective-permute-start.12 = (f32[1,1536]{1,0:T(1,128)S(1)}, f32[1,1536]{1,0:T(1,128)S(1)}, u32[]{:S(2)}, u32[]{:S(2)}) collective-permute-start(f32[1,1536]{1,0:T(1,128)S(1)} %get-tuple-element.62.sq0), channel_id=1, source_target_pairs={{0,2},{1,3},{2,0},{3,1},{4,6},{5,7},{6,4},{7,5},{8,10},{9,11},{10,... | collective-permute-start | bytes 18440 | tf_op jit(solution)/shard_map/ppermute | solution.py:481
  48.6 4.8 %collective-permute-start.11 = (f32[1,1536]{1,0:T(1,128)S(1)}, f32[1,1536]{1,0:T(1,128)S(1)}, u32[]{:S(2)}, u32[]{:S(2)}) collective-permute-start(f32[1,1536]{1,0:T(1,128)S(1)} %get-tuple-element.62.sq0), channel_id=1, source_target_pairs={{0,3},{1,2},{2,1},{3,0},{4,7},{5,6},{6,5},{7,4},{8,11},{9,10},{10,... | collective-permute-start | bytes 18440 | tf_op jit(solution)/shard_map/ppermute | solution.py:481

commit v4 on v3

--- a/solution.py
+++ b/solution.py
@@ -242,7 +242,7 @@
                 before = jnp.where(where[source] < place, 1.0, 0.0)
                 weight = jnp.where(first < ends(tokens, x, where[source]), before, 0.0)
                 total = total + refs[source][:part, :] * weight
-        for steps, ref in zip((3, 2, 1), ups):
+        for steps, ref in zip((1, 2, 3), ups):
             row = x ^ steps
             before = jnp.where(row < x, 1.0, 0.0)
             total = total + ref[...] * jnp.where(first < ends(tokens, row, SEQ_Y - 1), before, 0.0)
@@ -464,7 +464,7 @@
     first = local(0, mine[0])
     rows[3], first = lax.optimization_barrier((rows[3], first))
     (whole,) = small(row_kernel, tokens, rows, [part])
-    ups = [swap_rows(whole, d) for d in (3, 2, 1)]
+    ups = [swap_rows(whole, d) for d in (1, 2, 3)]
     second = local(1, whole)
     ups[2], second = lax.optimization_barrier((ups[2], second))
     carries = small(carry_kernel, tokens, (*rows, *ups), [part] * SEQ_Y)
@@ -478,7 +478,7 @@
     other, kept_squares = lax.optimization_barrier((other, kept_squares))
     away_attn, squares = finish(starts, queries, other, locals_, places_[: heads // 2], 0, kept_squares)
     sums = [squares] + [
-        lax.ppermute(squares, "head", [(z, z ^ d) for z in range(4)]) for d in (3, 2, 1)
+        lax.ppermute(squares, "head", [(z, (z + d) % 4) for z in range(4)]) for d in (1, 2, 3)
     ]
     return normalise(sums, norm_gain.reshape(1, width), away_attn, kept_attn)
 

time: 56.9 us -> 53.9 us (0.947)
  the two profiles are of different devices: /device:TPU:0 before, /device:TPU:2 now
where the time goes in v4:
time: 53.9 us; the launch traced here: 52.9 us
  Pallas kernels  25.2 us (47%)
  starting transfers between devices  20.6 us (38%)
  waiting for transfers between devices  6.8 us (13%)
    pallas_call x3, Pallas kernels, local_attention(): pl.pallas_call(functools.partial(local_kernel, column=column), out_shape=...  12.1 us
    ppermute x6, starting transfers between devices, turn_row(): lax.ppermute(value, 'seq', [(device_of(x, y, c), device_of(x, (y + steps)...  10.9 us
    ppermute x3, starting transfers between devices, on_device(): lax.ppermute(squares, 'head', [(z, (z + d) % 4) for z in range(4)])  5.37 us
    pallas_call x1, Pallas kernels, own_states(): pl.pallas_call(functools.partial(state_kernel, rows=rows), out_shape=[plt...  4.85 us
    ppermute x3, starting transfers between devices, swap_rows(): lax.ppermute(value, 'seq', [(device_of(x, y, c), device_of(x ^ steps, y,...  4.17 us
    ppermute x3, waiting for transfers between devices, on_device(): lax.ppermute(squares, 'head', [(z, (z + d) % 4) for z in range(4)])  3.87 us
    pallas_call x1, Pallas kernels, normalise(): pl.pallas_call(functools.partial(norm_kernel, rows=rows), out_shape=jax.S...  3.21 us
    pallas_call x2, Pallas kernels, finish(): pl.pallas_call(functools.partial(finish_kernel, places=places, kept=kept,...  3.04 us
  transfers between devices with their start and end apart: 14, of which 8 were waited for; matrix products, arithmetic and copies ran while one was open for 0% of the time, Pallas kernels for 28%

profile of v4, /device:TPU:2, one launch (start us, length us, event | category | flops | bytes accessed | tf_op | source)
XLA Modules:
  0.0 52.9 jit_solution(5224739567267789694)
XLA Ops:
  0.0 4.8 %shard_map.55 = (f32[1032,128]{1,0:T(8,128)S(1)}, bf16[1536,2048]{1,0:T(8,128)(2,1)S(1)}, bf16[1536,2048]{1,0:T(8,128)(2,1)S(1)}, s32[1,1536]{1,0:T(1,128)S(1)}) custom-call(s32[1536]{0:T(1024)} %starts_hbm.1, bf16[1536,2048]{1,0:T(8,128)(2,1)} %k_hbm.1, bf16[1536,2048]{1,0:T(8,128)(2,1)} %v_hbm.1), custom_call_target="tpu_custom_call" | custom-call | flops 402653184 | bytes 12582912 | tf_op jit(solution)/shard_map/pallas_call | solution.py:151
  5.0 1.4 %shard_map.56.keep = f32[1032,128]{1,0:T(8,128)S(1)} custom-call(s32[1,1536]{1,0:T(1,128)S(1)} %get-tuple-element.52.starts.starts_ref, bf16[1536,2048]{1,0:T(8,128)(2,1)S(1)} %get-tuple-element.38.k_ref, bf16[1536,2048]{1,0:T(8,128)(2,1)S(1)} %get-tuple-element.39.v_ref), custom_call_target="tpu_custom_call" | custom-call | flops 402653184 | bytes 6291456 | tf_op jit(solution)/shard_map/pallas_call | solution.py:166
  6.4 0.5 collective-permute-done.recv
  6.9 1.6 %collective-permute-start.1 = (f32[264,128]{1,0:T(8,128)S(1)}, f32[264,128]{1,0:T(8,128)S(1)}, u32[]{:S(2)}, u32[]{:S(2)}) collective-permute-start(f32[264,128]{1,0:T(8,128)S(1)} %get-tuple-element.41), channel_id=1, source_target_pairs={{0,8},{4,12},{8,16},{12,20},{16,24},{20,28},{24,0},{28,4},{32,40},... | collective-permute-start | bytes 405512 | tf_op jit(solution)/shard_map/ppermute | solution.py:38
  8.6 2.9 %collective-permute-start.2 = (f32[264,128]{1,0:T(8,128)S(1)}, f32[264,128]{1,0:T(8,128)S(1)}, u32[]{:S(2)}, u32[]{:S(2)}) collective-permute-start(f32[264,128]{1,0:T(8,128)S(1)} %get-tuple-element.42), channel_id=1, source_target_pairs={{0,16},{4,20},{8,24},{12,28},{16,0},{20,4},{24,8},{28,12},{32,48},... | collective-permute-start | bytes 405512 | tf_op jit(solution)/shard_map/ppermute | solution.py:38
  11.5 1.3 %collective-permute-start.3 = (f32[264,128]{1,0:T(8,128)S(1)}, f32[264,128]{1,0:T(8,128)S(1)}, u32[]{:S(2)}, u32[]{:S(2)}) collective-permute-start(f32[264,128]{1,0:T(8,128)S(1)} %get-tuple-element.43), channel_id=1, source_target_pairs={{0,24},{4,28},{8,0},{12,4},{16,8},{20,12},{24,16},{28,20},{32,56},... | collective-permute-start | bytes 405512 | tf_op jit(solution)/shard_map/ppermute | solution.py:38
  12.8 4.5 %shard_map.58.refs_0_ = f32[1536,768]{1,0:T(8,128)S(1)} custom-call(s32[1,1536]{1,0:T(1,128)S(1)} %get-tuple-element.52.starts.starts_ref, bf16[1536,2048]{1,0:T(8,128)(2,1)S(1)} %bitcast.2, bf16[1536,2048]{1,0:T(8,128)(2,1)S(1)} %get-tuple-element.38.k_ref, bf16[1536,2048]{1,0:T(8,128)(2,1)S(1)} %get-tuple-element.39.v_ref), custom_call_target="tpu_custom_call" | custom-call | flops 1811939328 | bytes 11796480 | tf_op jit(solution)/shard_map/pallas_call | solution.py:323
  17.5 0.5 collective-permute-done.2.from2
  18.0 1.6 %collective-permute-start.6 = (f32[256,128]{1,0:T(8,128)S(1)}, f32[256,128]{1,0:T(8,128)S(1)}, u32[]{:S(2)}, u32[]{:S(2)}) collective-permute-start(f32[256,128]{1,0:T(8,128)S(1)} %shard_map.59), channel_id=1, source_target_pairs={{0,96},{4,100},{8,104},{12,108},{16,112},{20,116},{24,120},{28,124... | collective-permute-start | bytes 393224 | tf_op jit(solution)/shard_map/ppermute | solution.py:46
  19.6 1.1 %collective-permute-start.5 = (f32[256,128]{1,0:T(8,128)S(1)}, f32[256,128]{1,0:T(8,128)S(1)}, u32[]{:S(2)}, u32[]{:S(2)}) collective-permute-start(f32[256,128]{1,0:T(8,128)S(1)} %shard_map.59), channel_id=1, source_target_pairs={{0,64},{4,68},{8,72},{12,76},{16,80},{20,84},{24,88},{28,92},{32,9... | collective-permute-start | bytes 393224 | tf_op jit(solution)/shard_map/ppermute | solution.py:46
  20.7 1.5 %collective-permute-start.4 = (f32[256,128]{1,0:T(8,128)S(1)}, f32[256,128]{1,0:T(8,128)S(1)}, u32[]{:S(2)}, u32[]{:S(2)}) collective-permute-start(f32[256,128]{1,0:T(8,128)S(1)} %shard_map.59), channel_id=1, source_target_pairs={{0,32},{4,36},{8,40},{12,44},{16,48},{20,52},{24,56},{28,60},{32,0... | collective-permute-start | bytes 393224 | tf_op jit(solution)/shard_map/ppermute | solution.py:46
  22.2 3.8 %shard_map.60.refs_1_ = f32[1536,640]{1,0:T(8,128)S(1)} custom-call(s32[1,1536]{1,0:T(1,128)S(1)} %get-tuple-element.52.starts.starts_ref, bf16[1536,2048]{1,0:T(8,128)(2,1)S(1)} %bitcast.2, bf16[1536,2048]{1,0:T(8,128)(2,1)S(1)} %get-tuple-element.38.k_ref, bf16[1536,2048]{1,0:T(8,128)(2,1)S(1)} %get-tuple-element.39.v_ref), custom_call_target="tpu_custom_call" | custom-call | flops 1509949440 | bytes 9830400 | tf_op jit(solution)/shard_map/pallas_call | solution.py:323
  26.0 1.0 %collective-permute-done.5.up2 = f32[256,128]{1,0:T(8,128)S(1)} collective-permute-done((f32[256,128]{1,0:T(8,128)S(1)}, f32[256,128]{1,0:T(8,128)S(1)}, u32[]{:S(2)}, u32[]{:S(2)}) %collective-permute-start.5) | collective-permute-done | bytes 131104 | tf_op jit(solution)/shard_map/ppermute | solution.py:46
  27.0 0.5 collective-permute-done.4.up3
  27.7 1.3 %collective-permute-start.7 = (f32[256,128]{1,0:T(8,128)S(1)}, f32[256,128]{1,0:T(8,128)S(1)}, u32[]{:S(2)}, u32[]{:S(2)}) collective-permute-start(f32[256,128]{1,0:T(8,128)S(1)} %get-tuple-element.49), channel_id=1, source_target_pairs={{0,8},{4,12},{8,16},{12,20},{16,24},{20,28},{24,0},{28,4},{32,40},... | collective-permute-start | bytes 393224 | tf_op jit(solution)/shard_map/ppermute | solution.py:38
  29.0 2.5 %collective-permute-start.8 = (f32[256,128]{1,0:T(8,128)S(1)}, f32[256,128]{1,0:T(8,128)S(1)}, u32[]{:S(2)}, u32[]{:S(2)}) collective-permute-start(f32[256,128]{1,0:T(8,128)S(1)} %get-tuple-element.50), channel_id=1, source_target_pairs={{0,16},{4,20},{8,24},{12,28},{16,0},{20,4},{24,8},{28,12},{32,48},... | collective-permute-start | bytes 393224 | tf_op jit(solution)/shard_map/ppermute | solution.py:38
  31.6 1.2 %collective-permute-start.9 = (f32[256,128]{1,0:T(8,128)S(1)}, f32[256,128]{1,0:T(8,128)S(1)}, u32[]{:S(2)}, u32[]{:S(2)}) collective-permute-start(f32[256,128]{1,0:T(8,128)S(1)} %get-tuple-element.51), channel_id=1, source_target_pairs={{0,24},{4,28},{8,0},{12,4},{16,8},{20,12},{24,16},{28,20},{32,56},... | collective-permute-start | bytes 393224 | tf_op jit(solution)/shard_map/ppermute | solution.py:38
  32.7 3.8 %shard_map.62.refs_2_ = f32[1536,640]{1,0:T(8,128)S(1)} custom-call(s32[1,1536]{1,0:T(1,128)S(1)} %get-tuple-element.52.starts.starts_ref, bf16[1536,2048]{1,0:T(8,128)(2,1)S(1)} %bitcast.2, bf16[1536,2048]{1,0:T(8,128)(2,1)S(1)} %get-tuple-element.38.k_ref, bf16[1536,2048]{1,0:T(8,128)(2,1)S(1)} %get-tuple-element.39.v_ref), custom_call_target="tpu_custom_call" | custom-call | flops 1509949440 | bytes 9830400 | tf_op jit(solution)/shard_map/pallas_call | solution.py:323
  36.8 1.5 %shard_map.64 = (f32[1536,1024]{1,0:T(8,128)S(1)}, f32[1,1536]{1,0:T(1,128)S(1)}) custom-call(s32[1,1536]{1,0:T(1,128)S(1)} %get-tuple-element.52.starts.starts_ref, bf16[1536,2048]{1,0:T(8,128)(2,1)S(1)} %bitcast.2, f32[1024,128]{1,0:T(8,128)S(1)} %get-tuple-element.55.carry, f32[1536,768]{1,0:T(8,128)S(1)} %shard_map.58.refs_0_, ...), custom_call_target="tpu_custom_call" | custom-call | flops 402653184 | bytes 9437184 | tf_op jit(solution)/shard_map/pallas_call | solution.py:373
  38.7 1.5 %shard_map.65 = (f32[1536,1024]{1,0:T(8,128)S(1)}, f32[1,1536]{1,0:T(1,128)S(1)}) custom-call(s32[1,1536]{1,0:T(1,128)S(1)} %get-tuple-element.52.starts.starts_ref, bf16[1536,2048]{1,0:T(8,128)(2,1)S(1)} %bitcast.2, f32[1024,128]{1,0:T(8,128)S(1)} %collective-permute-done.10.carry, f32[1536,768]{1,0:T(8,128)S(1)} %shard_map.58.refs_0_, ...), custom_call_target="tpu_custom_call" | custom-call | flops 402653184 | bytes 9437184 | tf_op jit(solution)/shard_map/pallas_call | solution.py:373
  40.3 4.1 %collective-permute-start.13 = (f32[1,1536]{1,0:T(1,128)S(1)}, f32[1,1536]{1,0:T(1,128)S(1)}, u32[]{:S(2)}, u32[]{:S(2)}) collective-permute-start(f32[1,1536]{1,0:T(1,128)S(1)} %get-tuple-element.62.sq0), channel_id=1, source_target_pairs={{0,3},{1,0},{2,1},{3,2},{4,7},{5,4},{6,5},{7,6},{8,11},{9,8},{10,9... | collective-permute-start | bytes 18440 | tf_op jit(solution)/shard_map/ppermute | solution.py:481
  44.4 1.3 %collective-permute-start.11 = (f32[1,1536]{1,0:T(1,128)S(1)}, f32[1,1536]{1,0:T(1,128)S(1)}, u32[]{:S(2)}, u32[]{:S(2)}) collective-permute-start(f32[1,1536]{1,0:T(1,128)S(1)} %get-tuple-element.62.sq0), channel_id=1, source_target_pairs={{0,1},{1,2},{2,3},{3,0},{4,5},{5,6},{6,7},{7,4},{8,9},{9,10},{10,1... | collective-permute-start | bytes 18440 | tf_op jit(solution)/shard_map/ppermute | solution.py:481
  45.7 3.8 %collective-permute-done.12.sq2 = f32[1,1536]{1,0:T(1,128)S(1)} collective-permute-done((f32[1,1536]{1,0:T(1,128)S(1)}, f32[1,1536]{1,0:T(1,128)S(1)}, u32[]{:S(2)}, u32[]{:S(2)}) %collective-permute-start.12) | collective-permute-done | bytes 6176 | tf_op jit(solution)/shard_map/ppermute | solution.py:481
  49.5 3.2 %shard_map.66 = bf16[1536,2048]{1,0:T(8,128)(2,1)} custom-call(f32[1,1536]{1,0:T(1,128)S(1)} %get-tuple-element.62.sq0, f32[1,1536]{1,0:T(1,128)S(1)} %collective-permute-done.11.sq1, f32[1,1536]{1,0:T(1,128)S(1)} %collective-permute-done.12.sq2, f32[1,1536]{1,0:T(1,128)S(1)} %collective-permute-done.13.sq3, f32[1,2048]{1,0:T(1,128)S(1)} %bitcast.3, ...), custom_call_target="tpu_custom_call" | custom-call | flops 6291456 | bytes 18874368 | tf_op jit(solution)/shard_map/pallas_call | solution.py:428
  (23 shorter events, 1.4 us)
Async XLA Ops:
  0.0 12.8 %slice-start = ((s8[6291456]{0:T(1024)(128)(4,1)}), s8[4194304]{0:T(1024)(128)(4,1)S(1)}, s32[]{:S(2)}) async-start(s8[6291456]{0:T(1024)(128)(4,1)} %bitcast.1), calls=%async_computation | async-start | bytes 8388608
  4.9 2.0 %collective-permute-start = (f32[1032,128]{1,0:T(8,128)S(1)}, f32[1032,128]{1,0:T(8,128)S(1)}, u32[]{:S(2)}, u32[]{:S(2)}) collective-permute-start(f32[1032,128]{1,0:T(8,128)S(1)} %get-tuple-element.36), channel_id=1, source_target_pairs={{0,4},{4,0},{8,12},{12,8},{16,20},{20,16},{24,28},{28,24},{32,36},... | collective-permute-start | bytes 1585160 | tf_op jit(solution)/shard_map/ppermute | solution.py:32
  5.0 7.9 %slice-start.1 = ((s8[6291456]{0:T(1024)(128)(4,1)}), s8[2097152]{0:T(1024)(128)(4,1)S(1)}, s32[]{:S(2)}) async-start(s8[6291456]{0:T(1024)(128)(4,1)} %bitcast.1), calls=%async_computation.1 | async-start | bytes 4194304
  6.9 10.5 %collective-permute-start.1 = (f32[264,128]{1,0:T(8,128)S(1)}, f32[264,128]{1,0:T(8,128)S(1)}, u32[]{:S(2)}, u32[]{:S(2)}) collective-permute-start(f32[264,128]{1,0:T(8,128)S(1)} %get-tuple-element.41), channel_id=1, source_target_pairs={{0,8},{4,12},{8,16},{12,20},{16,24},{20,28},{24,0},{28,4},{32,40},... | collective-permute-start | bytes 405512 | tf_op jit(solution)/shard_map/ppermute | solution.py:38
  8.6 9.4 %collective-permute-start.2 = (f32[264,128]{1,0:T(8,128)S(1)}, f32[264,128]{1,0:T(8,128)S(1)}, u32[]{:S(2)}, u32[]{:S(2)}) collective-permute-start(f32[264,128]{1,0:T(8,128)S(1)} %get-tuple-element.42), channel_id=1, source_target_pairs={{0,16},{4,20},{8,24},{12,28},{16,0},{20,4},{24,8},{28,12},{32,48},... | collective-permute-start | bytes 405512 | tf_op jit(solution)/shard_map/ppermute | solution.py:38
  11.5 6.0 %collective-permute-start.3 = (f32[264,128]{1,0:T(8,128)S(1)}, f32[264,128]{1,0:T(8,128)S(1)}, u32[]{:S(2)}, u32[]{:S(2)}) collective-permute-start(f32[264,128]{1,0:T(8,128)S(1)} %get-tuple-element.43), channel_id=1, source_target_pairs={{0,24},{4,28},{8,0},{12,4},{16,8},{20,12},{24,16},{28,20},{32,56},... | collective-permute-start | bytes 405512 | tf_op jit(solution)/shard_map/ppermute | solution.py:38
  18.0 8.0 %collective-permute-start.6 = (f32[256,128]{1,0:T(8,128)S(1)}, f32[256,128]{1,0:T(8,128)S(1)}, u32[]{:S(2)}, u32[]{:S(2)}) collective-permute-start(f32[256,128]{1,0:T(8,128)S(1)} %shard_map.59), channel_id=1, source_target_pairs={{0,96},{4,100},{8,104},{12,108},{16,112},{20,116},{24,120},{28,124... | collective-permute-start | bytes 393224 | tf_op jit(solution)/shard_map/ppermute | solution.py:46
  19.6 7.4 %collective-permute-start.5 = (f32[256,128]{1,0:T(8,128)S(1)}, f32[256,128]{1,0:T(8,128)S(1)}, u32[]{:S(2)}, u32[]{:S(2)}) collective-permute-start(f32[256,128]{1,0:T(8,128)S(1)} %shard_map.59), channel_id=1, source_target_pairs={{0,64},{4,68},{8,72},{12,76},{16,80},{20,84},{24,88},{28,92},{32,9... | collective-permute-start | bytes 393224 | tf_op jit(solution)/shard_map/ppermute | solution.py:46
  20.7 6.7 %collective-permute-start.4 = (f32[256,128]{1,0:T(8,128)S(1)}, f32[256,128]{1,0:T(8,128)S(1)}, u32[]{:S(2)}, u32[]{:S(2)}) collective-permute-start(f32[256,128]{1,0:T(8,128)S(1)} %shard_map.59), channel_id=1, source_target_pairs={{0,32},{4,36},{8,40},{12,44},{16,48},{20,52},{24,56},{28,60},{32,0... | collective-permute-start | bytes 393224 | tf_op jit(solution)/shard_map/ppermute | solution.py:46
  27.7 8.8 %collective-permute-start.7 = (f32[256,128]{1,0:T(8,128)S(1)}, f32[256,128]{1,0:T(8,128)S(1)}, u32[]{:S(2)}, u32[]{:S(2)}) collective-permute-start(f32[256,128]{1,0:T(8,128)S(1)} %get-tuple-element.49), channel_id=1, source_target_pairs={{0,8},{4,12},{8,16},{12,20},{16,24},{20,28},{24,0},{28,4},{32,40},... | collective-permute-start | bytes 393224 | tf_op jit(solution)/shard_map/ppermute | solution.py:38
  29.0 7.5 %collective-permute-start.8 = (f32[256,128]{1,0:T(8,128)S(1)}, f32[256,128]{1,0:T(8,128)S(1)}, u32[]{:S(2)}, u32[]{:S(2)}) collective-permute-start(f32[256,128]{1,0:T(8,128)S(1)} %get-tuple-element.50), channel_id=1, source_target_pairs={{0,16},{4,20},{8,24},{12,28},{16,0},{20,4},{24,8},{28,12},{32,48},... | collective-permute-start | bytes 393224 | tf_op jit(solution)/shard_map/ppermute | solution.py:38
  31.6 5.0 %collective-permute-start.9 = (f32[256,128]{1,0:T(8,128)S(1)}, f32[256,128]{1,0:T(8,128)S(1)}, u32[]{:S(2)}, u32[]{:S(2)}) collective-permute-start(f32[256,128]{1,0:T(8,128)S(1)} %get-tuple-element.51), channel_id=1, source_target_pairs={{0,24},{4,28},{8,0},{12,4},{16,8},{20,12},{24,16},{28,20},{32,56},... | collective-permute-start | bytes 393224 | tf_op jit(solution)/shard_map/ppermute | solution.py:38
  36.7 2.0 %collective-permute-start.10 = (f32[1024,128]{1,0:T(8,128)S(1)}, f32[1024,128]{1,0:T(8,128)S(1)}, u32[]{:S(2)}, u32[]{:S(2)}) collective-permute-start(f32[1024,128]{1,0:T(8,128)S(1)} %get-tuple-element.54), channel_id=1, source_target_pairs={{0,4},{4,0},{8,12},{12,8},{16,20},{20,16},{24,28},{28,24},{32,36},... | collective-permute-start | bytes 1572872 | tf_op jit(solution)/shard_map/ppermute | solution.py:32
  38.7 10.8 %copy-start = (f32[2048]{0:T(1024)S(1)}, f32[2048]{0:T(1024)}, u32[]{:S(2)}) copy-start(f32[2048]{0:T(1024)} %param.9) | copy-start | bytes 24580
  40.3 5.4 %collective-permute-start.13 = (f32[1,1536]{1,0:T(1,128)S(1)}, f32[1,1536]{1,0:T(1,128)S(1)}, u32[]{:S(2)}, u32[]{:S(2)}) collective-permute-start(f32[1,1536]{1,0:T(1,128)S(1)} %get-tuple-element.62.sq0), channel_id=1, source_target_pairs={{0,3},{1,0},{2,1},{3,2},{4,7},{5,4},{6,5},{7,6},{8,11},{9,8},{10,9... | collective-permute-start | bytes 18440 | tf_op jit(solution)/shard_map/ppermute | solution.py:481
  44.4 5.1 %collective-permute-start.12 = (f32[1,1536]{1,0:T(1,128)S(1)}, f32[1,1536]{1,0:T(1,128)S(1)}, u32[]{:S(2)}, u32[]{:S(2)}) collective-permute-start(f32[1,1536]{1,0:T(1,128)S(1)} %get-tuple-element.62.sq0), channel_id=1, source_target_pairs={{0,2},{1,3},{2,0},{3,1},{4,6},{5,7},{6,4},{7,5},{8,10},{9,11},{10,... | collective-permute-start | bytes 18440 | tf_op jit(solution)/shard_map/ppermute | solution.py:481
  44.4 5.1 %collective-permute-start.11 = (f32[1,1536]{1,0:T(1,128)S(1)}, f32[1,1536]{1,0:T(1,128)S(1)}, u32[]{:S(2)}, u32[]{:S(2)}) collective-permute-start(f32[1,1536]{1,0:T(1,128)S(1)} %get-tuple-element.62.sq0), channel_id=1, source_target_pairs={{0,1},{1,2},{2,3},{3,0},{4,5},{5,6},{6,7},{7,4},{8,9},{9,10},{10,1... | collective-permute-start | bytes 18440 | tf_op jit(solution)/shard_map/ppermute | solution.py:481

commit v5 on v4

--- a/solution.py
+++ b/solution.py
@@ -242,7 +242,7 @@
                 before = jnp.where(where[source] < place, 1.0, 0.0)
                 weight = jnp.where(first < ends(tokens, x, where[source]), before, 0.0)
                 total = total + refs[source][:part, :] * weight
-        for steps, ref in zip((1, 2, 3), ups):
+        for steps, ref in zip((1, 3, 2), ups):
             row = x ^ steps
             before = jnp.where(row < x, 1.0, 0.0)
             total = total + ref[...] * jnp.where(first < ends(tokens, row, SEQ_Y - 1), before, 0.0)
@@ -464,7 +464,7 @@
     first = local(0, mine[0])
     rows[3], first = lax.optimization_barrier((rows[3], first))
     (whole,) = small(row_kernel, tokens, rows, [part])
-    ups = [swap_rows(whole, d) for d in (1, 2, 3)]
+    ups = [swap_rows(whole, d) for d in (1, 3, 2)]
     second = local(1, whole)
     ups[2], second = lax.optimization_barrier((ups[2], second))
     carries = small(carry_kernel, tokens, (*rows, *ups), [part] * SEQ_Y)
@@ -478,7 +478,7 @@
     other, kept_squares = lax.optimization_barrier((other, kept_squares))
     away_attn, squares = finish(starts, queries, other, locals_, places_[: heads // 2], 0, kept_squares)
     sums = [squares] + [
-        lax.ppermute(squares, "head", [(z, (z + d) % 4) for z in range(4)]) for d in (1, 2, 3)
+        lax.ppermute(squares, "head", [(z, (z + d) % 4) for z in range(4)]) for d in (3, 2, 1)
     ]
     return normalise(sums, norm_gain.reshape(1, width), away_attn, kept_attn)
 

time: 53.9 us -> 53.7 us (level); the launches traced: 52.9 us -> 53.6 us
  starting transfers between devices: 20.6 us -> 22.4 us
  waiting for transfers between devices: 6.8 us -> 5.66 us
    ppermute x3, waiting for transfers between devices: 3.87 us -> 2.61 us  [on_device(): lax.ppermute(squares, 'head', [(z, (z + d) % 4) for z in range(4)])]
    ppermute x3, starting transfers between devices: 5.37 us -> 6.58 us  [on_device(): lax.ppermute(squares, 'head', [(z, (z + d) % 4) for z in range(4)])]
    ppermute x6, waiting for transfers between devices: 0.66 us -> 1.63 us  [turn_row(): lax.ppermute(value, 'seq', [(device_of(x, y, c), device_of(x, (y + steps)...]
    ppermute x3, waiting for transfers between devices: 1.44 us -> 0.59 us  [swap_rows(): lax.ppermute(value, 'seq', [(device_of(x, y, c), device_of(x ^ steps, y,...]
    ppermute x3, starting transfers between devices: 4.17 us -> 4.78 us  [swap_rows(): lax.ppermute(value, 'seq', [(device_of(x, y, c), device_of(x ^ steps, y,...]
  transfers between devices with their start and end apart: 14 -> 14, of which waited for: 8 -> 9; matrix products, arithmetic and copies ran while one was open for 0% -> 0% of each run, Pallas kernels for 28% -> 28%
where the time goes in v5:
time: 53.7 us; the launch traced here: 53.6 us
  Pallas kernels  25.2 us (47%)
  starting transfers between devices  22.4 us (42%)
  waiting for transfers between devices  5.66 us (11%)
    pallas_call x3, Pallas kernels, local_attention(): pl.pallas_call(functools.partial(local_kernel, column=column), out_shape=...  12.1 us
    ppermute x6, starting transfers between devices, turn_row(): lax.ppermute(value, 'seq', [(device_of(x, y, c), device_of(x, (y + steps)...  10.9 us
    ppermute x3, starting transfers between devices, on_device(): lax.ppermute(squares, 'head', [(z, (z + d) % 4) for z in range(4)])  6.58 us
    pallas_call x1, Pallas kernels, own_states(): pl.pallas_call(functools.partial(state_kernel, rows=rows), out_shape=[plt...  4.85 us
    ppermute x3, starting transfers between devices, swap_rows(): lax.ppermute(value, 'seq', [(device_of(x, y, c), device_of(x ^ steps, y,...  4.78 us
    pallas_call x1, Pallas kernels, normalise(): pl.pallas_call(functools.partial(norm_kernel, rows=rows), out_shape=jax.S...  3.2 us
    pallas_call x2, Pallas kernels, finish(): pl.pallas_call(functools.partial(finish_kernel, places=places, kept=kept,...  3.04 us
    ppermute x3, waiting for transfers between devices, on_device(): lax.ppermute(squares, 'head', [(z, (z + d) % 4) for z in range(4)])  2.61 us
  transfers between devices with their start and end apart: 14, of which 9 were waited for; matrix products, arithmetic and copies ran while one was open for 0% of the time, Pallas kernels for 28%

profile of v5, /device:TPU:2, one launch (start us, length us, event | category | flops | bytes accessed | tf_op | source)
XLA Modules:
  0.0 53.6 jit_solution(17623677637800228451)
XLA Ops:
  0.0 4.8 %shard_map.55 = (f32[1032,128]{1,0:T(8,128)S(1)}, bf16[1536,2048]{1,0:T(8,128)(2,1)S(1)}, bf16[1536,2048]{1,0:T(8,128)(2,1)S(1)}, s32[1,1536]{1,0:T(1,128)S(1)}) custom-call(s32[1536]{0:T(1024)} %starts_hbm.1, bf16[1536,2048]{1,0:T(8,128)(2,1)} %k_hbm.1, bf16[1536,2048]{1,0:T(8,128)(2,1)} %v_hbm.1), custom_call_target="tpu_custom_call" | custom-call | flops 402653184 | bytes 12582912 | tf_op jit(solution)/shard_map/pallas_call | solution.py:151
  5.0 1.4 %shard_map.56.keep = f32[1032,128]{1,0:T(8,128)S(1)} custom-call(s32[1,1536]{1,0:T(1,128)S(1)} %get-tuple-element.52.starts.starts_ref, bf16[1536,2048]{1,0:T(8,128)(2,1)S(1)} %get-tuple-element.38.k_ref, bf16[1536,2048]{1,0:T(8,128)(2,1)S(1)} %get-tuple-element.39.v_ref), custom_call_target="tpu_custom_call" | custom-call | flops 402653184 | bytes 6291456 | tf_op jit(solution)/shard_map/pallas_call | solution.py:166
  6.9 1.6 %collective-permute-start.1 = (f32[264,128]{1,0:T(8,128)S(1)}, f32[264,128]{1,0:T(8,128)S(1)}, u32[]{:S(2)}, u32[]{:S(2)}) collective-permute-start(f32[264,128]{1,0:T(8,128)S(1)} %get-tuple-element.41), channel_id=1, source_target_pairs={{0,8},{4,12},{8,16},{12,20},{16,24},{20,28},{24,0},{28,4},{32,40},... | collective-permute-start | bytes 405512 | tf_op jit(solution)/shard_map/ppermute | solution.py:38
  8.6 2.9 %collective-permute-start.2 = (f32[264,128]{1,0:T(8,128)S(1)}, f32[264,128]{1,0:T(8,128)S(1)}, u32[]{:S(2)}, u32[]{:S(2)}) collective-permute-start(f32[264,128]{1,0:T(8,128)S(1)} %get-tuple-element.42), channel_id=1, source_target_pairs={{0,16},{4,20},{8,24},{12,28},{16,0},{20,4},{24,8},{28,12},{32,48},... | collective-permute-start | bytes 405512 | tf_op jit(solution)/shard_map/ppermute | solution.py:38
  11.5 1.3 %collective-permute-start.3 = (f32[264,128]{1,0:T(8,128)S(1)}, f32[264,128]{1,0:T(8,128)S(1)}, u32[]{:S(2)}, u32[]{:S(2)}) collective-permute-start(f32[264,128]{1,0:T(8,128)S(1)} %get-tuple-element.43), channel_id=1, source_target_pairs={{0,24},{4,28},{8,0},{12,4},{16,8},{20,12},{24,16},{28,20},{32,56},... | collective-permute-start | bytes 405512 | tf_op jit(solution)/shard_map/ppermute | solution.py:38
  12.8 4.5 %shard_map.58.refs_0_ = f32[1536,768]{1,0:T(8,128)S(1)} custom-call(s32[1,1536]{1,0:T(1,128)S(1)} %get-tuple-element.52.starts.starts_ref, bf16[1536,2048]{1,0:T(8,128)(2,1)S(1)} %bitcast.2, bf16[1536,2048]{1,0:T(8,128)(2,1)S(1)} %get-tuple-element.38.k_ref, bf16[1536,2048]{1,0:T(8,128)(2,1)S(1)} %get-tuple-element.39.v_ref), custom_call_target="tpu_custom_call" | custom-call | flops 1811939328 | bytes 11796480 | tf_op jit(solution)/shard_map/pallas_call | solution.py:323
  17.5 0.5 collective-permute-done.2.from2
  18.0 2.2 %collective-permute-start.6 = (f32[256,128]{1,0:T(8,128)S(1)}, f32[256,128]{1,0:T(8,128)S(1)}, u32[]{:S(2)}, u32[]{:S(2)}) collective-permute-start(f32[256,128]{1,0:T(8,128)S(1)} %shard_map.59), channel_id=1, source_target_pairs={{0,64},{4,68},{8,72},{12,76},{16,80},{20,84},{24,88},{28,92},{32,9... | collective-permute-start | bytes 393224 | tf_op jit(solution)/shard_map/ppermute | solution.py:46
  20.2 2.6 %collective-permute-start.4 = (f32[256,128]{1,0:T(8,128)S(1)}, f32[256,128]{1,0:T(8,128)S(1)}, u32[]{:S(2)}, u32[]{:S(2)}) collective-permute-start(f32[256,128]{1,0:T(8,128)S(1)} %shard_map.59), channel_id=1, source_target_pairs={{0,32},{4,36},{8,40},{12,44},{16,48},{20,52},{24,56},{28,60},{32,0... | collective-permute-start | bytes 393224 | tf_op jit(solution)/shard_map/ppermute | solution.py:46
  22.8 3.8 %shard_map.60.refs_1_ = f32[1536,640]{1,0:T(8,128)S(1)} custom-call(s32[1,1536]{1,0:T(1,128)S(1)} %get-tuple-element.52.starts.starts_ref, bf16[1536,2048]{1,0:T(8,128)(2,1)S(1)} %bitcast.2, bf16[1536,2048]{1,0:T(8,128)(2,1)S(1)} %get-tuple-element.38.k_ref, bf16[1536,2048]{1,0:T(8,128)(2,1)S(1)} %get-tuple-element.39.v_ref), custom_call_target="tpu_custom_call" | custom-call | flops 1509949440 | bytes 9830400 | tf_op jit(solution)/shard_map/pallas_call | solution.py:323
  26.6 0.5 collective-permute-done.5.up2
  27.5 1.3 %collective-permute-start.7 = (f32[256,128]{1,0:T(8,128)S(1)}, f32[256,128]{1,0:T(8,128)S(1)}, u32[]{:S(2)}, u32[]{:S(2)}) collective-permute-start(f32[256,128]{1,0:T(8,128)S(1)} %get-tuple-element.49), channel_id=1, source_target_pairs={{0,8},{4,12},{8,16},{12,20},{16,24},{20,28},{24,0},{28,4},{32,40},... | collective-permute-start | bytes 393224 | tf_op jit(solution)/shard_map/ppermute | solution.py:38
  28.8 2.5 %collective-permute-start.8 = (f32[256,128]{1,0:T(8,128)S(1)}, f32[256,128]{1,0:T(8,128)S(1)}, u32[]{:S(2)}, u32[]{:S(2)}) collective-permute-start(f32[256,128]{1,0:T(8,128)S(1)} %get-tuple-element.50), channel_id=1, source_target_pairs={{0,16},{4,20},{8,24},{12,28},{16,0},{20,4},{24,8},{28,12},{32,48},... | collective-permute-start | bytes 393224 | tf_op jit(solution)/shard_map/ppermute | solution.py:38
  31.3 1.2 %collective-permute-start.9 = (f32[256,128]{1,0:T(8,128)S(1)}, f32[256,128]{1,0:T(8,128)S(1)}, u32[]{:S(2)}, u32[]{:S(2)}) collective-permute-start(f32[256,128]{1,0:T(8,128)S(1)} %get-tuple-element.51), channel_id=1, source_target_pairs={{0,24},{4,28},{8,0},{12,4},{16,8},{20,12},{24,16},{28,20},{32,56},... | collective-permute-start | bytes 393224 | tf_op jit(solution)/shard_map/ppermute | solution.py:38
  32.5 3.8 %shard_map.62.refs_2_ = f32[1536,640]{1,0:T(8,128)S(1)} custom-call(s32[1,1536]{1,0:T(1,128)S(1)} %get-tuple-element.52.starts.starts_ref, bf16[1536,2048]{1,0:T(8,128)(2,1)S(1)} %bitcast.2, bf16[1536,2048]{1,0:T(8,128)(2,1)S(1)} %get-tuple-element.38.k_ref, bf16[1536,2048]{1,0:T(8,128)(2,1)S(1)} %get-tuple-element.39.v_ref), custom_call_target="tpu_custom_call" | custom-call | flops 1509949440 | bytes 9830400 | tf_op jit(solution)/shard_map/pallas_call | solution.py:323
  36.3 1.0 %collective-permute-done.9.got3 = f32[256,128]{1,0:T(8,128)S(1)} collective-permute-done((f32[256,128]{1,0:T(8,128)S(1)}, f32[256,128]{1,0:T(8,128)S(1)}, u32[]{:S(2)}, u32[]{:S(2)}) %collective-permute-start.9) | collective-permute-done | bytes 131104 | tf_op jit(solution)/shard_map/ppermute | solution.py:38
  37.6 1.5 %shard_map.64 = (f32[1536,1024]{1,0:T(8,128)S(1)}, f32[1,1536]{1,0:T(1,128)S(1)}) custom-call(s32[1,1536]{1,0:T(1,128)S(1)} %get-tuple-element.52.starts.starts_ref, bf16[1536,2048]{1,0:T(8,128)(2,1)S(1)} %bitcast.2, f32[1024,128]{1,0:T(8,128)S(1)} %get-tuple-element.55.carry, f32[1536,768]{1,0:T(8,128)S(1)} %shard_map.58.refs_0_, ...), custom_call_target="tpu_custom_call" | custom-call | flops 402653184 | bytes 9437184 | tf_op jit(solution)/shard_map/pallas_call | solution.py:373
  39.5 1.5 %shard_map.65 = (f32[1536,1024]{1,0:T(8,128)S(1)}, f32[1,1536]{1,0:T(1,128)S(1)}) custom-call(s32[1,1536]{1,0:T(1,128)S(1)} %get-tuple-element.52.starts.starts_ref, bf16[1536,2048]{1,0:T(8,128)(2,1)S(1)} %bitcast.2, f32[1024,128]{1,0:T(8,128)S(1)} %collective-permute-done.10.carry, f32[1536,768]{1,0:T(8,128)S(1)} %shard_map.58.refs_0_, ...), custom_call_target="tpu_custom_call" | custom-call | flops 402653184 | bytes 9437184 | tf_op jit(solution)/shard_map/pallas_call | solution.py:373
  41.0 2.0 %collective-permute-start.13 = (f32[1,1536]{1,0:T(1,128)S(1)}, f32[1,1536]{1,0:T(1,128)S(1)}, u32[]{:S(2)}, u32[]{:S(2)}) collective-permute-start(f32[1,1536]{1,0:T(1,128)S(1)} %get-tuple-element.62.sq0), channel_id=1, source_target_pairs={{0,1},{1,2},{2,3},{3,0},{4,5},{5,6},{6,7},{7,4},{8,9},{9,10},{10,1... | collective-permute-start | bytes 18440 | tf_op jit(solution)/shard_map/ppermute | solution.py:481
  43.0 3.6 %collective-permute-start.12 = (f32[1,1536]{1,0:T(1,128)S(1)}, f32[1,1536]{1,0:T(1,128)S(1)}, u32[]{:S(2)}, u32[]{:S(2)}) collective-permute-start(f32[1,1536]{1,0:T(1,128)S(1)} %get-tuple-element.62.sq0), channel_id=1, source_target_pairs={{0,2},{1,3},{2,0},{3,1},{4,6},{5,7},{6,4},{7,5},{8,10},{9,11},{10,... | collective-permute-start | bytes 18440 | tf_op jit(solution)/shard_map/ppermute | solution.py:481
  46.6 1.0 %collective-permute-start.11 = (f32[1,1536]{1,0:T(1,128)S(1)}, f32[1,1536]{1,0:T(1,128)S(1)}, u32[]{:S(2)}, u32[]{:S(2)}) collective-permute-start(f32[1,1536]{1,0:T(1,128)S(1)} %get-tuple-element.62.sq0), channel_id=1, source_target_pairs={{0,3},{1,0},{2,1},{3,2},{4,7},{5,4},{6,5},{7,6},{8,11},{9,8},{10,9... | collective-permute-start | bytes 18440 | tf_op jit(solution)/shard_map/ppermute | solution.py:481
  47.6 0.7 %collective-permute-done.12.sq2 = f32[1,1536]{1,0:T(1,128)S(1)} collective-permute-done((f32[1,1536]{1,0:T(1,128)S(1)}, f32[1,1536]{1,0:T(1,128)S(1)}, u32[]{:S(2)}, u32[]{:S(2)}) %collective-permute-start.12) | collective-permute-done | bytes 6176 | tf_op jit(solution)/shard_map/ppermute | solution.py:481
  48.2 2.0 %collective-permute-done.11.sq1 = f32[1,1536]{1,0:T(1,128)S(1)} collective-permute-done((f32[1,1536]{1,0:T(1,128)S(1)}, f32[1,1536]{1,0:T(1,128)S(1)}, u32[]{:S(2)}, u32[]{:S(2)}) %collective-permute-start.11) | collective-permute-done | bytes 6176 | tf_op jit(solution)/shard_map/ppermute | solution.py:481
  50.2 3.2 %shard_map.66 = bf16[1536,2048]{1,0:T(8,128)(2,1)} custom-call(f32[1,1536]{1,0:T(1,128)S(1)} %get-tuple-element.62.sq0, f32[1,1536]{1,0:T(1,128)S(1)} %collective-permute-done.11.sq1, f32[1,1536]{1,0:T(1,128)S(1)} %collective-permute-done.12.sq2, f32[1,1536]{1,0:T(1,128)S(1)} %collective-permute-done.13.sq3, f32[1,2048]{1,0:T(1,128)S(1)} %bitcast.3, ...), custom_call_target="tpu_custom_call" | custom-call | flops 6291456 | bytes 18874368 | tf_op jit(solution)/shard_map/pallas_call | solution.py:428
  (23 shorter events, 1.8 us)
Async XLA Ops:
  0.0 12.8 %slice-start = ((s8[6291456]{0:T(1024)(128)(4,1)}), s8[4194304]{0:T(1024)(128)(4,1)S(1)}, s32[]{:S(2)}) async-start(s8[6291456]{0:T(1024)(128)(4,1)} %bitcast.1), calls=%async_computation | async-start | bytes 8388608
  4.9 2.0 %collective-permute-start = (f32[1032,128]{1,0:T(8,128)S(1)}, f32[1032,128]{1,0:T(8,128)S(1)}, u32[]{:S(2)}, u32[]{:S(2)}) collective-permute-start(f32[1032,128]{1,0:T(8,128)S(1)} %get-tuple-element.36), channel_id=1, source_target_pairs={{0,4},{4,0},{8,12},{12,8},{16,20},{20,16},{24,28},{28,24},{32,36},... | collective-permute-start | bytes 1585160 | tf_op jit(solution)/shard_map/ppermute | solution.py:32
  5.0 7.9 %slice-start.1 = ((s8[6291456]{0:T(1024)(128)(4,1)}), s8[2097152]{0:T(1024)(128)(4,1)S(1)}, s32[]{:S(2)}) async-start(s8[6291456]{0:T(1024)(128)(4,1)} %bitcast.1), calls=%async_computation.1 | async-start | bytes 4194304
  6.9 10.5 %collective-permute-start.1 = (f32[264,128]{1,0:T(8,128)S(1)}, f32[264,128]{1,0:T(8,128)S(1)}, u32[]{:S(2)}, u32[]{:S(2)}) collective-permute-start(f32[264,128]{1,0:T(8,128)S(1)} %get-tuple-element.41), channel_id=1, source_target_pairs={{0,8},{4,12},{8,16},{12,20},{16,24},{20,28},{24,0},{28,4},{32,40},... | collective-permute-start | bytes 405512 | tf_op jit(solution)/shard_map/ppermute | solution.py:38
  8.6 9.4 %collective-permute-start.2 = (f32[264,128]{1,0:T(8,128)S(1)}, f32[264,128]{1,0:T(8,128)S(1)}, u32[]{:S(2)}, u32[]{:S(2)}) collective-permute-start(f32[264,128]{1,0:T(8,128)S(1)} %get-tuple-element.42), channel_id=1, source_target_pairs={{0,16},{4,20},{8,24},{12,28},{16,0},{20,4},{24,8},{28,12},{32,48},... | collective-permute-start | bytes 405512 | tf_op jit(solution)/shard_map/ppermute | solution.py:38
  11.5 6.0 %collective-permute-start.3 = (f32[264,128]{1,0:T(8,128)S(1)}, f32[264,128]{1,0:T(8,128)S(1)}, u32[]{:S(2)}, u32[]{:S(2)}) collective-permute-start(f32[264,128]{1,0:T(8,128)S(1)} %get-tuple-element.43), channel_id=1, source_target_pairs={{0,24},{4,28},{8,0},{12,4},{16,8},{20,12},{24,16},{28,20},{32,56},... | collective-permute-start | bytes 405512 | tf_op jit(solution)/shard_map/ppermute | solution.py:38
  18.0 8.6 %collective-permute-start.6 = (f32[256,128]{1,0:T(8,128)S(1)}, f32[256,128]{1,0:T(8,128)S(1)}, u32[]{:S(2)}, u32[]{:S(2)}) collective-permute-start(f32[256,128]{1,0:T(8,128)S(1)} %shard_map.59), channel_id=1, source_target_pairs={{0,64},{4,68},{8,72},{12,76},{16,80},{20,84},{24,88},{28,92},{32,9... | collective-permute-start | bytes 393224 | tf_op jit(solution)/shard_map/ppermute | solution.py:46
  20.2 6.9 %collective-permute-start.5 = (f32[256,128]{1,0:T(8,128)S(1)}, f32[256,128]{1,0:T(8,128)S(1)}, u32[]{:S(2)}, u32[]{:S(2)}) collective-permute-start(f32[256,128]{1,0:T(8,128)S(1)} %shard_map.59), channel_id=1, source_target_pairs={{0,96},{4,100},{8,104},{12,108},{16,112},{20,116},{24,120},{28,124... | collective-permute-start | bytes 393224 | tf_op jit(solution)/shard_map/ppermute | solution.py:46
  20.2 7.0 %collective-permute-start.4 = (f32[256,128]{1,0:T(8,128)S(1)}, f32[256,128]{1,0:T(8,128)S(1)}, u32[]{:S(2)}, u32[]{:S(2)}) collective-permute-start(f32[256,128]{1,0:T(8,128)S(1)} %shard_map.59), channel_id=1, source_target_pairs={{0,32},{4,36},{8,40},{12,44},{16,48},{20,52},{24,56},{28,60},{32,0... | collective-permute-start | bytes 393224 | tf_op jit(solution)/shard_map/ppermute | solution.py:46
  27.5 9.8 %collective-permute-start.7 = (f32[256,128]{1,0:T(8,128)S(1)}, f32[256,128]{1,0:T(8,128)S(1)}, u32[]{:S(2)}, u32[]{:S(2)}) collective-permute-start(f32[256,128]{1,0:T(8,128)S(1)} %get-tuple-element.49), channel_id=1, source_target_pairs={{0,8},{4,12},{8,16},{12,20},{16,24},{20,28},{24,0},{28,4},{32,40},... | collective-permute-start | bytes 393224 | tf_op jit(solution)/shard_map/ppermute | solution.py:38
  28.8 8.5 %collective-permute-start.8 = (f32[256,128]{1,0:T(8,128)S(1)}, f32[256,128]{1,0:T(8,128)S(1)}, u32[]{:S(2)}, u32[]{:S(2)}) collective-permute-start(f32[256,128]{1,0:T(8,128)S(1)} %get-tuple-element.50), channel_id=1, source_target_pairs={{0,16},{4,20},{8,24},{12,28},{16,0},{20,4},{24,8},{28,12},{32,48},... | collective-permute-start | bytes 393224 | tf_op jit(solution)/shard_map/ppermute | solution.py:38
  31.3 6.0 %collective-permute-start.9 = (f32[256,128]{1,0:T(8,128)S(1)}, f32[256,128]{1,0:T(8,128)S(1)}, u32[]{:S(2)}, u32[]{:S(2)}) collective-permute-start(f32[256,128]{1,0:T(8,128)S(1)} %get-tuple-element.51), channel_id=1, source_target_pairs={{0,24},{4,28},{8,0},{12,4},{16,8},{20,12},{24,16},{28,20},{32,56},... | collective-permute-start | bytes 393224 | tf_op jit(solution)/shard_map/ppermute | solution.py:38
  37.5 2.0 %collective-permute-start.10 = (f32[1024,128]{1,0:T(8,128)S(1)}, f32[1024,128]{1,0:T(8,128)S(1)}, u32[]{:S(2)}, u32[]{:S(2)}) collective-permute-start(f32[1024,128]{1,0:T(8,128)S(1)} %get-tuple-element.54), channel_id=1, source_target_pairs={{0,4},{4,0},{8,12},{12,8},{16,20},{20,16},{24,28},{28,24},{32,36},... | collective-permute-start | bytes 1572872 | tf_op jit(solution)/shard_map/ppermute | solution.py:32
  39.5 10.7 %copy-start = (f32[2048]{0:T(1024)S(1)}, f32[2048]{0:T(1024)}, u32[]{:S(2)}) copy-start(f32[2048]{0:T(1024)} %param.9) | copy-start | bytes 24580
  41.0 6.6 %collective-permute-start.13 = (f32[1,1536]{1,0:T(1,128)S(1)}, f32[1,1536]{1,0:T(1,128)S(1)}, u32[]{:S(2)}, u32[]{:S(2)}) collective-permute-start(f32[1,1536]{1,0:T(1,128)S(1)} %get-tuple-element.62.sq0), channel_id=1, source_target_pairs={{0,1},{1,2},{2,3},{3,0},{4,5},{5,6},{6,7},{7,4},{8,9},{9,10},{10,1... | collective-permute-start | bytes 18440 | tf_op jit(solution)/shard_map/ppermute | solution.py:481
  43.0 5.2 %collective-permute-start.12 = (f32[1,1536]{1,0:T(1,128)S(1)}, f32[1,1536]{1,0:T(1,128)S(1)}, u32[]{:S(2)}, u32[]{:S(2)}) collective-permute-start(f32[1,1536]{1,0:T(1,128)S(1)} %get-tuple-element.62.sq0), channel_id=1, source_target_pairs={{0,2},{1,3},{2,0},{3,1},{4,6},{5,7},{6,4},{7,5},{8,10},{9,11},{10,... | collective-permute-start | bytes 18440 | tf_op jit(solution)/shard_map/ppermute | solution.py:481
  46.6 3.6 %collective-permute-start.11 = (f32[1,1536]{1,0:T(1,128)S(1)}, f32[1,1536]{1,0:T(1,128)S(1)}, u32[]{:S(2)}, u32[]{:S(2)}) collective-permute-start(f32[1,1536]{1,0:T(1,128)S(1)} %get-tuple-element.62.sq0), channel_id=1, source_target_pairs={{0,3},{1,0},{2,1},{3,2},{4,7},{5,4},{6,5},{7,6},{8,11},{9,8},{10,9... | collective-permute-start | bytes 18440 | tf_op jit(solution)/shard_map/ppermute | solution.py:481

commit v6 on v5

--- a/solution.py
+++ b/solution.py
@@ -415,7 +415,7 @@
         return 0
 
     steps = tokens // rows
-    lax.fori_loop(0, steps, step, 0)
+    lax.fori_loop(0, steps, step, 0, unroll=2)
     for index in range(steps):
         for copy in copies(index):
             copy.wait()

time: 53.7 us -> 53.7 us (level)
  no operation moved by 1% of the time
where the time goes in v6:
time: 53.7 us; the launch traced here: 53.6 us
  Pallas kernels  25.3 us (47%)
  starting transfers between devices  22.4 us (42%)
  waiting for transfers between devices  5.66 us (11%)
    pallas_call x3, Pallas kernels, local_attention(): pl.pallas_call(functools.partial(local_kernel, column=column), out_shape=...  12.1 us
    ppermute x6, starting transfers between devices, turn_row(): lax.ppermute(value, 'seq', [(device_of(x, y, c), device_of(x, (y + steps)...  10.9 us
    ppermute x3, starting transfers between devices, on_device(): lax.ppermute(squares, 'head', [(z, (z + d) % 4) for z in range(4)])  6.58 us
    pallas_call x1, Pallas kernels, own_states(): pl.pallas_call(functools.partial(state_kernel, rows=rows), out_shape=[plt...  4.85 us
    ppermute x3, starting transfers between devices, swap_rows(): lax.ppermute(value, 'seq', [(device_of(x, y, c), device_of(x ^ steps, y,...  4.78 us
    pallas_call x1, Pallas kernels, normalise(): pl.pallas_call(functools.partial(norm_kernel, rows=rows), out_shape=jax.S...  3.28 us
    pallas_call x2, Pallas kernels, finish(): pl.pallas_call(functools.partial(finish_kernel, places=places, kept=kept,...  3.04 us
    ppermute x3, waiting for transfers between devices, on_device(): lax.ppermute(squares, 'head', [(z, (z + d) % 4) for z in range(4)])  2.61 us
  transfers between devices with their start and end apart: 14, of which 9 were waited for; matrix products, arithmetic and copies ran while one was open for 0% of the time, Pallas kernels for 28%

profile of v6, /device:TPU:2, one launch (start us, length us, event | category | flops | bytes accessed | tf_op | source)
XLA Modules:
  0.0 53.6 jit_solution(12741521983244702933)
XLA Ops:
  0.0 4.8 %shard_map.55 = (f32[1032,128]{1,0:T(8,128)S(1)}, bf16[1536,2048]{1,0:T(8,128)(2,1)S(1)}, bf16[1536,2048]{1,0:T(8,128)(2,1)S(1)}, s32[1,1536]{1,0:T(1,128)S(1)}) custom-call(s32[1536]{0:T(1024)} %starts_hbm.1, bf16[1536,2048]{1,0:T(8,128)(2,1)} %k_hbm.1, bf16[1536,2048]{1,0:T(8,128)(2,1)} %v_hbm.1), custom_call_target="tpu_custom_call" | custom-call | flops 402653184 | bytes 12582912 | tf_op jit(solution)/shard_map/pallas_call | solution.py:151
  5.0 1.4 %shard_map.56.keep = f32[1032,128]{1,0:T(8,128)S(1)} custom-call(s32[1,1536]{1,0:T(1,128)S(1)} %get-tuple-element.52.starts.starts_ref, bf16[1536,2048]{1,0:T(8,128)(2,1)S(1)} %get-tuple-element.38.k_ref, bf16[1536,2048]{1,0:T(8,128)(2,1)S(1)} %get-tuple-element.39.v_ref), custom_call_target="tpu_custom_call" | custom-call | flops 402653184 | bytes 6291456 | tf_op jit(solution)/shard_map/pallas_call | solution.py:166
  6.9 1.6 %collective-permute-start.1 = (f32[264,128]{1,0:T(8,128)S(1)}, f32[264,128]{1,0:T(8,128)S(1)}, u32[]{:S(2)}, u32[]{:S(2)}) collective-permute-start(f32[264,128]{1,0:T(8,128)S(1)} %get-tuple-element.41), channel_id=1, source_target_pairs={{0,8},{4,12},{8,16},{12,20},{16,24},{20,28},{24,0},{28,4},{32,40},... | collective-permute-start | bytes 405512 | tf_op jit(solution)/shard_map/ppermute | solution.py:38
  8.6 2.9 %collective-permute-start.2 = (f32[264,128]{1,0:T(8,128)S(1)}, f32[264,128]{1,0:T(8,128)S(1)}, u32[]{:S(2)}, u32[]{:S(2)}) collective-permute-start(f32[264,128]{1,0:T(8,128)S(1)} %get-tuple-element.42), channel_id=1, source_target_pairs={{0,16},{4,20},{8,24},{12,28},{16,0},{20,4},{24,8},{28,12},{32,48},... | collective-permute-start | bytes 405512 | tf_op jit(solution)/shard_map/ppermute | solution.py:38
  11.5 1.3 %collective-permute-start.3 = (f32[264,128]{1,0:T(8,128)S(1)}, f32[264,128]{1,0:T(8,128)S(1)}, u32[]{:S(2)}, u32[]{:S(2)}) collective-permute-start(f32[264,128]{1,0:T(8,128)S(1)} %get-tuple-element.43), channel_id=1, source_target_pairs={{0,24},{4,28},{8,0},{12,4},{16,8},{20,12},{24,16},{28,20},{32,56},... | collective-permute-start | bytes 405512 | tf_op jit(solution)/shard_map/ppermute | solution.py:38
  12.8 4.5 %shard_map.58.refs_0_ = f32[1536,768]{1,0:T(8,128)S(1)} custom-call(s32[1,1536]{1,0:T(1,128)S(1)} %get-tuple-element.52.starts.starts_ref, bf16[1536,2048]{1,0:T(8,128)(2,1)S(1)} %bitcast.2, bf16[1536,2048]{1,0:T(8,128)(2,1)S(1)} %get-tuple-element.38.k_ref, bf16[1536,2048]{1,0:T(8,128)(2,1)S(1)} %get-tuple-element.39.v_ref), custom_call_target="tpu_custom_call" | custom-call | flops 1811939328 | bytes 11796480 | tf_op jit(solution)/shard_map/pallas_call | solution.py:323
  17.5 0.5 collective-permute-done.2.from2
  18.0 2.2 %collective-permute-start.6 = (f32[256,128]{1,0:T(8,128)S(1)}, f32[256,128]{1,0:T(8,128)S(1)}, u32[]{:S(2)}, u32[]{:S(2)}) collective-permute-start(f32[256,128]{1,0:T(8,128)S(1)} %shard_map.59), channel_id=1, source_target_pairs={{0,64},{4,68},{8,72},{12,76},{16,80},{20,84},{24,88},{28,92},{32,9... | collective-permute-start | bytes 393224 | tf_op jit(solution)/shard_map/ppermute | solution.py:46
  20.2 2.6 %collective-permute-start.4 = (f32[256,128]{1,0:T(8,128)S(1)}, f32[256,128]{1,0:T(8,128)S(1)}, u32[]{:S(2)}, u32[]{:S(2)}) collective-permute-start(f32[256,128]{1,0:T(8,128)S(1)} %shard_map.59), channel_id=1, source_target_pairs={{0,32},{4,36},{8,40},{12,44},{16,48},{20,52},{24,56},{28,60},{32,0... | collective-permute-start | bytes 393224 | tf_op jit(solution)/shard_map/ppermute | solution.py:46
  22.8 3.8 %shard_map.60.refs_1_ = f32[1536,640]{1,0:T(8,128)S(1)} custom-call(s32[1,1536]{1,0:T(1,128)S(1)} %get-tuple-element.52.starts.starts_ref, bf16[1536,2048]{1,0:T(8,128)(2,1)S(1)} %bitcast.2, bf16[1536,2048]{1,0:T(8,128)(2,1)S(1)} %get-tuple-element.38.k_ref, bf16[1536,2048]{1,0:T(8,128)(2,1)S(1)} %get-tuple-element.39.v_ref), custom_call_target="tpu_custom_call" | custom-call | flops 1509949440 | bytes 9830400 | tf_op jit(solution)/shard_map/pallas_call | solution.py:323
  26.6 0.5 collective-permute-done.5.up2
  27.5 1.3 %collective-permute-start.7 = (f32[256,128]{1,0:T(8,128)S(1)}, f32[256,128]{1,0:T(8,128)S(1)}, u32[]{:S(2)}, u32[]{:S(2)}) collective-permute-start(f32[256,128]{1,0:T(8,128)S(1)} %get-tuple-element.49), channel_id=1, source_target_pairs={{0,8},{4,12},{8,16},{12,20},{16,24},{20,28},{24,0},{28,4},{32,40},... | collective-permute-start | bytes 393224 | tf_op jit(solution)/shard_map/ppermute | solution.py:38
  28.8 2.5 %collective-permute-start.8 = (f32[256,128]{1,0:T(8,128)S(1)}, f32[256,128]{1,0:T(8,128)S(1)}, u32[]{:S(2)}, u32[]{:S(2)}) collective-permute-start(f32[256,128]{1,0:T(8,128)S(1)} %get-tuple-element.50), channel_id=1, source_target_pairs={{0,16},{4,20},{8,24},{12,28},{16,0},{20,4},{24,8},{28,12},{32,48},... | collective-permute-start | bytes 393224 | tf_op jit(solution)/shard_map/ppermute | solution.py:38
  31.3 1.2 %collective-permute-start.9 = (f32[256,128]{1,0:T(8,128)S(1)}, f32[256,128]{1,0:T(8,128)S(1)}, u32[]{:S(2)}, u32[]{:S(2)}) collective-permute-start(f32[256,128]{1,0:T(8,128)S(1)} %get-tuple-element.51), channel_id=1, source_target_pairs={{0,24},{4,28},{8,0},{12,4},{16,8},{20,12},{24,16},{28,20},{32,56},... | collective-permute-start | bytes 393224 | tf_op jit(solution)/shard_map/ppermute | solution.py:38
  32.5 3.8 %shard_map.62.refs_2_ = f32[1536,640]{1,0:T(8,128)S(1)} custom-call(s32[1,1536]{1,0:T(1,128)S(1)} %get-tuple-element.52.starts.starts_ref, bf16[1536,2048]{1,0:T(8,128)(2,1)S(1)} %bitcast.2, bf16[1536,2048]{1,0:T(8,128)(2,1)S(1)} %get-tuple-element.38.k_ref, bf16[1536,2048]{1,0:T(8,128)(2,1)S(1)} %get-tuple-element.39.v_ref), custom_call_target="tpu_custom_call" | custom-call | flops 1509949440 | bytes 9830400 | tf_op jit(solution)/shard_map/pallas_call | solution.py:323
  36.3 1.0 %collective-permute-done.9.got3 = f32[256,128]{1,0:T(8,128)S(1)} collective-permute-done((f32[256,128]{1,0:T(8,128)S(1)}, f32[256,128]{1,0:T(8,128)S(1)}, u32[]{:S(2)}, u32[]{:S(2)}) %collective-permute-start.9) | collective-permute-done | bytes 131104 | tf_op jit(solution)/shard_map/ppermute | solution.py:38
  37.6 1.5 %shard_map.64 = (f32[1536,1024]{1,0:T(8,128)S(1)}, f32[1,1536]{1,0:T(1,128)S(1)}) custom-call(s32[1,1536]{1,0:T(1,128)S(1)} %get-tuple-element.52.starts.starts_ref, bf16[1536,2048]{1,0:T(8,128)(2,1)S(1)} %bitcast.2, f32[1024,128]{1,0:T(8,128)S(1)} %get-tuple-element.55.carry, f32[1536,768]{1,0:T(8,128)S(1)} %shard_map.58.refs_0_, ...), custom_call_target="tpu_custom_call" | custom-call | flops 402653184 | bytes 9437184 | tf_op jit(solution)/shard_map/pallas_call | solution.py:373
  39.5 1.5 %shard_map.65 = (f32[1536,1024]{1,0:T(8,128)S(1)}, f32[1,1536]{1,0:T(1,128)S(1)}) custom-call(s32[1,1536]{1,0:T(1,128)S(1)} %get-tuple-element.52.starts.starts_ref, bf16[1536,2048]{1,0:T(8,128)(2,1)S(1)} %bitcast.2, f32[1024,128]{1,0:T(8,128)S(1)} %collective-permute-done.10.carry, f32[1536,768]{1,0:T(8,128)S(1)} %shard_map.58.refs_0_, ...), custom_call_target="tpu_custom_call" | custom-call | flops 402653184 | bytes 9437184 | tf_op jit(solution)/shard_map/pallas_call | solution.py:373
  41.0 2.0 %collective-permute-start.13 = (f32[1,1536]{1,0:T(1,128)S(1)}, f32[1,1536]{1,0:T(1,128)S(1)}, u32[]{:S(2)}, u32[]{:S(2)}) collective-permute-start(f32[1,1536]{1,0:T(1,128)S(1)} %get-tuple-element.62.sq0), channel_id=1, source_target_pairs={{0,1},{1,2},{2,3},{3,0},{4,5},{5,6},{6,7},{7,4},{8,9},{9,10},{10,1... | collective-permute-start | bytes 18440 | tf_op jit(solution)/shard_map/ppermute | solution.py:481
  43.0 3.6 %collective-permute-start.12 = (f32[1,1536]{1,0:T(1,128)S(1)}, f32[1,1536]{1,0:T(1,128)S(1)}, u32[]{:S(2)}, u32[]{:S(2)}) collective-permute-start(f32[1,1536]{1,0:T(1,128)S(1)} %get-tuple-element.62.sq0), channel_id=1, source_target_pairs={{0,2},{1,3},{2,0},{3,1},{4,6},{5,7},{6,4},{7,5},{8,10},{9,11},{10,... | collective-permute-start | bytes 18440 | tf_op jit(solution)/shard_map/ppermute | solution.py:481
  46.6 1.0 %collective-permute-start.11 = (f32[1,1536]{1,0:T(1,128)S(1)}, f32[1,1536]{1,0:T(1,128)S(1)}, u32[]{:S(2)}, u32[]{:S(2)}) collective-permute-start(f32[1,1536]{1,0:T(1,128)S(1)} %get-tuple-element.62.sq0), channel_id=1, source_target_pairs={{0,3},{1,0},{2,1},{3,2},{4,7},{5,4},{6,5},{7,6},{8,11},{9,8},{10,9... | collective-permute-start | bytes 18440 | tf_op jit(solution)/shard_map/ppermute | solution.py:481
  47.6 0.7 %collective-permute-done.12.sq2 = f32[1,1536]{1,0:T(1,128)S(1)} collective-permute-done((f32[1,1536]{1,0:T(1,128)S(1)}, f32[1,1536]{1,0:T(1,128)S(1)}, u32[]{:S(2)}, u32[]{:S(2)}) %collective-permute-start.12) | collective-permute-done | bytes 6176 | tf_op jit(solution)/shard_map/ppermute | solution.py:481
  48.2 2.0 %collective-permute-done.11.sq1 = f32[1,1536]{1,0:T(1,128)S(1)} collective-permute-done((f32[1,1536]{1,0:T(1,128)S(1)}, f32[1,1536]{1,0:T(1,128)S(1)}, u32[]{:S(2)}, u32[]{:S(2)}) %collective-permute-start.11) | collective-permute-done | bytes 6176 | tf_op jit(solution)/shard_map/ppermute | solution.py:481
  50.2 3.3 %shard_map.66 = bf16[1536,2048]{1,0:T(8,128)(2,1)} custom-call(f32[1,1536]{1,0:T(1,128)S(1)} %get-tuple-element.62.sq0, f32[1,1536]{1,0:T(1,128)S(1)} %collective-permute-done.11.sq1, f32[1,1536]{1,0:T(1,128)S(1)} %collective-permute-done.12.sq2, f32[1,1536]{1,0:T(1,128)S(1)} %collective-permute-done.13.sq3, f32[1,2048]{1,0:T(1,128)S(1)} %bitcast.3, ...), custom_call_target="tpu_custom_call" | custom-call | flops 6291456 | bytes 18874368 | tf_op jit(solution)/shard_map/pallas_call | solution.py:428
  (23 shorter events, 1.8 us)
Async XLA Ops:
  0.0 12.8 %slice-start = ((s8[6291456]{0:T(1024)(128)(4,1)}), s8[4194304]{0:T(1024)(128)(4,1)S(1)}, s32[]{:S(2)}) async-start(s8[6291456]{0:T(1024)(128)(4,1)} %bitcast.1), calls=%async_computation | async-start | bytes 8388608
  4.9 2.0 %collective-permute-start = (f32[1032,128]{1,0:T(8,128)S(1)}, f32[1032,128]{1,0:T(8,128)S(1)}, u32[]{:S(2)}, u32[]{:S(2)}) collective-permute-start(f32[1032,128]{1,0:T(8,128)S(1)} %get-tuple-element.36), channel_id=1, source_target_pairs={{0,4},{4,0},{8,12},{12,8},{16,20},{20,16},{24,28},{28,24},{32,36},... | collective-permute-start | bytes 1585160 | tf_op jit(solution)/shard_map/ppermute | solution.py:32
  5.0 7.9 %slice-start.1 = ((s8[6291456]{0:T(1024)(128)(4,1)}), s8[2097152]{0:T(1024)(128)(4,1)S(1)}, s32[]{:S(2)}) async-start(s8[6291456]{0:T(1024)(128)(4,1)} %bitcast.1), calls=%async_computation.1 | async-start | bytes 4194304
  6.9 10.5 %collective-permute-start.1 = (f32[264,128]{1,0:T(8,128)S(1)}, f32[264,128]{1,0:T(8,128)S(1)}, u32[]{:S(2)}, u32[]{:S(2)}) collective-permute-start(f32[264,128]{1,0:T(8,128)S(1)} %get-tuple-element.41), channel_id=1, source_target_pairs={{0,8},{4,12},{8,16},{12,20},{16,24},{20,28},{24,0},{28,4},{32,40},... | collective-permute-start | bytes 405512 | tf_op jit(solution)/shard_map/ppermute | solution.py:38
  8.6 9.4 %collective-permute-start.2 = (f32[264,128]{1,0:T(8,128)S(1)}, f32[264,128]{1,0:T(8,128)S(1)}, u32[]{:S(2)}, u32[]{:S(2)}) collective-permute-start(f32[264,128]{1,0:T(8,128)S(1)} %get-tuple-element.42), channel_id=1, source_target_pairs={{0,16},{4,20},{8,24},{12,28},{16,0},{20,4},{24,8},{28,12},{32,48},... | collective-permute-start | bytes 405512 | tf_op jit(solution)/shard_map/ppermute | solution.py:38
  11.5 6.0 %collective-permute-start.3 = (f32[264,128]{1,0:T(8,128)S(1)}, f32[264,128]{1,0:T(8,128)S(1)}, u32[]{:S(2)}, u32[]{:S(2)}) collective-permute-start(f32[264,128]{1,0:T(8,128)S(1)} %get-tuple-element.43), channel_id=1, source_target_pairs={{0,24},{4,28},{8,0},{12,4},{16,8},{20,12},{24,16},{28,20},{32,56},... | collective-permute-start | bytes 405512 | tf_op jit(solution)/shard_map/ppermute | solution.py:38
  18.0 8.6 %collective-permute-start.6 = (f32[256,128]{1,0:T(8,128)S(1)}, f32[256,128]{1,0:T(8,128)S(1)}, u32[]{:S(2)}, u32[]{:S(2)}) collective-permute-start(f32[256,128]{1,0:T(8,128)S(1)} %shard_map.59), channel_id=1, source_target_pairs={{0,64},{4,68},{8,72},{12,76},{16,80},{20,84},{24,88},{28,92},{32,9... | collective-permute-start | bytes 393224 | tf_op jit(solution)/shard_map/ppermute | solution.py:46
  20.2 6.9 %collective-permute-start.5 = (f32[256,128]{1,0:T(8,128)S(1)}, f32[256,128]{1,0:T(8,128)S(1)}, u32[]{:S(2)}, u32[]{:S(2)}) collective-permute-start(f32[256,128]{1,0:T(8,128)S(1)} %shard_map.59), channel_id=1, source_target_pairs={{0,96},{4,100},{8,104},{12,108},{16,112},{20,116},{24,120},{28,124... | collective-permute-start | bytes 393224 | tf_op jit(solution)/shard_map/ppermute | solution.py:46
  20.2 7.0 %collective-permute-start.4 = (f32[256,128]{1,0:T(8,128)S(1)}, f32[256,128]{1,0:T(8,128)S(1)}, u32[]{:S(2)}, u32[]{:S(2)}) collective-permute-start(f32[256,128]{1,0:T(8,128)S(1)} %shard_map.59), channel_id=1, source_target_pairs={{0,32},{4,36},{8,40},{12,44},{16,48},{20,52},{24,56},{28,60},{32,0... | collective-permute-start | bytes 393224 | tf_op jit(solution)/shard_map/ppermute | solution.py:46
  27.5 9.8 %collective-permute-start.7 = (f32[256,128]{1,0:T(8,128)S(1)}, f32[256,128]{1,0:T(8,128)S(1)}, u32[]{:S(2)}, u32[]{:S(2)}) collective-permute-start(f32[256,128]{1,0:T(8,128)S(1)} %get-tuple-element.49), channel_id=1, source_target_pairs={{0,8},{4,12},{8,16},{12,20},{16,24},{20,28},{24,0},{28,4},{32,40},... | collective-permute-start | bytes 393224 | tf_op jit(solution)/shard_map/ppermute | solution.py:38
  28.8 8.5 %collective-permute-start.8 = (f32[256,128]{1,0:T(8,128)S(1)}, f32[256,128]{1,0:T(8,128)S(1)}, u32[]{:S(2)}, u32[]{:S(2)}) collective-permute-start(f32[256,128]{1,0:T(8,128)S(1)} %get-tuple-element.50), channel_id=1, source_target_pairs={{0,16},{4,20},{8,24},{12,28},{16,0},{20,4},{24,8},{28,12},{32,48},... | collective-permute-start | bytes 393224 | tf_op jit(solution)/shard_map/ppermute | solution.py:38
  31.3 6.0 %collective-permute-start.9 = (f32[256,128]{1,0:T(8,128)S(1)}, f32[256,128]{1,0:T(8,128)S(1)}, u32[]{:S(2)}, u32[]{:S(2)}) collective-permute-start(f32[256,128]{1,0:T(8,128)S(1)} %get-tuple-element.51), channel_id=1, source_target_pairs={{0,24},{4,28},{8,0},{12,4},{16,8},{20,12},{24,16},{28,20},{32,56},... | collective-permute-start | bytes 393224 | tf_op jit(solution)/shard_map/ppermute | solution.py:38
  37.5 2.0 %collective-permute-start.10 = (f32[1024,128]{1,0:T(8,128)S(1)}, f32[1024,128]{1,0:T(8,128)S(1)}, u32[]{:S(2)}, u32[]{:S(2)}) collective-permute-start(f32[1024,128]{1,0:T(8,128)S(1)} %get-tuple-element.54), channel_id=1, source_target_pairs={{0,4},{4,0},{8,12},{12,8},{16,20},{20,16},{24,28},{28,24},{32,36},... | collective-permute-start | bytes 1572872 | tf_op jit(solution)/shard_map/ppermute | solution.py:32
  39.5 10.7 %copy-start = (f32[2048]{0:T(1024)S(1)}, f32[2048]{0:T(1024)}, u32[]{:S(2)}) copy-start(f32[2048]{0:T(1024)} %param.9) | copy-start | bytes 24580
  41.0 6.6 %collective-permute-start.13 = (f32[1,1536]{1,0:T(1,128)S(1)}, f32[1,1536]{1,0:T(1,128)S(1)}, u32[]{:S(2)}, u32[]{:S(2)}) collective-permute-start(f32[1,1536]{1,0:T(1,128)S(1)} %get-tuple-element.62.sq0), channel_id=1, source_target_pairs={{0,1},{1,2},{2,3},{3,0},{4,5},{5,6},{6,7},{7,4},{8,9},{9,10},{10,1... | collective-permute-start | bytes 18440 | tf_op jit(solution)/shard_map/ppermute | solution.py:481
  43.0 5.2 %collective-permute-start.12 = (f32[1,1536]{1,0:T(1,128)S(1)}, f32[1,1536]{1,0:T(1,128)S(1)}, u32[]{:S(2)}, u32[]{:S(2)}) collective-permute-start(f32[1,1536]{1,0:T(1,128)S(1)} %get-tuple-element.62.sq0), channel_id=1, source_target_pairs={{0,2},{1,3},{2,0},{3,1},{4,6},{5,7},{6,4},{7,5},{8,10},{9,11},{10,... | collective-permute-start | bytes 18440 | tf_op jit(solution)/shard_map/ppermute | solution.py:481
  46.6 3.6 %collective-permute-start.11 = (f32[1,1536]{1,0:T(1,128)S(1)}, f32[1,1536]{1,0:T(1,128)S(1)}, u32[]{:S(2)}, u32[]{:S(2)}) collective-permute-start(f32[1,1536]{1,0:T(1,128)S(1)} %get-tuple-element.62.sq0), channel_id=1, source_target_pairs={{0,3},{1,0},{2,1},{3,2},{4,7},{5,4},{6,5},{7,6},{8,11},{9,8},{10,9... | collective-permute-start | bytes 18440 | tf_op jit(solution)/shard_map/ppermute | solution.py:481
